TPU v7x, 32 devices: a whole 2x2x4 slice. The times are simulated.
32 devices in a mesh: rows: 8 (over z, y), rep: 4 (over x, core).
Axes of the slice: x: 2, y: 2, z: 4, core: 2. Of those that a mesh axis runs over, the one named last changes fastest.
Arguments:
- features: bfloat16 [32768, 256], P(('rows', 'rep')), may hold values from -6 to 6
- weight: bfloat16 [256, 256], replicated, may hold values from -0.375 to 0.375
- block_cols: int32 [256, 4, 2], P('rows', 'rep'), may hold values from 0 to 63, as said below
- block_vals: bfloat16 [256, 4, 2, 128, 128], P('rows', 'rep'), as said below
- out_grad: bfloat16 [32768, 256], P('rows'), may hold values from -6 to 6
Outputs:
- activations: bfloat16 [32768, 256], P(('rows', 'rep'))
- input_grad: bfloat16 [32768, 256], P(('rows', 'rep'))
- weight_grad: float32 [256, 256], replicated
Inputs may be any that keep to these rules, and one draw needn't show every extreme that they name: `block_cols`: layer c's k-th block column is global block column (k // 8) * 32 + c * 8 + k % 8, whose rows the device of index k // 8 along rows holds in layer c. In the layer that owns a block row, slot 0 is its diagonal block; no other held block of a device lies in its own block columns. For every layer, every device along rows and every other device along rows, at most 10 of the first device's held blocks in that layer lie in block columns of the other, and in every draw some pair has exactly 10. `block_vals`: the adjacency is symmetric: every held block at block row b, block column g in slot s has a partner held at block row g, block column b in slot s (of the layer owning b) that is its transpose; diagonal blocks are symmetric.
All inputs are finite; a program needn't handle non-finite values.
Results may differ from a plain program's by a relative error of at most 0.006.
Values may be sent and summed in bfloat16 or wider, within the bound.
No kernel may reach another device: no remote copies, remote signals or barrier semaphores. Data moves between devices by JAX's collectives and lax.ppermute only.
A program may use at most 128 MiB of HBM per device.

v0:
```python
import math

import jax
import jax.numpy as jnp
from jax import lax
from jax.sharding import PartitionSpec as P


def silu_parts(summed):
    sigmoid_vals = jax.nn.sigmoid(summed)
    return (summed * sigmoid_vals, sigmoid_vals * (1.0 + summed * (1.0 - sigmoid_vals)))


def apply_blocks(local_vals, fetched):
    product = jnp.einsum("bsij,bsjf->bif", local_vals, fetched, preferred_element_type=jnp.float32)
    return product.reshape(-1, fetched.shape[-1])


def serve_blocks(source_rows, asked_places, block_size):
    feature_width = source_rows.shape[1]
    blocks = source_rows.reshape(-1, block_size, feature_width)
    flat_ask = asked_places.reshape(-1)
    picked = jnp.take(blocks, jnp.clip(flat_ask, 0, blocks.shape[0] - 1), axis=0)
    picked = jnp.where((flat_ask >= 0)[:, None, None], picked, jnp.zeros_like(picked))
    return picked.reshape(asked_places.shape[0], asked_places.shape[1] * block_size, feature_width)


def on_device(features, weight, block_cols, block_vals, out_grad):
    own_rows, feature_width = features.shape
    block_size = block_vals.shape[-1]
    row_blocks, slot_count = (block_cols.shape[0], block_cols.shape[2])
    own_blocks = own_rows // block_size
    peer_count = lax.axis_size("rows")
    layer_count = lax.axis_size("rep")
    couple_total = ((layer_count - 1) * slot_count * own_blocks + own_blocks) // 2
    reach_classes = peer_count // 2 - 1
    capacity = (couple_total + reach_classes - 1) // reach_classes
    my_group = lax.axis_index("rows")
    layer_index = lax.axis_index("rep")
    local_vals = block_vals[:, 0]
    flat_cols = block_cols[:, 0].reshape(-1)
    request_total = flat_cols.shape[0]
    owners = flat_cols // own_blocks
    places = flat_cols % own_blocks
    remote = owners != my_group
    positions = jnp.arange(request_total, dtype=jnp.int32)
    same_owner = (owners[:, None] == owners[None, :]) & (positions[:, None] > positions[None, :])
    owner_ranks = jnp.sum(same_owner.astype(jnp.int32), axis=1)
    slot_keys = jnp.where(remote, owners * capacity + owner_ranks, -1)
    slot_table = jnp.arange(peer_count * capacity, dtype=jnp.int32)
    matches = slot_keys[:, None] == slot_table[None, :]
    requests = (jnp.sum(jnp.where(matches, places[:, None] + 1, 0), axis=0) - 1).reshape(
        peer_count, capacity
    )
    asked_places = lax.all_to_all(requests, "rows", split_axis=0, concat_axis=0, tiled=True)
    mixed_rows = jnp.dot(features, weight, preferred_element_type=jnp.float32).astype(jnp.bfloat16)
    arrived = lax.all_to_all(
        serve_blocks(mixed_rows, asked_places, block_size),
        "rows",
        split_axis=0,
        concat_axis=0,
        tiled=True,
    )
    arrived_pool = arrived.reshape(-1, block_size, feature_width)
    from_peers = jnp.take(arrived_pool, jnp.clip(slot_keys, 0, arrived_pool.shape[0] - 1), axis=0)
    from_self = jnp.take(mixed_rows.reshape(own_blocks, block_size, feature_width), places, axis=0)
    joined = jnp.where(remote[:, None, None], from_peers, from_self)
    partial_sum = apply_blocks(
        local_vals, joined.reshape(row_blocks, slot_count, block_size, feature_width)
    )
    share_start = layer_index * own_rows
    summed = lax.psum(partial_sum, "rep")
    values_all, slopes_all = silu_parts(summed)
    grad_rows = (out_grad.astype(jnp.float32) * slopes_all).astype(jnp.bfloat16)
    activated = lax.dynamic_slice_in_dim(values_all, share_start, own_rows, 0).astype(jnp.bfloat16)
    slot_terms = jnp.einsum(
        "bsji,bjf->bsif",
        local_vals,
        grad_rows.reshape(row_blocks, block_size, feature_width),
        preferred_element_type=jnp.float32,
    ).reshape(request_total, block_size, feature_width)
    filler = jnp.sum(jnp.where(matches, positions[:, None], 0), axis=0)
    filled = jnp.any(matches, axis=0)
    outgoing = jnp.where(
        filled[:, None, None], jnp.take(slot_terms, filler, axis=0), jnp.zeros((), jnp.float32)
    )
    returned = lax.all_to_all(
        outgoing.reshape(peer_count, capacity * block_size, feature_width),
        "rows",
        split_axis=0,
        concat_axis=0,
        tiled=True,
    )
    block_span = block_size * feature_width
    own_index = jnp.arange(own_blocks, dtype=jnp.int32)
    arrive_hot = (asked_places.reshape(-1)[:, None] == own_index[None, :]).astype(jnp.float32)
    self_hot = ((~remote)[:, None] & (places[:, None] == own_index[None, :])).astype(jnp.float32)
    collected = jnp.einsum(
        "qo,qx->ox", arrive_hot, returned.reshape(-1, block_span), precision=lax.Precision.HIGHEST
    )
    self_terms = jnp.einsum(
        "no,nx->ox", self_hot, slot_terms.reshape(-1, block_span), precision=lax.Precision.HIGHEST
    )
    back_rows = (collected + self_terms).reshape(own_rows, feature_width)
    node_total = own_rows * peer_count * layer_count
    local_weight = jnp.dot(
        features.astype(jnp.float32).T, back_rows, precision=lax.Precision.HIGHEST
    )
    weight_grad = lax.psum(local_weight, ("rows", "rep")) * (1.0 / math.sqrt(node_total))
    input_grad = jnp.dot(
        back_rows.astype(jnp.bfloat16), weight.T, preferred_element_type=jnp.float32
    ).astype(jnp.bfloat16)
    return (activated, input_grad, weight_grad)


def solution(mesh):
    placed = (
        P(("rows", "rep"), None),
        P(),
        P("rows", "rep", None),
        P("rows", "rep", None, None, None),
        P("rows", None),
    )
    return jax.shard_map(
        on_device,
        mesh=mesh,
        in_specs=placed,
        out_specs=(P(("rows", "rep"), None), P(("rows", "rep"), None), P()),
        check_vma=False,
    )
```

profile of v0, /device:TPU:0, one launch (start us, length us, event | category | flops | bytes accessed | tf_op | source)
XLA Modules:
  0.0 690.2 jit_solution(4021376884378207021)
XLA Ops:
  9.2 7.3 %all-to-all-start = ((s32[8,1,10]{2,1,0:T(1,128)}), s32[8,1,10]{2,1,0:T(1,128)S(1)}, u32[]{:S(2)}, u32[]{:S(2)}) async-start(s32[8,1,10]{2,1,0:T(1,128)} %bitcast.1), calls=%async_computation | async-start | bytes 8192 | tf_op jit(solution)/shard_map/all_to_all | solution.py:55
  17.9 5.0 all-to-all-done
  23.3 5.6 gather_fusion
  28.9 9.3 %fusion.1 = bf16[8,1280,256]{2,1,0:T(8,128)(2,1)} fusion(pred[8,1280]{1,0:T(8,128)(4,1)S(1)} %get-tuple-element.33, pred[8,1280]{1,0:T(8,128)(4,1)S(1)} %get-tuple-element.34, bf16[8,1280,256]{2,1,0:T(8,128)(2,1)} %bitcast.114), kind=kLoop, calls=%fused_computation.8 | loop fusion | flops 5242880 | bytes 10506240 | tf_op jit(solution)/shard_map/jit(_where)/select_n | solution.py:24
  38.2 4.8 all-to-all-start.1
  43.7 2.9 gather_fusion.2
  46.6 110.9 %all-to-all-done.1 = bf16[8,1280,256]{2,1,0:T(8,128)(2,1)} async-done(((bf16[8,1280,256]{2,1,0:T(8,128)(2,1)}), bf16[8,1280,256]{2,1,0:T(8,128)(2,1)}, u32[]{:S(2)}, u32[]{:S(2)}) %all-to-all-start.1) | async-done | bytes 5242912 | tf_op jit(solution)/shard_map/all_to_all | solution.py:57
  157.5 5.3 gather_fusion.1
  162.8 7.5 %fusion.2 = f32[32,256,128,1]{1,2,3,0:T(8,128)} fusion(bf16[32,2,128,256]{3,2,1,0:T(8,128)(2,1)} %bitcast.117, bf16[32,2,128,256]{3,2,1,0:T(8,128)(2,1)} %bitcast.118, pred[32,2]{1,0:T(8,128)(4,1)S(1)} %copy.73, pred[32,2]{1,0:T(8,128)(4,1)S(1)} %copy.66, pred[32,2]{1,0:T(8,128)(4,1)S(1)} %copy.63, bf16[32,1,2,128,128]{4,3,2,1,0:T(8,128)(2,1)S(1)} %copy-done), kind=kOutput, calls=%fused_computation.11 | convolution fusion | flops 543162368 | bytes 14680256 | tf_op jit(solution)/shard_map/bsij,bsjf->bif/dot_general | solution.py:15
  170.9 84.1 %all-reduce.3.cloned.1.call-done = f32[4096,256]{1,0:T(8,128)} async-done(((f32[4096,256]{1,0:T(8,128)}), f32[4096,256]{1,0:T(8,128)}) %all-reduce.3.cloned.1.call-update) | async-done | bytes 4194320 | tf_op jit(solution)/shard_map/psum | solution.py:72
  255.0 6.4 multiply_convert_fusion
  261.4 4.6 fusion.9
  266.0 9.0 %copy.77 = f32[64,128,256]{2,1,0:T(8,128)} copy(f32[64,128,256]{1,2,0:T(8,128)} %bitcast.110) | data formatting | bytes 16777216 | tf_op jit(solution)/shard_map/reshape | solution.py:81
  275.0 11.5 %gather_fusion.3 = f32[80,128,256]{2,1,0:T(8,128)} fusion(f32[64,128,256]{2,1,0:T(8,128)} %copy.77, s32[1024]{0:T(1024)S(1)} %pad_clamp_fusion), kind=kCustom, calls=%fused_computation.3 | custom fusion | bytes 20971840 | tf_op jit(solution)/shard_map/jit(_take)/gather | solution.py:85
  286.5 8.5 %fusion = f32[8,1280,256]{2,1,0:T(8,128)} fusion(pred[8,1280]{1,0:T(8,128)(4,1)S(1)} %get-tuple-element.35, pred[8,1280]{1,0:T(8,128)(4,1)S(1)} %get-tuple-element.36, f32[8,1280,256]{2,1,0:T(8,128)} %bitcast.112), kind=kLoop, calls=%fused_computation.6 | loop fusion | flops 5242880 | bytes 20992000 | tf_op jit(solution)/shard_map/jit(_where)/select_n | solution.py:84
  295.0 5.5 all-to-all-start.2
  302.0 9.2 %copy.84 = f32[8,8,128,256]{3,1,2,0:T(8,128)} copy(f32[8,8,128,256]{2,3,1,0:T(8,128)} %bitcast.111) | data formatting | bytes 16777216
  311.2 2.4 fusion.13
  313.6 214.9 %all-to-all-done.2 = f32[8,1280,256]{2,1,0:T(8,128)} async-done(((f32[8,1280,256]{2,1,0:T(8,128)}), f32[8,1280,256]{2,1,0:T(8,128)}, u32[]{:S(2)}, u32[]{:S(2)}) %all-to-all-start.2) | async-done | bytes 10485792 | tf_op jit(solution)/shard_map/all_to_all | solution.py:87
  528.5 11.6 %reshape.400 = f32[80,32768]{1,0:T(8,128)} reshape(f32[8,1280,256]{2,1,0:T(8,128)} %all-to-all-done.2) | data formatting | bytes 20971520 | tf_op jit(solution)/shard_map/reshape | solution.py:99
  540.1 6.2 fusion.15
  546.3 7.4 %convolution_add_fusion = f32[8,32768]{1,0:T(8,128)} fusion(f32[8,32768]{1,0:T(8,128)S(1)} %fusion.15, f32[64,32768]{1,0:T(8,128)} %bitcast.113, s32[64]{0:T(128)S(1)} %get-tuple-element.25, pred[64]{0:T(512)(128)(4,1)S(1)} %get-tuple-element.20), kind=kOutput, calls=%fused_computation.4 | convolution fusion | flops 201589760 | bytes 10486080 | tf_op jit(solution)/shard_map/no,nx->ox/dot_general | solution.py:101
  555.1 2.7 convolution_bitcast_fusion
  559.0 122.6 %all-reduce.5.cloned.1.call-done = f32[256,256]{0,1:T(8,128)} async-done(((f32[256,256]{0,1:T(8,128)}), f32[256,256]{0,1:T(8,128)}) %all-reduce.5.cloned.1.call-update) | async-done | bytes 262160 | tf_op jit(solution)/shard_map/psum | solution.py:109
  (57 shorter events, 10.9 us)
Async XLA Ops:
  7.2 155.7 %copy-start = (bf16[32,1,2,128,128]{4,3,2,1,0:T(8,128)(2,1)S(1)}, bf16[32,1,2,128,128]{4,3,2,1,0:T(8,128)(2,1)}, u32[]{:S(2)}) copy-start(bf16[32,1,2,128,128]{4,3,2,1,0:T(8,128)(2,1)} %param.8) | copy-start | bytes 6291460
  9.2 13.7 %all-to-all-start = ((s32[8,1,10]{2,1,0:T(1,128)}), s32[8,1,10]{2,1,0:T(1,128)S(1)}, u32[]{:S(2)}, u32[]{:S(2)}) async-start(s32[8,1,10]{2,1,0:T(1,128)} %bitcast.1), calls=%async_computation | async-start | bytes 8192 | tf_op jit(solution)/shard_map/all_to_all | solution.py:55
  38.2 5.1 copy-start.3
  38.2 119.3 %all-to-all-start.1 = ((bf16[8,1280,256]{2,1,0:T(8,128)(2,1)}), bf16[8,1280,256]{2,1,0:T(8,128)(2,1)}, u32[]{:S(2)}, u32[]{:S(2)}) async-start(bf16[8,1280,256]{2,1,0:T(8,128)(2,1)} %fusion.1), calls=%async_computation.1 | async-start | bytes 10485760 | tf_op jit(solution)/shard_map/all_to_all | solution.py:57
  43.0 212.0 %all-reduce.3.cloned.1.call-start = ((), (), s32[]{:S(2)}) async-start(), calls=%async_computation.3 | async-start | bytes 8388608 | tf_op jit(solution)/shard_map/psum | solution.py:72
  295.0 233.5 %all-to-all-start.2 = ((f32[8,1280,256]{2,1,0:T(8,128)}), f32[8,1280,256]{2,1,0:T(8,128)}, u32[]{:S(2)}, u32[]{:S(2)}) async-start(f32[8,1280,256]{2,1,0:T(8,128)} %fusion), calls=%async_computation.2 | async-start | bytes 20971520 | tf_op jit(solution)/shard_map/all_to_all | solution.py:87
  300.5 381.0 %all-reduce.5.cloned.1.call-start = ((), (), s32[]{:S(2)}) async-start(), calls=%async_computation.4 | async-start | bytes 524288 | tf_op jit(solution)/shard_map/psum | solution.py:109
  546.3 137.1 %copy-start.1 = (bf16[32,1,2,128,128]{4,3,2,1,0:T(8,128)(2,1)S(1)}, bf16[32,1,2,128,128]{4,3,2,1,0:T(8,128)(2,1)}, u32[]{:S(2)}) copy-start(bf16[32,1,2,128,128]{4,3,2,1,0:T(8,128)(2,1)} %param.8) | copy-start | bytes 6291460
  553.7 4.2 copy-start.2
Sparse Core Ops, SparseCore 0:
  170.4 84.5 all-reduce.2
  558.0 123.5 all-reduce.4
where the time goes:
time: 692 us; the launch traced here: 690 us
  waiting for transfers between devices  537 us (78%)
  local copies, waits for them, and re-layouts  61 us (9%)
  matrix products  30.9 us (4%)
  other arithmetic  28.8 us (4%)
  starting transfers between devices  17.8 us (3%)
  between operations  14.2 us (2%)
    all_to_all x1, waiting for transfers between devices, on_device(): lax.all_to_all(outgoing.reshape(peer_count, capacity * block_size, featur...  215 us
    psum x1, waiting for transfers between devices, on_device(): lax.psum(local_weight, ('rows', 'rep')) * (1.0 / math.sqrt(node_total))  123 us
    all_to_all x1, waiting for transfers between devices, on_device(): lax.all_to_all(serve_blocks(mixed_rows, asked_places, block_size), 'rows'...  111 us
    psum x1, waiting for transfers between devices, on_device(): summed = lax.psum(partial_sum, 'rep')  84.1 us
  transfers between devices with their start and end apart: 5, of which 5 were waited for; matrix products, arithmetic and copies ran while one was open for 3% of the time, Pallas kernels for 0%

commit v1 on v0

v1 whole, which is shorter than its diff:
```python
import functools
import math

import jax
import jax.numpy as jnp
from jax import lax
from jax.experimental import pallas as pl
from jax.experimental.pallas import tpu as pltpu
from jax.sharding import PartitionSpec as P

F32 = jnp.float32
BF16 = jnp.bfloat16
HALF = 128
SCALE = 2.0**-21
VMEM = pl.BlockSpec(memory_space=pltpu.VMEM)
SMEM = pl.BlockSpec(memory_space=pltpu.SMEM)


def ring_order(n):
    return list(range(0, n, 2)) + list(range(n - 1, 0, -2))


def split_dot(left, right, dims):
    high = left.astype(BF16)
    low = (left - high.astype(F32)).astype(BF16)
    out = lax.dot_general(high, right, (dims, ((), ())), preferred_element_type=F32)
    return out + lax.dot_general(low, right, (dims, ((), ())), preferred_element_type=F32)


def gather_ring(chunks, n):
    order = ring_order(n)
    ahead = [(order[i], order[(i + 1) % n]) for i in range(n)]
    behind = [(b, a) for a, b in ahead]
    right, left = list(chunks), list(chunks)
    pieces = [[c] + [None] * (n - 1) for c in chunks]
    for step in range(1, n // 2 + 1):
        for k in range(len(chunks)):
            last = step == n // 2
            if not last or k % 2 == 0:
                right[k] = lax.ppermute(right[k], "rows", ahead)
                pieces[k][step] = right[k]
            if not last or k % 2 == 1:
                left[k] = lax.ppermute(left[k], "rows", behind)
                pieces[k][n - step] = left[k]
    return pieces


def blocks_kernel(n, own_blocks, block, where_ref, rep_ref, vals_ref, *refs):
    pieces, (send_far, send_near, keep_far, keep_near, pool) = refs[:n], refs[n:]
    rows = own_blocks * block
    for p in range(n):
        pool[p * rows : (p + 1) * rows, :] = pieces[p][...]
    me = rep_ref[0]
    for mask, out in ((3, send_far), (1, send_near), (2, keep_far), (0, keep_near)):
        base = lax.bitwise_xor(me, mask) * own_blocks
        for j in range(own_blocks):
            total = None
            for s in range(2):
                item = (base + j) * 2 + s
                start = pl.multiple_of(where_ref[item] * block, block)
                term = jnp.dot(vals_ref[item], pool[pl.ds(start, block), :], preferred_element_type=F32)
                total = term if total is None else total + term
            out[j * block : (j + 1) * block, :] = total.astype(out.dtype)


def apply_blocks(where, rep, vals, pieces, own_blocks):
    n, block = len(pieces), vals.shape[-1]
    rows, width = pieces[0].shape
    shapes = [jax.ShapeDtypeStruct((rows, width), t) for t in (BF16, BF16, F32, F32)]
    size = vals.size * 2 + 2 * n * rows * width * 2 + rows * width * 12
    return pl.pallas_call(
        functools.partial(blocks_kernel, n, own_blocks, block),
        out_shape=shapes,
        in_specs=[SMEM, SMEM, VMEM] + [VMEM] * n,
        out_specs=[VMEM] * 4,
        scratch_shapes=[pltpu.VMEM((n * rows, width), BF16)],
        compiler_params=pltpu.CompilerParams(vmem_limit_bytes=size + (8 << 20)),
        cost_estimate=pl.CostEstimate(
            flops=2 * vals.size * width, bytes_accessed=size, transcendentals=0
        ),
        name="apply_blocks",
    )(where, rep, vals, *pieces)


def reduce_rep(parts):
    send_far, send_near, keep_far, keep_near = parts
    swap = [(i, i ^ 1) for i in range(4)]
    cross = [(i, i ^ 2) for i in range(4)]
    got_far = lax.ppermute(send_far, "rep", swap)
    got_near = lax.ppermute(send_near, "rep", swap)
    crossing = (keep_far + got_far.astype(F32)).astype(BF16)
    return keep_near, got_near, lax.ppermute(crossing, "rep", cross)


def joined(refs):
    halves = []
    for h in range(len(refs) // 3):
        near, got, cross = refs[3 * h : 3 * h + 3]
        halves.append(near[...] + got[...].astype(F32) + cross[...].astype(F32))
    return jnp.concatenate(halves, axis=1)


def middle_kernel(weight_ref, grad_ref, *refs):
    sums, (act_ref, held_ref, *masked_refs) = refs[:6], refs[6:]
    held = joined(sums)
    held_ref[...] = held
    summed = split_dot(held, weight_ref[...], ((1,), (0,))) * (1.0 / SCALE)
    gate = jax.nn.sigmoid(summed)
    act_ref[...] = (summed * gate).astype(BF16)
    slope = gate * (1.0 + summed * (1.0 - gate))
    masked = (grad_ref[...].astype(F32) * slope).astype(BF16)
    for h, ref in enumerate(masked_refs):
        ref[...] = masked[:, h * HALF : (h + 1) * HALF]


def middle(weight, grad, sums):
    rows, width = grad.shape
    shapes = [jax.ShapeDtypeStruct((rows, width), BF16), jax.ShapeDtypeStruct((rows, width), F32)]
    shapes += [jax.ShapeDtypeStruct((rows, HALF), BF16)] * (width // HALF)
    return pl.pallas_call(
        middle_kernel,
        out_shape=shapes,
        in_specs=[VMEM] * 8,
        out_specs=[VMEM] * len(shapes),
        compiler_params=pltpu.CompilerParams(vmem_limit_bytes=24 << 20),
        cost_estimate=pl.CostEstimate(
            flops=4 * rows * width * width, bytes_accessed=rows * width * 18, transcendentals=rows * width
        ),
        name="middle",
    )(weight, grad, *sums)


def last_kernel(weight_ref, *refs):
    back = joined(refs[:6])
    refs[6][...] = split_dot(back, weight_ref[...], ((1,), (1,))).astype(BF16)


def last(weight, sums):
    rows, width = sums[0].shape[0], weight.shape[0]
    return pl.pallas_call(
        last_kernel,
        out_shape=jax.ShapeDtypeStruct((rows, width), BF16),
        in_specs=[VMEM] * 7,
        out_specs=VMEM,
        compiler_params=pltpu.CompilerParams(vmem_limit_bytes=24 << 20),
        cost_estimate=pl.CostEstimate(
            flops=4 * rows * width * width, bytes_accessed=rows * width * 14, transcendentals=0
        ),
        name="last",
    )(weight, *sums)


def sum_everywhere(value, n):
    layer = lax.axis_index("rep")
    for bit in (0, 1):
        half = value.shape[0] // 2
        mine = lax.shift_right_logical(layer, bit) & 1
        pair = [(i, i ^ (1 << bit)) for i in range(4)]
        got = lax.ppermute(lax.dynamic_slice_in_dim(value, (1 - mine) * half, half, 0), "rep", pair)
        value = lax.dynamic_slice_in_dim(value, mine * half, half, 0) + got
    step = 1
    while step < n:
        value = value + lax.ppermute(value, "rows", [(i, i ^ step) for i in range(n)])
        step *= 2
    for bit in (1, 0):
        mine = lax.shift_right_logical(layer, bit) & 1
        other = lax.ppermute(value, "rep", [(i, i ^ (1 << bit)) for i in range(4)])
        value = jnp.where(
            mine == 0, jnp.concatenate([value, other], 0), jnp.concatenate([other, value], 0)
        )
    return value


def on_device(n, features, weight, block_cols, block_vals, out_grad):
    own_rows, width = features.shape
    block = block_vals.shape[-1]
    own_blocks = own_rows // block
    me, layer = lax.axis_index("rows"), lax.axis_index("rep")
    order = ring_order(n)
    place = [order.index(i) for i in range(n)]
    place = jnp.array(place, jnp.int32)
    cols = block_cols.reshape(-1)
    owners = cols // own_blocks
    owner_place = jnp.sum(
        jnp.where(owners[:, None] == jnp.arange(n, dtype=jnp.int32)[None, :], place[None, :], 0), axis=1
    )
    back_steps = (place[me] - owner_place + n) % n
    where = back_steps * own_blocks + cols % own_blocks
    rep = layer.astype(jnp.int32).reshape(1)
    vals = block_vals.reshape(-1, block, block)
    halves = width // HALF
    scaled = features * jnp.asarray(SCALE, BF16)

    def spread(chunks):
        sums = []
        for pieces in gather_ring(chunks, n):
            sums += reduce_rep(apply_blocks(where, rep, vals, pieces, own_blocks))
        return sums

    grad = lax.dynamic_slice_in_dim(out_grad, layer * own_rows, own_rows, 0)
    sums = spread([scaled[:, h * HALF : (h + 1) * HALF] for h in range(halves)])
    activated, held, *masked = middle(weight, grad, sums)
    local = jnp.concatenate([split_dot(held, m, ((0,), (0,))) for m in masked], axis=1)
    node_total = own_rows * n * 4
    weight_grad = sum_everywhere(local, n) * (1.0 / (SCALE * math.sqrt(node_total)))
    input_grad = last(weight, spread(masked))
    return activated, input_grad, weight_grad


def solution(mesh):
    placed = (
        P(("rows", "rep"), None),
        P(),
        P("rows", "rep", None),
        P("rows", "rep", None, None, None),
        P("rows", None),
    )
    return jax.shard_map(
        functools.partial(on_device, mesh.shape["rows"]),
        mesh=mesh,
        in_specs=placed,
        out_specs=(P(("rows", "rep"), None), P(("rows", "rep"), None), P()),
        check_vma=False,
    )
```

time: 692 us -> 165 us (0.24)
  waiting for transfers between devices: 537 us -> 69.1 us
  local copies, waits for them, and re-layouts: 61 us -> 21.6 us
  matrix products: 30.9 us -> 3.07 us
  starting transfers between devices: 17.8 us -> 44 us
  other arithmetic: 28.8 us -> 10.9 us
  Pallas kernels: 0 us -> 14.1 us
  between operations: 14.2 us -> 0.94 us
    all_to_all x3 -> x0, waiting for transfers between devices: 331 us -> none  [the longest x1 215 us: on_device(): lax.all_to_all(outgoing.reshape(peer_count, capacity * block_size, featur...]
    psum x2 -> x0, waiting for transfers between devices: 207 us -> none  [the longest x1 123 us: on_device(): lax.psum(local_weight, ('rows', 'rep')) * (1.0 / math.sqrt(node_total))]
    ppermute x0 -> x47, waiting for transfers between devices: none -> 69.1 us  [the longest x14 22.7 us: gather_ring(): left[k] = lax.ppermute(left[k], 'rows', behind)]
    ppermute x0 -> x47, starting transfers between devices: none -> 44 us  [the longest x14 16.8 us: gather_ring(): left[k] = lax.ppermute(left[k], 'rows', behind)]
    dot_general x7 -> x4, matrix products: 30.9 us -> 3.07 us  [the longest x2 1.56 us: split_dot(): lax.dot_general(low, right, (dims, ((), ())), preferred_element_type=F32)]
    gather x4 -> x0, local copies, waits for them, and re-layouts: 25.3 us -> none  [the longest x1 11.5 us: on_device(): jnp.take(slot_terms, filler, axis=0)]
    reshape x4 -> x1, local copies, waits for them, and re-layouts: 22.1 us -> 0.1 us  [on_device(): cols = block_cols.reshape(-1)]
    select_n x5 -> x2, other arithmetic: 17.8 us -> 0.14 us  [the longest x1 0.14 us: sum_everywhere(): jnp.where(mine == 0, jnp.concatenate([value, other], 0), jnp.concatenate(...]
  transfers between devices with their start and end apart: 5 -> 47, of which waited for: 5 -> 23; matrix products, arithmetic and copies ran while one was open for 3% -> 9% of each run, Pallas kernels for 0% -> 6%
where the time goes in v1:
time: 165 us; the launch traced here: 164 us
  waiting for transfers between devices  69.1 us (42%)
  starting transfers between devices  44 us (27%)
  local copies, waits for them, and re-layouts  21.6 us (13%)
  Pallas kernels  14.1 us (9%)
  other arithmetic  10.9 us (7%)
  matrix products  3.07 us (2%)
    ppermute x14, waiting for transfers between devices, gather_ring(): left[k] = lax.ppermute(left[k], 'rows', behind)  22.7 us
    unnamed x64, local copies, waits for them, and re-layouts  20.7 us
    ppermute x14, waiting for transfers between devices, gather_ring(): right[k] = lax.ppermute(right[k], 'rows', ahead)  19 us
    ppermute x14, starting transfers between devices, gather_ring(): left[k] = lax.ppermute(left[k], 'rows', behind)  16.8 us
    ppermute x4, waiting for transfers between devices, reduce_rep(): return (keep_near, got_near, lax.ppermute(crossing, 'rep', cross))  15.8 us
    ppermute x14, starting transfers between devices, gather_ring(): right[k] = lax.ppermute(right[k], 'rows', ahead)  13.8 us
    ppermute x3, waiting for transfers between devices, sum_everywhere(): lax.ppermute(value, 'rows', [(i, i ^ step) for i in range(n)])  10.6 us
    pallas_call x4, Pallas kernels, apply_blocks(): pl.pallas_call(functools.partial(blocks_kernel, n, own_blocks, block), ou...  10.2 us
  transfers between devices with their start and end apart: 47, of which 23 were waited for; matrix products, arithmetic and copies ran while one was open for 9% of the time, Pallas kernels for 6%

profile of v1, /device:TPU:0, one launch (start us, length us, event | category | flops | bytes accessed | tf_op | source)
XLA Modules:
  0.0 163.7 jit_solution(3509093682754307202)
XLA Ops:
  2.0 3.0 %collective-permute-start.13 = (bf16[1024,128]{1,0:T(8,128)(2,1)S(1)}, bf16[1024,128]{1,0:T(8,128)(2,1)S(1)}, u32[]{:S(2)}, u32[]{:S(2)}) collective-permute-start(bf16[1024,128]{1,0:T(8,128)(2,1)S(1)} %get-tuple-element.52.refs_0_), channel_id=1, source_target_pairs={{8,0},{16,8},{24,16},{28,24},{20,28},{12,20},{4,12},{0,4},{9,1},{1... | collective-permute-start | bytes 786440 | tf_op jit(solution)/shard_map/ppermute | solution.py:43
  5.1 2.0 %collective-permute-start.10 = (bf16[1024,128]{1,0:T(8,128)(2,1)S(1)}, bf16[1024,128]{1,0:T(8,128)(2,1)}, u32[]{:S(2)}, u32[]{:S(2)}) collective-permute-start(bf16[1024,128]{1,0:T(8,128)(2,1)S(1)} %get-tuple-element.52.refs_0_), channel_id=1, source_target_pairs={{0,8},{8,16},{16,24},{24,28},{28,20},{20,12},{12,4},{4,0},{1,9},{9... | collective-permute-start | bytes 786440 | tf_op jit(solution)/shard_map/ppermute | solution.py:40
  7.1 4.3 %collective-permute-done.13.refs_7_ = bf16[1024,128]{1,0:T(8,128)(2,1)S(1)} collective-permute-done((bf16[1024,128]{1,0:T(8,128)(2,1)S(1)}, bf16[1024,128]{1,0:T(8,128)(2,1)S(1)}, u32[]{:S(2)}, u32[]{:S(2)}) %collective-permute-start.13) | collective-permute-done | bytes 262176 | tf_op jit(solution)/shard_map/ppermute | solution.py:43
  15.1 4.9 %collective-permute-done.10.refs_1_ = bf16[1024,128]{1,0:T(8,128)(2,1)} collective-permute-done((bf16[1024,128]{1,0:T(8,128)(2,1)S(1)}, bf16[1024,128]{1,0:T(8,128)(2,1)}, u32[]{:S(2)}, u32[]{:S(2)}) %collective-permute-start.10) | collective-permute-done | bytes 262176 | tf_op jit(solution)/shard_map/ppermute | solution.py:40
  22.6 3.6 %collective-permute-done.4.refs_7_ = bf16[1024,128]{1,0:T(8,128)(2,1)S(1)} collective-permute-done((bf16[1024,128]{1,0:T(8,128)(2,1)S(1)}, bf16[1024,128]{1,0:T(8,128)(2,1)S(1)}, u32[]{:S(2)}, u32[]{:S(2)}) %collective-permute-start.4) | collective-permute-done | bytes 262176 | tf_op jit(solution)/shard_map/ppermute | solution.py:43
  28.3 2.9 %collective-permute-done.11.refs_2_ = bf16[1024,128]{1,0:T(8,128)(2,1)} collective-permute-done((bf16[1024,128]{1,0:T(8,128)(2,1)}, bf16[1024,128]{1,0:T(8,128)(2,1)}, u32[]{:S(2)}, u32[]{:S(2)}) %collective-permute-start.11) | collective-permute-done | bytes 262176 | tf_op jit(solution)/shard_map/ppermute | solution.py:40
  34.3 3.3 %collective-permute-done.5.refs_6_ = bf16[1024,128]{1,0:T(8,128)(2,1)} collective-permute-done((bf16[1024,128]{1,0:T(8,128)(2,1)S(1)}, bf16[1024,128]{1,0:T(8,128)(2,1)}, u32[]{:S(2)}, u32[]{:S(2)}) %collective-permute-start.5) | collective-permute-done | bytes 262176 | tf_op jit(solution)/shard_map/ppermute | solution.py:43
  40.3 2.8 %collective-permute-done.12.refs_3_ = bf16[1024,128]{1,0:T(8,128)(2,1)} collective-permute-done((bf16[1024,128]{1,0:T(8,128)(2,1)}, bf16[1024,128]{1,0:T(8,128)(2,1)}, u32[]{:S(2)}, u32[]{:S(2)}) %collective-permute-start.12) | collective-permute-done | bytes 262176 | tf_op jit(solution)/shard_map/ppermute | solution.py:40
  44.8 2.7 %apply_blocks.5 = (bf16[1024,128]{1,0:T(8,128)(2,1)S(1)}, bf16[1024,128]{1,0:T(8,128)(2,1)}, f32[1024,128]{1,0:T(8,128)S(1)}, f32[1024,128]{1,0:T(8,128)S(1)}) custom-call(s32[64]{0:T(128)S(1)} %fusion.4.where_ref, s32[1]{0:T(128)} %bitcast.1.rep_ref, bf16[64,128,128]{2,1,0:T(8,128)(2,1)S(1)} %bitcast.9, bf16[1024,128]{1,0:T(8,128)(2,1)S(1)} %get-tuple-element.52.refs_0_, ...), custom_call_target="tpu_custom_call" | custom-call | flops 268435456 | bytes 7864320 | tf_op jit(solution)/shard_map/apply_blocks/pallas_call | solution.py:71
  48.3 2.1 %apply_blocks.4 = (bf16[1024,128]{1,0:T(8,128)(2,1)S(1)}, bf16[1024,128]{1,0:T(8,128)(2,1)S(1)}, f32[1024,128]{1,0:T(8,128)S(1)}, f32[1024,128]{1,0:T(8,128)S(1)}) custom-call(s32[64]{0:T(128)S(1)} %fusion.4.where_ref, s32[1]{0:T(128)} %bitcast.1.rep_ref, bf16[64,128,128]{2,1,0:T(8,128)(2,1)S(1)} %bitcast.10, ...), custom_call_target="tpu_custom_call" | custom-call | flops 268435456 | bytes 7864320 | tf_op jit(solution)/shard_map/apply_blocks/pallas_call | solution.py:71
  56.5 5.1 %collective-permute-done.19.refs_5_ = bf16[1024,128]{1,0:T(8,128)(2,1)S(1)} collective-permute-done((bf16[1024,128]{1,0:T(8,128)(2,1)}, bf16[1024,128]{1,0:T(8,128)(2,1)S(1)}, u32[]{:S(2)}, u32[]{:S(2)}) %collective-permute-start.19) | collective-permute-done | bytes 262176 | tf_op jit(solution)/shard_map/ppermute | solution.py:92
  62.3 4.0 %collective-permute-done.9.refs_2_ = bf16[1024,128]{1,0:T(8,128)(2,1)S(1)} collective-permute-done((bf16[1024,128]{1,0:T(8,128)(2,1)}, bf16[1024,128]{1,0:T(8,128)(2,1)S(1)}, u32[]{:S(2)}, u32[]{:S(2)}) %collective-permute-start.9) | collective-permute-done | bytes 262176 | tf_op jit(solution)/shard_map/ppermute | solution.py:92
  78.9 5.2 %collective-permute-done.20.refs_1_ = bf16[1024,128]{1,0:T(8,128)(2,1)} collective-permute-done((bf16[1024,128]{1,0:T(8,128)(2,1)}, bf16[1024,128]{1,0:T(8,128)(2,1)}, u32[]{:S(2)}, u32[]{:S(2)}) %collective-permute-start.20) | collective-permute-done | bytes 262176 | tf_op jit(solution)/shard_map/ppermute | solution.py:40
  87.8 3.7 %collective-permute-done.33.refs_7_ = bf16[1024,128]{1,0:T(8,128)(2,1)} collective-permute-done((bf16[1024,128]{1,0:T(8,128)(2,1)S(1)}, bf16[1024,128]{1,0:T(8,128)(2,1)}, u32[]{:S(2)}, u32[]{:S(2)}) %collective-permute-start.33) | collective-permute-done | bytes 262176 | tf_op jit(solution)/shard_map/ppermute | solution.py:43
  91.8 1.8 %collective-permute-done.21.refs_2_ = bf16[1024,128]{1,0:T(8,128)(2,1)} collective-permute-done((bf16[1024,128]{1,0:T(8,128)(2,1)}, bf16[1024,128]{1,0:T(8,128)(2,1)}, u32[]{:S(2)}, u32[]{:S(2)}) %collective-permute-start.21) | collective-permute-done | bytes 262176 | tf_op jit(solution)/shard_map/ppermute | solution.py:40
  108.2 5.0 %collective-permute-done.35.refs_5_ = bf16[1024,128]{1,0:T(8,128)(2,1)} collective-permute-done((bf16[1024,128]{1,0:T(8,128)(2,1)}, bf16[1024,128]{1,0:T(8,128)(2,1)}, u32[]{:S(2)}, u32[]{:S(2)}) %collective-permute-start.35) | collective-permute-done | bytes 262176 | tf_op jit(solution)/shard_map/ppermute | solution.py:43
  118.6 2.7 %apply_blocks.6 = (bf16[1024,128]{1,0:T(8,128)(2,1)}, bf16[1024,128]{1,0:T(8,128)(2,1)S(1)}, f32[1024,128]{1,0:T(8,128)S(1)}, f32[1024,128]{1,0:T(8,128)S(1)}) custom-call(s32[64]{0:T(128)S(1)} %fusion.4.where_ref, s32[1]{0:T(128)} %bitcast.1.rep_ref, bf16[64,128,128]{2,1,0:T(8,128)(2,1)S(1)} %bitcast.11, bf16[1024,128]{1,0:T(8,128)(2,1)} %get-tuple-element.32.refs_0_, ...), custom_call_target="tpu_custom_call" | custom-call | flops 268435456 | bytes 7864320 | tf_op jit(solution)/shard_map/apply_blocks/pallas_call | solution.py:71
  121.8 5.6 %collective-permute-done.42 = f32[64,256]{0,1:T(8,128)S(1)} collective-permute-done((f32[64,256]{0,1:T(8,128)S(1)}, f32[64,256]{0,1:T(8,128)S(1)}, u32[]{:S(2)}, u32[]{:S(2)}) %collective-permute-start.42) | collective-permute-done | bytes 65568 | tf_op jit(solution)/shard_map/ppermute | solution.py:163
  129.1 3.5 %collective-permute-done.43 = f32[64,256]{0,1:T(8,128)S(1)} collective-permute-done((f32[64,256]{0,1:T(8,128)S(1)}, f32[64,256]{0,1:T(8,128)S(1)}, u32[]{:S(2)}, u32[]{:S(2)}) %collective-permute-start.43) | collective-permute-done | bytes 65568 | tf_op jit(solution)/shard_map/ppermute | solution.py:163
  133.3 2.6 %collective-permute-start.44 = (f32[64,256]{0,1:T(8,128)}, f32[64,256]{0,1:T(8,128)}, u32[]{:S(2)}, u32[]{:S(2)}) collective-permute-start(f32[64,256]{0,1:T(8,128)} %add.91), channel_id=1, source_target_pairs={{0,16},{4,20},{8,24},{12,28},{16,0},{20,4},{24,8},{28,12},{1,17},{... | collective-permute-start | bytes 196616 | tf_op jit(solution)/shard_map/ppermute | solution.py:163
  135.9 2.6 %apply_blocks.7 = (bf16[1024,128]{1,0:T(8,128)(2,1)}, bf16[1024,128]{1,0:T(8,128)(2,1)S(1)}, f32[1024,128]{1,0:T(8,128)S(1)}, f32[1024,128]{1,0:T(8,128)S(1)}) custom-call(s32[64]{0:T(128)S(1)} %fusion.4.where_ref, s32[1]{0:T(128)} %bitcast.1.rep_ref, bf16[64,128,128]{2,1,0:T(8,128)(2,1)S(1)} %bitcast.12, bf16[1024,128]{1,0:T(8,128)(2,1)S(1)} %get-tuple-element.37.refs_0_, ...), custom_call_target="tpu_custom_call" | custom-call | flops 268435456 | bytes 7864320 | tf_op jit(solution)/shard_map/apply_blocks/pallas_call | solution.py:71
  153.7 2.1 %collective-permute-done.29.refs_2_ = bf16[1024,128]{1,0:T(8,128)(2,1)} collective-permute-done((bf16[1024,128]{1,0:T(8,128)(2,1)}, bf16[1024,128]{1,0:T(8,128)(2,1)}, u32[]{:S(2)}, u32[]{:S(2)}) %collective-permute-start.29) | collective-permute-done | bytes 262176 | tf_op jit(solution)/shard_map/ppermute | solution.py:92
  155.8 4.6 %collective-permute-done.39.refs_5_ = bf16[1024,128]{1,0:T(8,128)(2,1)S(1)} collective-permute-done((bf16[1024,128]{1,0:T(8,128)(2,1)}, bf16[1024,128]{1,0:T(8,128)(2,1)S(1)}, u32[]{:S(2)}, u32[]{:S(2)}) %collective-permute-start.39) | collective-permute-done | bytes 262176 | tf_op jit(solution)/shard_map/ppermute | solution.py:92
  161.4 2.3 %last.1 = bf16[1024,256]{1,0:T(8,128)(2,1)} custom-call(bf16[256,256]{1,0:T(8,128)(2,1)S(1)} %copy-done.11, f32[1024,128]{1,0:T(8,128)S(1)} %copy-done.4, bf16[1024,128]{1,0:T(8,128)(2,1)S(1)} %collective-permute-done.27.refs_1_, bf16[1024,128]{1,0:T(8,128)(2,1)} %collective-permute-done.29.refs_2_, f32[1024,128]{1,0:T(8,128)S(1)} %copy-done.8, ...), custom_call_target="tpu_custom_call" | custom-call | flops 268435456 | bytes 3670016 | tf_op jit(solution)/shard_map/last/pallas_call | solution.py:140
  (165 shorter events, 80.4 us)
Async XLA Ops:
  5.1 14.8 %collective-permute-start.10 = (bf16[1024,128]{1,0:T(8,128)(2,1)S(1)}, bf16[1024,128]{1,0:T(8,128)(2,1)}, u32[]{:S(2)}, u32[]{:S(2)}) collective-permute-start(bf16[1024,128]{1,0:T(8,128)(2,1)S(1)} %get-tuple-element.52.refs_0_), channel_id=1, source_target_pairs={{0,8},{8,16},{16,24},{24,28},{28,20},{20,12},{12,4},{4,0},{1,9},{9... | collective-permute-start | bytes 786440 | tf_op jit(solution)/shard_map/ppermute | solution.py:40
  13.0 13.2 %collective-permute-start.4 = (bf16[1024,128]{1,0:T(8,128)(2,1)S(1)}, bf16[1024,128]{1,0:T(8,128)(2,1)S(1)}, u32[]{:S(2)}, u32[]{:S(2)}) collective-permute-start(bf16[1024,128]{1,0:T(8,128)(2,1)S(1)} %get-tuple-element.53.refs_0_), channel_id=1, source_target_pairs={{8,0},{16,8},{24,16},{28,24},{20,28},{12,20},{4,12},{0,4},{9,1},{1... | collective-permute-start | bytes 786440 | tf_op jit(solution)/shard_map/ppermute | solution.py:43
  14.6 13.3 %collective-permute-start.1 = (bf16[1024,128]{1,0:T(8,128)(2,1)S(1)}, bf16[1024,128]{1,0:T(8,128)(2,1)}, u32[]{:S(2)}, u32[]{:S(2)}) collective-permute-start(bf16[1024,128]{1,0:T(8,128)(2,1)S(1)} %collective-permute-done.refs_1_), channel_id=1, source_target_pairs={{0,8},{8,16},{16,24},{24,28},{28,20},{20,12},{12,4},{4,0},{1,9},{9... | collective-permute-start | bytes 786440 | tf_op jit(solution)/shard_map/ppermute | solution.py:40
  19.9 11.2 %collective-permute-start.11 = (bf16[1024,128]{1,0:T(8,128)(2,1)}, bf16[1024,128]{1,0:T(8,128)(2,1)}, u32[]{:S(2)}, u32[]{:S(2)}) collective-permute-start(bf16[1024,128]{1,0:T(8,128)(2,1)} %collective-permute-done.10.refs_1_), channel_id=1, source_target_pairs={{0,8},{8,16},{16,24},{24,28},{28,20},{20,12},{12,4},{4,0},{1,9},{9... | collective-permute-start | bytes 786440 | tf_op jit(solution)/shard_map/ppermute | solution.py:40
  20.7 11.2 %collective-permute-start.15 = (bf16[1024,128]{1,0:T(8,128)(2,1)}, bf16[1024,128]{1,0:T(8,128)(2,1)}, u32[]{:S(2)}, u32[]{:S(2)}) collective-permute-start(bf16[1024,128]{1,0:T(8,128)(2,1)} %collective-permute-done.14.refs_6_), channel_id=1, source_target_pairs={{8,0},{16,8},{24,16},{28,24},{20,28},{12,20},{4,12},{0,4},{9,1},{1... | collective-permute-start | bytes 786440 | tf_op jit(solution)/shard_map/ppermute | solution.py:43
  26.2 11.3 %collective-permute-start.5 = (bf16[1024,128]{1,0:T(8,128)(2,1)S(1)}, bf16[1024,128]{1,0:T(8,128)(2,1)}, u32[]{:S(2)}, u32[]{:S(2)}) collective-permute-start(bf16[1024,128]{1,0:T(8,128)(2,1)S(1)} %collective-permute-done.4.refs_7_), channel_id=1, source_target_pairs={{8,0},{16,8},{24,16},{28,24},{20,28},{12,20},{4,12},{0,4},{9,1},{1... | collective-permute-start | bytes 786440 | tf_op jit(solution)/shard_map/ppermute | solution.py:43
  27.9 11.3 %collective-permute-start.2 = (bf16[1024,128]{1,0:T(8,128)(2,1)}, bf16[1024,128]{1,0:T(8,128)(2,1)}, u32[]{:S(2)}, u32[]{:S(2)}) collective-permute-start(bf16[1024,128]{1,0:T(8,128)(2,1)} %collective-permute-done.1.refs_2_), channel_id=1, source_target_pairs={{0,8},{8,16},{16,24},{24,28},{28,20},{20,12},{12,4},{4,0},{1,9},{9... | collective-permute-start | bytes 786440 | tf_op jit(solution)/shard_map/ppermute | solution.py:40
  31.2 11.9 %collective-permute-start.12 = (bf16[1024,128]{1,0:T(8,128)(2,1)}, bf16[1024,128]{1,0:T(8,128)(2,1)}, u32[]{:S(2)}, u32[]{:S(2)}) collective-permute-start(bf16[1024,128]{1,0:T(8,128)(2,1)} %collective-permute-done.11.refs_2_), channel_id=1, source_target_pairs={{0,8},{8,16},{16,24},{24,28},{28,20},{20,12},{12,4},{4,0},{1,9},{9... | collective-permute-start | bytes 786440 | tf_op jit(solution)/shard_map/ppermute | solution.py:40
  31.9 11.2 %collective-permute-start.16 = (bf16[1024,128]{1,0:T(8,128)(2,1)}, bf16[1024,128]{1,0:T(8,128)(2,1)}, u32[]{:S(2)}, u32[]{:S(2)}) collective-permute-start(bf16[1024,128]{1,0:T(8,128)(2,1)} %collective-permute-done.15.refs_5_), channel_id=1, source_target_pairs={{8,0},{16,8},{24,16},{28,24},{20,28},{12,20},{4,12},{0,4},{9,1},{1... | collective-permute-start | bytes 786440 | tf_op jit(solution)/shard_map/ppermute | solution.py:43
  37.6 10.7 %collective-permute-start.6 = (bf16[1024,128]{1,0:T(8,128)(2,1)}, bf16[1024,128]{1,0:T(8,128)(2,1)}, u32[]{:S(2)}, u32[]{:S(2)}) collective-permute-start(bf16[1024,128]{1,0:T(8,128)(2,1)} %collective-permute-done.5.refs_6_), channel_id=1, source_target_pairs={{8,0},{16,8},{24,16},{28,24},{20,28},{12,20},{4,12},{0,4},{9,1},{1... | collective-permute-start | bytes 786440 | tf_op jit(solution)/shard_map/ppermute | solution.py:43
  54.7 11.7 %collective-permute-start.9 = (bf16[1024,128]{1,0:T(8,128)(2,1)}, bf16[1024,128]{1,0:T(8,128)(2,1)S(1)}, u32[]{:S(2)}, u32[]{:S(2)}) collective-permute-start(bf16[1024,128]{1,0:T(8,128)(2,1)} %add_convert_fusion.3), channel_id=1, source_target_pairs={{0,2},{1,3},{2,0},{3,1},{4,6},{5,7},{6,4},{7,5},{8,10},{9,11},{10,... | collective-permute-start | bytes 786440 | tf_op jit(solution)/shard_map/ppermute | solution.py:92
  76.3 11.1 %collective-permute-start.24 = (bf16[1024,128]{1,0:T(8,128)(2,1)}, bf16[1024,128]{1,0:T(8,128)(2,1)}, u32[]{:S(2)}, u32[]{:S(2)}) collective-permute-start(bf16[1024,128]{1,0:T(8,128)(2,1)} %get-tuple-element.32.refs_0_), channel_id=1, source_target_pairs={{8,0},{16,8},{24,16},{28,24},{20,28},{12,20},{4,12},{0,4},{9,1},{1... | collective-permute-start | bytes 786440 | tf_op jit(solution)/shard_map/ppermute | solution.py:43
  76.6 14.9 %collective-permute-start.33 = (bf16[1024,128]{1,0:T(8,128)(2,1)S(1)}, bf16[1024,128]{1,0:T(8,128)(2,1)}, u32[]{:S(2)}, u32[]{:S(2)}) collective-permute-start(bf16[1024,128]{1,0:T(8,128)(2,1)S(1)} %get-tuple-element.37.refs_0_), channel_id=1, source_target_pairs={{8,0},{16,8},{24,16},{28,24},{20,28},{12,20},{4,12},{0,4},{9,1},{1... | collective-permute-start | bytes 786440 | tf_op jit(solution)/shard_map/ppermute | solution.py:43
  78.3 18.9 %collective-permute-start.30 = (bf16[1024,128]{1,0:T(8,128)(2,1)S(1)}, bf16[1024,128]{1,0:T(8,128)(2,1)}, u32[]{:S(2)}, u32[]{:S(2)}) collective-permute-start(bf16[1024,128]{1,0:T(8,128)(2,1)S(1)} %get-tuple-element.37.refs_0_), channel_id=1, source_target_pairs={{0,8},{8,16},{16,24},{24,28},{28,20},{20,12},{12,4},{4,0},{1,9},{9... | collective-permute-start | bytes 786440 | tf_op jit(solution)/shard_map/ppermute | solution.py:40
  87.5 11.4 %collective-permute-start.25 = (bf16[1024,128]{1,0:T(8,128)(2,1)}, bf16[1024,128]{1,0:T(8,128)(2,1)}, u32[]{:S(2)}, u32[]{:S(2)}) collective-permute-start(bf16[1024,128]{1,0:T(8,128)(2,1)} %collective-permute-done.24.refs_7_), channel_id=1, source_target_pairs={{8,0},{16,8},{24,16},{28,24},{20,28},{12,20},{4,12},{0,4},{9,1},{1... | collective-permute-start | bytes 786440 | tf_op jit(solution)/shard_map/ppermute | solution.py:43
  98.8 14.8 %collective-permute-start.26 = (bf16[1024,128]{1,0:T(8,128)(2,1)}, bf16[1024,128]{1,0:T(8,128)(2,1)S(1)}, u32[]{:S(2)}, u32[]{:S(2)}) collective-permute-start(bf16[1024,128]{1,0:T(8,128)(2,1)} %collective-permute-done.25.refs_6_), channel_id=1, source_target_pairs={{8,0},{16,8},{24,16},{28,24},{20,28},{12,20},{4,12},{0,4},{9,1},{1... | collective-permute-start | bytes 786440 | tf_op jit(solution)/shard_map/ppermute | solution.py:43
  100.7 12.5 %collective-permute-start.35 = (bf16[1024,128]{1,0:T(8,128)(2,1)}, bf16[1024,128]{1,0:T(8,128)(2,1)}, u32[]{:S(2)}, u32[]{:S(2)}) collective-permute-start(bf16[1024,128]{1,0:T(8,128)(2,1)} %collective-permute-done.34.refs_6_), channel_id=1, source_target_pairs={{8,0},{16,8},{24,16},{28,24},{20,28},{12,20},{4,12},{0,4},{9,1},{1... | collective-permute-start | bytes 786440 | tf_op jit(solution)/shard_map/ppermute | solution.py:43
  101.0 13.4 %collective-permute-start.23 = (bf16[1024,128]{1,0:T(8,128)(2,1)}, bf16[1024,128]{1,0:T(8,128)(2,1)S(1)}, u32[]{:S(2)}, u32[]{:S(2)}) collective-permute-start(bf16[1024,128]{1,0:T(8,128)(2,1)} %collective-permute-done.22.refs_3_), channel_id=1, source_target_pairs={{0,8},{8,16},{16,24},{24,28},{28,20},{20,12},{12,4},{4,0},{1,9},{9... | collective-permute-start | bytes 786440 | tf_op jit(solution)/shard_map/ppermute | solution.py:40
  103.7 17.6 %collective-permute-start.41 = (f32[64,256]{0,1:T(8,128)S(1)}, f32[64,256]{0,1:T(8,128)S(1)}, u32[]{:S(2)}, u32[]{:S(2)}) collective-permute-start(f32[64,256]{0,1:T(8,128)S(1)} %constant_dynamic-slice_fusion), channel_id=1, source_target_pairs={{0,2},{1,3},{2,0},{3,1},{4,6},{5,7},{6,4},{7,5},{8,10},{9,11},{10,... | collective-permute-start | bytes 196616 | tf_op jit(solution)/shard_map/ppermute | solution.py:159
  106.7 29.2 %collective-permute-start.32 = (bf16[1024,128]{1,0:T(8,128)(2,1)}, bf16[1024,128]{1,0:T(8,128)(2,1)S(1)}, u32[]{:S(2)}, u32[]{:S(2)}) collective-permute-start(bf16[1024,128]{1,0:T(8,128)(2,1)} %collective-permute-done.31.refs_2_), channel_id=1, source_target_pairs={{0,8},{8,16},{16,24},{24,28},{28,20},{20,12},{12,4},{4,0},{1,9},{9... | collective-permute-start | bytes 786440 | tf_op jit(solution)/shard_map/ppermute | solution.py:40
  113.2 22.6 %collective-permute-start.36 = (bf16[1024,128]{1,0:T(8,128)(2,1)}, bf16[1024,128]{1,0:T(8,128)(2,1)S(1)}, u32[]{:S(2)}, u32[]{:S(2)}) collective-permute-start(bf16[1024,128]{1,0:T(8,128)(2,1)} %collective-permute-done.35.refs_5_), channel_id=1, source_target_pairs={{8,0},{16,8},{24,16},{28,24},{20,28},{12,20},{4,12},{0,4},{9,1},{1... | collective-permute-start | bytes 786440 | tf_op jit(solution)/shard_map/ppermute | solution.py:43
  121.3 23.2 %collective-permute-start.28 = (bf16[1024,128]{1,0:T(8,128)(2,1)}, bf16[1024,128]{1,0:T(8,128)(2,1)}, u32[]{:S(2)}, u32[]{:S(2)}) collective-permute-start(bf16[1024,128]{1,0:T(8,128)(2,1)} %get-tuple-element.36), channel_id=1, source_target_pairs={{0,1},{1,0},{2,3},{3,2},{4,5},{5,4},{6,7},{7,6},{8,9},{9,8},{10,11... | collective-permute-start | bytes 786440 | tf_op jit(solution)/shard_map/ppermute | solution.py:89
  144.0 9.7 %collective-permute-start.27 = (bf16[1024,128]{1,0:T(8,128)(2,1)}, bf16[1024,128]{1,0:T(8,128)(2,1)S(1)}, u32[]{:S(2)}, u32[]{:S(2)}) collective-permute-start(bf16[1024,128]{1,0:T(8,128)(2,1)} %copy-done.24), channel_id=1, source_target_pairs={{0,1},{1,0},{2,3},{3,2},{4,5},{5,4},{6,7},{7,6},{8,9},{9,8},{10,11... | collective-permute-start | bytes 786440 | tf_op jit(solution)/shard_map/ppermute | solution.py:90
  148.6 11.8 %collective-permute-start.39 = (bf16[1024,128]{1,0:T(8,128)(2,1)}, bf16[1024,128]{1,0:T(8,128)(2,1)S(1)}, u32[]{:S(2)}, u32[]{:S(2)}) collective-permute-start(bf16[1024,128]{1,0:T(8,128)(2,1)} %add_convert_fusion), channel_id=1, source_target_pairs={{0,2},{1,3},{2,0},{3,1},{4,6},{5,7},{6,4},{7,5},{8,10},{9,11},{10,... | collective-permute-start | bytes 786440 | tf_op jit(solution)/shard_map/ppermute | solution.py:92
  (54 other events, 370.7 us)

commit v2 on v1

v2 whole, which is shorter than its diff:
```python
import functools
import math

import jax
import jax.numpy as jnp
from jax import lax
from jax.experimental import pallas as pl
from jax.experimental.pallas import tpu as pltpu
from jax.sharding import PartitionSpec as P

F32 = jnp.float32
BF16 = jnp.bfloat16
HALF = 128
SCALE = 2.0**-21
VMEM = pl.BlockSpec(memory_space=pltpu.VMEM)
SMEM = pl.BlockSpec(memory_space=pltpu.SMEM)


def ring_order(n):
    return list(range(0, n, 2)) + list(range(n - 1, 0, -2))


def ring_place(i, n):
    return jnp.where(i % 2 == 0, i // 2, n - 1 - i // 2)


def split_dot(left, right, dims):
    high = left.astype(BF16)
    low = (left - high.astype(F32)).astype(BF16)
    out = lax.dot_general(high, right, (dims, ((), ())), preferred_element_type=F32)
    return out + lax.dot_general(low, right, (dims, ((), ())), preferred_element_type=F32)


def tie(arrays, other):
    return lax.optimization_barrier((arrays, other))[0]


def gather_ring(chunks, n, beside=None):
    order = ring_order(n)
    ahead = [(order[i], order[(i + 1) % n]) for i in range(n)]
    behind = [(b, a) for a, b in ahead]
    right, left = list(chunks), list(chunks)
    pieces = [[c] + [None] * (n - 1) for c in chunks]
    for step in range(1, n // 2 + 1):
        for k in range(len(chunks)):
            last = step == n // 2
            if beside and (step, k) in beside:
                right[k], left[k] = tie((right[k], left[k]), beside[step, k](before))
            before = right[k]
            if not last or k % 2 == 0:
                right[k] = lax.ppermute(right[k], "rows", ahead)
                pieces[k][step] = right[k]
            if not last or k % 2 == 1:
                left[k] = lax.ppermute(left[k], "rows", behind)
                pieces[k][n - step] = left[k]
    return pieces


def blocks_kernel(n, own_blocks, block, scale, where_ref, rep_ref, vals_ref, *refs):
    pieces, (send, keep_far, keep_near, pool) = refs[:n], refs[n:]
    rows = own_blocks * block
    for p in range(n):
        piece = pieces[p][...]
        pool[p * rows : (p + 1) * rows, :] = piece if scale is None else piece * jnp.asarray(scale, BF16)
    me = rep_ref[0]
    for mask, out, first in ((3, send, 0), (1, send, own_blocks), (2, keep_far, 0), (0, keep_near, 0)):
        base = lax.bitwise_xor(me, mask) * own_blocks
        for j in range(own_blocks):
            total = None
            for s in range(2):
                item = (base + j) * 2 + s
                start = pl.multiple_of(where_ref[item] * block, block)
                term = jnp.dot(vals_ref[item], pool[pl.ds(start, block), :], preferred_element_type=F32)
                total = term if total is None else total + term
            out[(first + j) * block : (first + j + 1) * block, :] = total.astype(out.dtype)


def apply_blocks(where, rep, vals, pieces, own_blocks, scale):
    n, block = len(pieces), vals.shape[-1]
    rows, width = pieces[0].shape
    shapes = [jax.ShapeDtypeStruct((2 * rows, width), BF16)]
    shapes += [jax.ShapeDtypeStruct((rows, width), F32)] * 2
    size = vals.size * 2 + 2 * n * rows * width * 2 + rows * width * 12
    return pl.pallas_call(
        functools.partial(blocks_kernel, n, own_blocks, block, scale),
        out_shape=shapes,
        in_specs=[SMEM, SMEM, VMEM] + [VMEM] * n,
        out_specs=[VMEM] * 3,
        scratch_shapes=[pltpu.VMEM((n * rows, width), BF16)],
        compiler_params=pltpu.CompilerParams(vmem_limit_bytes=size + (8 << 20)),
        cost_estimate=pl.CostEstimate(
            flops=2 * vals.size * width, bytes_accessed=size, transcendentals=0
        ),
        name="apply_blocks",
    )(where, rep, vals, *pieces)


def reduce_rep(parts):
    send, keep_far, keep_near = parts
    got = lax.ppermute(send, "rep", [(i, i ^ 1) for i in range(4)])
    crossing = (keep_far + got[: keep_far.shape[0]].astype(F32)).astype(BF16)
    return keep_near, got, lax.ppermute(crossing, "rep", [(i, i ^ 2) for i in range(4)]), crossing


def joined(refs):
    halves = []
    for h in range(len(refs) // 3):
        near, got, cross = refs[3 * h : 3 * h + 3]
        rows = near.shape[0]
        halves.append(near[...] + got[rows:, :].astype(F32) + cross[...].astype(F32))
    return jnp.concatenate(halves, axis=1)


def middle_kernel(rep_ref, weight_ref, grad_ref, *refs):
    sums, (act_ref, high_ref, low_ref, *masked_refs, grad, sem) = refs[:6], refs[6:]
    rows = act_ref.shape[0]
    start = pl.multiple_of(rep_ref[0] * rows, rows)
    copy = pltpu.make_async_copy(grad_ref.at[pl.ds(start, rows), :], grad, sem)
    copy.start()
    held = joined(sums)
    high = held.astype(BF16)
    low = (held - high.astype(F32)).astype(BF16)
    high_ref[...] = high
    low_ref[...] = low
    weight = weight_ref[...]
    summed = jnp.dot(high, weight, preferred_element_type=F32)
    summed = (summed + jnp.dot(low, weight, preferred_element_type=F32)) * (1.0 / SCALE)
    gate = jax.nn.sigmoid(summed)
    act_ref[...] = (summed * gate).astype(BF16)
    slope = gate * (1.0 + summed * (1.0 - gate))
    copy.wait()
    masked = (grad[...].astype(F32) * slope).astype(BF16)
    for h, ref in enumerate(masked_refs):
        ref[...] = masked[:, h * HALF : (h + 1) * HALF]


def middle(rep, weight, grad, sums):
    rows, width = sums[0].shape[0], grad.shape[1]
    shapes = [jax.ShapeDtypeStruct((rows, width), BF16)] * 3
    shapes += [jax.ShapeDtypeStruct((rows, HALF), BF16)] * (width // HALF)
    return pl.pallas_call(
        middle_kernel,
        out_shape=shapes,
        in_specs=[SMEM, VMEM, pl.BlockSpec(memory_space=pl.ANY)] + [VMEM] * 6,
        out_specs=[VMEM] * len(shapes),
        scratch_shapes=[pltpu.VMEM((rows, width), BF16), pltpu.SemaphoreType.DMA],
        compiler_params=pltpu.CompilerParams(vmem_limit_bytes=16 << 20),
        cost_estimate=pl.CostEstimate(
            flops=4 * rows * width * width, bytes_accessed=rows * width * 18, transcendentals=rows * width
        ),
        name="middle",
    )(rep, weight, grad, *sums)


def last_kernel(weight_ref, *refs):
    back = joined(refs[:6])
    refs[6][...] = split_dot(back, weight_ref[...], ((1,), (1,))).astype(BF16)


def last(weight, sums):
    rows, width = sums[0].shape[0], weight.shape[0]
    return pl.pallas_call(
        last_kernel,
        out_shape=jax.ShapeDtypeStruct((rows, width), BF16),
        in_specs=[VMEM] * 7,
        out_specs=VMEM,
        compiler_params=pltpu.CompilerParams(vmem_limit_bytes=24 << 20),
        cost_estimate=pl.CostEstimate(
            flops=4 * rows * width * width, bytes_accessed=rows * width * 14, transcendentals=0
        ),
        name="last",
    )(weight, *sums)


def local_kernel(rep_ref, high_ref, low_ref, *refs):
    masked, outs = refs[:2], refs[2:6]
    total = refs[6]
    for h, ref in enumerate(masked):
        part = None
        for held in (high_ref, low_ref):
            term = lax.dot_general(held[...], ref[...], (((0,), (0,)), ((), ())), preferred_element_type=F32)
            part = term if part is None else part + term
        total[:, h * HALF : (h + 1) * HALF] = part
    rows = outs[0].shape[0]
    for mask, out in enumerate(outs):
        start = pl.multiple_of(lax.bitwise_xor(rep_ref[0], mask) * rows, rows)
        out[...] = total[pl.ds(start, rows), :]


def local_grad(rep, high, low, masked):
    rows, width = high.shape
    return pl.pallas_call(
        local_kernel,
        out_shape=[jax.ShapeDtypeStruct((width // 4, width), F32)] * 4,
        in_specs=[SMEM] + [VMEM] * 4,
        out_specs=[VMEM] * 4,
        scratch_shapes=[pltpu.VMEM((width, width), F32)],
        compiler_params=pltpu.CompilerParams(vmem_limit_bytes=16 << 20),
        cost_estimate=pl.CostEstimate(
            flops=4 * rows * width * width, bytes_accessed=rows * width * 6, transcendentals=0
        ),
        name="local_grad",
    )(rep, high, low, *masked)


def whole_kernel(scale, rep_ref, *refs):
    rows = refs[0].shape[0]
    for mask in range(4):
        start = pl.multiple_of(lax.bitwise_xor(rep_ref[0], mask) * rows, rows)
        refs[4][pl.ds(start, rows), :] = refs[mask][...] * scale


def whole_grad(rep, quarters, scale):
    rows, width = quarters[0].shape
    return pl.pallas_call(
        functools.partial(whole_kernel, scale),
        out_shape=jax.ShapeDtypeStruct((4 * rows, width), F32),
        in_specs=[SMEM] + [VMEM] * 4,
        out_specs=VMEM,
        compiler_params=pltpu.CompilerParams(vmem_limit_bytes=4 << 20),
        name="whole_grad",
    )(rep, *quarters)


class GradientSum:
    def __init__(self, rep, high, low, masked, n, scale):
        self.rep, self.local, self.n, self.scale = rep, (high, low, masked), n, scale
        self.pairs = [[(i, i ^ mask) for i in range(4)] for mask in range(4)]

    def start(self, after):
        high, low, masked = tie(self.local, after)
        self.quarters = local_grad(self.rep, high, low, masked)
        return self.quarters

    def over_rep(self, after):
        value = self.quarters[0]
        for mask in (1, 2, 3):
            value = value + lax.ppermute(self.quarters[mask], "rep", self.pairs[mask])
        self.value = value
        return value

    def over_rows(self, strides):
        value = self.value
        pairs = [[(i, i ^ step) for i in range(self.n)] for step in range(self.n)]
        if len(strides) == 2:
            low, high = strides
            near = value + lax.ppermute(value, "rows", pairs[low])
            far = [lax.ppermute(value, "rows", pairs[step]) for step in (high, high + low)]
            self.value = near + (far[0] + far[1])
        else:
            for step in strides:
                value = value + lax.ppermute(value, "rows", pairs[step])
            self.value = value
        return self.value

    def finish(self, after):
        self.value = tie(self.value, after)
        others = [lax.ppermute(self.value, "rep", self.pairs[mask]) for mask in (1, 2, 3)]
        return whole_grad(self.rep, [self.value, *others], self.scale)


def on_device(n, features, weight, block_cols, block_vals, out_grad):
    own_rows, width = features.shape
    block = block_vals.shape[-1]
    own_blocks = own_rows // block
    me, layer = lax.axis_index("rows"), lax.axis_index("rep")
    vals = block_vals.reshape(-1, block, block)
    chunks = [features[:, h * HALF : (h + 1) * HALF] for h in range(width // HALF)]
    ready = {}

    def prepared(after):
        my, rep, cols = tie((me.astype(jnp.int32), layer.astype(jnp.int32).reshape(1), block_cols), after)
        cols = cols.reshape(-1)
        back_steps = (ring_place(my, n) - ring_place(cols // own_blocks, n) + n) % n
        ready["rep"], ready["where"] = rep, back_steps * own_blocks + cols % own_blocks
        return ready["rep"], ready["where"]

    sums = []
    for pieces in gather_ring(chunks, n, {(2, 1): prepared}):
        parts = apply_blocks(ready["where"], ready["rep"], vals, pieces, own_blocks, SCALE)
        sums += reduce_rep(parts)[:3]
    rep = ready["rep"]
    activated, high, low, *masked = middle(rep, weight, out_grad, sums)

    node_total = own_rows * n * 4
    grad = GradientSum(rep, high, low, masked, n, 1.0 / (SCALE * math.sqrt(node_total)))
    beside = {(2, 0): grad.start, (3, 0): grad.over_rep, (4, 0): lambda _: grad.over_rows([1])}
    gathered = gather_ring(masked, n, beside)
    gathered[1] = tie(gathered[1], grad.over_rows([1 << i for i in range(1, n.bit_length() - 1)]))
    sums = []
    for pieces in gathered:
        parts = apply_blocks(ready["where"], rep, vals, pieces, own_blocks, None)
        *parts, crossing = reduce_rep(parts)
        sums += parts
    weight_grad = grad.finish(crossing)
    input_grad = last(weight, sums)
    return activated, input_grad, weight_grad


def solution(mesh):
    placed = (
        P(("rows", "rep"), None),
        P(),
        P("rows", "rep", None),
        P("rows", "rep", None, None, None),
        P("rows", None),
    )
    return jax.shard_map(
        functools.partial(on_device, mesh.shape["rows"]),
        mesh=mesh,
        in_specs=placed,
        out_specs=(P(("rows", "rep"), None), P(("rows", "rep"), None), P()),
        check_vma=False,
    )
```

time: 165 us -> 135 us (0.82)
  local copies, waits for them, and re-layouts: 21.6 us -> 3.54 us
  other arithmetic: 10.9 us -> 0.33 us
  starting transfers between devices: 44 us -> 53 us
  Pallas kernels: 14.1 us -> 10.6 us
  matrix products: 3.07 us -> 0 us
  waiting for transfers between devices: 69.1 us -> 66.3 us
    unnamed x64 -> x8, local copies, waits for them, and re-layouts: 20.7 us -> 1.61 us
    ppermute x14, starting transfers between devices: 13.8 us -> 23.4 us  [gather_ring(): right[k] = lax.ppermute(right[k], 'rows', ahead)]
    convert_element_type x4, other arithmetic: 4.96 us -> 0.25 us  [reduce_rep(): crossing = (keep_far + got[:keep_far.shape[0]].astype(F32)).astype(BF16)]
    add x6 -> x4, other arithmetic: 3.31 us -> 0.08 us  [the longest x1 0.03 us: prepared(): back_steps * own_blocks + cols % own_blocks]
    dot_general x4 -> x0, matrix products: 3.07 us -> none  [the longest x2 1.56 us: split_dot(): lax.dot_general(low, right, (dims, ((), ())), preferred_element_type=F32)]
    pallas_call x5 -> x7, Pallas kernels: 11.8 us -> 9.31 us  [the longest x4 6.23 us: apply_blocks(): pl.pallas_call(functools.partial(blocks_kernel, n, own_blocks, block, sca...]
    mul x2 -> x0, other arithmetic: 2.37 us -> none  [the longest x1 1.25 us: on_device(): scaled = features * jnp.asarray(SCALE, BF16)]
    ppermute x14, waiting for transfers between devices: 19 us -> 16.7 us  [gather_ring(): right[k] = lax.ppermute(right[k], 'rows', ahead)]
  transfers between devices with their start and end apart: 47 -> 46, of which waited for: 23 -> 24; matrix products, arithmetic and copies ran while one was open for 9% -> 1% of each run, Pallas kernels for 6% -> 6%
where the time goes in v2:
time: 135 us
  waiting for transfers between devices  66.3 us (49%)
  starting transfers between devices  53 us (39%)
  Pallas kernels  10.6 us (8%)
  local copies, waits for them, and re-layouts  3.54 us (3%)
    ppermute x14, starting transfers between devices, gather_ring(): right[k] = lax.ppermute(right[k], 'rows', ahead)  23.4 us
    ppermute x14, waiting for transfers between devices, gather_ring(): left[k] = lax.ppermute(left[k], 'rows', behind)  22.3 us
    ppermute x14, waiting for transfers between devices, gather_ring(): right[k] = lax.ppermute(right[k], 'rows', ahead)  16.7 us
    ppermute x14, starting transfers between devices, gather_ring(): left[k] = lax.ppermute(left[k], 'rows', behind)  15.2 us
    ppermute x3, waiting for transfers between devices, finish(): lax.ppermute(self.value, 'rep', self.pairs[mask])  11.7 us
    ppermute x4, waiting for transfers between devices, reduce_rep(): lax.ppermute(crossing, 'rep', [(i, i ^ 2) for i in range(4)])  10.8 us
    pallas_call x4, Pallas kernels, apply_blocks(): pl.pallas_call(functools.partial(blocks_kernel, n, own_blocks, block, sca...  6.23 us
    ppermute x4, starting transfers between devices, reduce_rep(): lax.ppermute(crossing, 'rep', [(i, i ^ 2) for i in range(4)])  6.21 us
  transfers between devices with their start and end apart: 46, of which 24 were waited for; matrix products, arithmetic and copies ran while one was open for 1% of the time, Pallas kernels for 6%

profile of v2, /device:TPU:0, one launch (start us, length us, event | category | flops | bytes accessed | tf_op | source)
XLA Modules:
  0.0 134.6 jit_solution(401460153698242558)
XLA Ops:
  1.7 3.1 %collective-permute-start = (bf16[1024,128]{1,0:T(8,128)(2,1)S(1)}, bf16[1024,128]{1,0:T(8,128)(2,1)S(1)}, u32[]{:S(2)}, u32[]{:S(2)}) collective-permute-start(bf16[1024,128]{1,0:T(8,128)(2,1)S(1)} %get-tuple-element.92.refs_0_), channel_id=1, source_target_pairs={{0,8},{8,16},{16,24},{24,28},{28,20},{20,12},{12,4},{4,0},{1,9},{9... | collective-permute-start | bytes 786440 | tf_op jit(solution)/shard_map/ppermute | solution.py:51
  6.8 5.0 %collective-permute-done.refs_1_ = bf16[1024,128]{1,0:T(8,128)(2,1)S(1)} collective-permute-done((bf16[1024,128]{1,0:T(8,128)(2,1)S(1)}, bf16[1024,128]{1,0:T(8,128)(2,1)S(1)}, u32[]{:S(2)}, u32[]{:S(2)}) %collective-permute-start) | collective-permute-done | bytes 262176 | tf_op jit(solution)/shard_map/ppermute | solution.py:51
  11.9 2.1 %collective-permute-start.1 = (bf16[1024,128]{1,0:T(8,128)(2,1)S(1)}, bf16[1024,128]{1,0:T(8,128)(2,1)S(1)}, u32[]{:S(2)}, u32[]{:S(2)}) collective-permute-start(bf16[1024,128]{1,0:T(8,128)(2,1)S(1)} %collective-permute-done.refs_1_), channel_id=1, source_target_pairs={{0,8},{8,16},{16,24},{24,28},{28,20},{20,12},{12,4},{4,0},{1,9},{9... | collective-permute-start | bytes 786440 | tf_op jit(solution)/shard_map/ppermute | solution.py:51
  14.9 2.6 %collective-permute-done.9.refs_1_ = bf16[1024,128]{1,0:T(8,128)(2,1)S(1)} collective-permute-done((bf16[1024,128]{1,0:T(8,128)(2,1)S(1)}, bf16[1024,128]{1,0:T(8,128)(2,1)S(1)}, u32[]{:S(2)}, u32[]{:S(2)}) %collective-permute-start.9) | collective-permute-done | bytes 262176 | tf_op jit(solution)/shard_map/ppermute | solution.py:51
  17.5 2.1 %collective-permute-start.13 = (bf16[1024,128]{1,0:T(8,128)(2,1)S(1)}, bf16[1024,128]{1,0:T(8,128)(2,1)S(1)}, u32[]{:S(2)}, u32[]{:S(2)}) collective-permute-start(bf16[1024,128]{1,0:T(8,128)(2,1)S(1)} %collective-permute-done.10.refs_7_), channel_id=1, source_target_pairs={{8,0},{16,8},{24,16},{28,24},{20,28},{12,20},{4,12},{0,4},{9,1},{1... | collective-permute-start | bytes 786440 | tf_op jit(solution)/shard_map/ppermute | solution.py:54
  22.3 1.8 %collective-permute-start.2 = (bf16[1024,128]{1,0:T(8,128)(2,1)S(1)}, bf16[1024,128]{1,0:T(8,128)(2,1)S(1)}, u32[]{:S(2)}, u32[]{:S(2)}) collective-permute-start(bf16[1024,128]{1,0:T(8,128)(2,1)S(1)} %collective-permute-done.1.refs_2_), channel_id=1, source_target_pairs={{0,8},{8,16},{16,24},{24,28},{28,20},{20,12},{12,4},{4,0},{1,9},{9... | collective-permute-start | bytes 786440 | tf_op jit(solution)/shard_map/ppermute | solution.py:51
  26.8 2.0 %collective-permute-start.14 = (bf16[1024,128]{1,0:T(8,128)(2,1)S(1)}, bf16[1024,128]{1,0:T(8,128)(2,1)S(1)}, u32[]{:S(2)}, u32[]{:S(2)}) collective-permute-start(bf16[1024,128]{1,0:T(8,128)(2,1)S(1)} %collective-permute-done.13.refs_6_), channel_id=1, source_target_pairs={{8,0},{16,8},{24,16},{28,24},{20,28},{12,20},{4,12},{0,4},{9,1},{1... | collective-permute-start | bytes 786440 | tf_op jit(solution)/shard_map/ppermute | solution.py:54
  28.8 3.7 %collective-permute-done.5.refs_6_ = bf16[1024,128]{1,0:T(8,128)(2,1)S(1)} collective-permute-done((bf16[1024,128]{1,0:T(8,128)(2,1)S(1)}, bf16[1024,128]{1,0:T(8,128)(2,1)S(1)}, u32[]{:S(2)}, u32[]{:S(2)}) %collective-permute-start.5) | collective-permute-done | bytes 262176 | tf_op jit(solution)/shard_map/ppermute | solution.py:54
  32.4 2.0 %collective-permute-start.6 = (bf16[1024,128]{1,0:T(8,128)(2,1)S(1)}, bf16[1024,128]{1,0:T(8,128)(2,1)S(1)}, u32[]{:S(2)}, u32[]{:S(2)}) collective-permute-start(bf16[1024,128]{1,0:T(8,128)(2,1)S(1)} %collective-permute-done.5.refs_6_), channel_id=1, source_target_pairs={{8,0},{16,8},{24,16},{28,24},{20,28},{12,20},{4,12},{0,4},{9,1},{1... | collective-permute-start | bytes 786440 | tf_op jit(solution)/shard_map/ppermute | solution.py:54
  34.5 2.7 %collective-permute-done.11.refs_2_ = bf16[1024,128]{1,0:T(8,128)(2,1)S(1)} collective-permute-done((bf16[1024,128]{1,0:T(8,128)(2,1)S(1)}, bf16[1024,128]{1,0:T(8,128)(2,1)S(1)}, u32[]{:S(2)}, u32[]{:S(2)}) %collective-permute-start.11) | collective-permute-done | bytes 262176 | tf_op jit(solution)/shard_map/ppermute | solution.py:51
  37.1 1.8 %collective-permute-start.12 = (bf16[1024,128]{1,0:T(8,128)(2,1)S(1)}, bf16[1024,128]{1,0:T(8,128)(2,1)S(1)}, u32[]{:S(2)}, u32[]{:S(2)}) collective-permute-start(bf16[1024,128]{1,0:T(8,128)(2,1)S(1)} %collective-permute-done.11.refs_2_), channel_id=1, source_target_pairs={{0,8},{8,16},{16,24},{24,28},{28,20},{20,12},{12,4},{4,0},{1,9},{9... | collective-permute-start | bytes 786440 | tf_op jit(solution)/shard_map/ppermute | solution.py:51
  40.0 3.7 %collective-permute-done.6.refs_5_ = bf16[1024,128]{1,0:T(8,128)(2,1)S(1)} collective-permute-done((bf16[1024,128]{1,0:T(8,128)(2,1)S(1)}, bf16[1024,128]{1,0:T(8,128)(2,1)S(1)}, u32[]{:S(2)}, u32[]{:S(2)}) %collective-permute-start.6) | collective-permute-done | bytes 262176 | tf_op jit(solution)/shard_map/ppermute | solution.py:54
  49.4 2.0 %collective-permute-start.8 = (bf16[1024,128]{1,0:T(8,128)(2,1)S(1)}, bf16[1024,128]{1,0:T(8,128)(2,1)S(1)}, u32[]{:S(2)}, u32[]{:S(2)}) collective-permute-start(bf16[1024,128]{1,0:T(8,128)(2,1)S(1)} %add_convert_fusion.3), channel_id=1, source_target_pairs={{0,2},{1,3},{2,0},{3,1},{4,6},{5,7},{6,4},{7,5},{8,10},{9,11},{10,... | collective-permute-start | bytes 786440 | tf_op jit(solution)/shard_map/ppermute | solution.py:102
  53.0 5.6 %collective-permute-done.8.refs_2_ = bf16[1024,128]{1,0:T(8,128)(2,1)S(1)} collective-permute-done((bf16[1024,128]{1,0:T(8,128)(2,1)S(1)}, bf16[1024,128]{1,0:T(8,128)(2,1)S(1)}, u32[]{:S(2)}, u32[]{:S(2)}) %collective-permute-start.8) | collective-permute-done | bytes 262176 | tf_op jit(solution)/shard_map/ppermute | solution.py:102
  58.6 5.2 %collective-permute-done.17.refs_5_ = bf16[1024,128]{1,0:T(8,128)(2,1)S(1)} collective-permute-done((bf16[1024,128]{1,0:T(8,128)(2,1)S(1)}, bf16[1024,128]{1,0:T(8,128)(2,1)S(1)}, u32[]{:S(2)}, u32[]{:S(2)}) %collective-permute-start.17) | collective-permute-done | bytes 262176 | tf_op jit(solution)/shard_map/ppermute | solution.py:102
  70.2 3.2 %collective-permute-done.18.refs_1_ = bf16[1024,128]{1,0:T(8,128)(2,1)S(1)} collective-permute-done((bf16[1024,128]{1,0:T(8,128)(2,1)S(1)}, bf16[1024,128]{1,0:T(8,128)(2,1)S(1)}, u32[]{:S(2)}, u32[]{:S(2)}) %collective-permute-start.18) | collective-permute-done | bytes 262176 | tf_op jit(solution)/shard_map/ppermute | solution.py:51
  74.2 1.9 %collective-permute-start.20 = (bf16[1024,128]{1,0:T(8,128)(2,1)S(1)}, bf16[1024,128]{1,0:T(8,128)(2,1)S(1)}, u32[]{:S(2)}, u32[]{:S(2)}) collective-permute-start(bf16[1024,128]{1,0:T(8,128)(2,1)S(1)} %collective-permute-done.18.refs_1_), channel_id=1, source_target_pairs={{0,8},{8,16},{16,24},{24,28},{28,20},{20,12},{12,4},{4,0},{1,9},{9... | collective-permute-start | bytes 786440 | tf_op jit(solution)/shard_map/ppermute | solution.py:51
  76.2 1.9 %collective-permute-start.31 = (bf16[1024,128]{1,0:T(8,128)(2,1)S(1)}, bf16[1024,128]{1,0:T(8,128)(2,1)S(1)}, u32[]{:S(2)}, u32[]{:S(2)}) collective-permute-start(bf16[1024,128]{1,0:T(8,128)(2,1)S(1)} %get-tuple-element.79.refs_1_.refs_0_), channel_id=1, source_target_pairs={{0,8},{8,16},{16,24},{24,28},{28,20},{20,12},{12,4},{4,0},{1,9},{9... | collective-permute-start | bytes 786440 | tf_op jit(solution)/shard_map/ppermute | solution.py:51
  78.1 4.5 %collective-permute-done.34.refs_7_ = bf16[1024,128]{1,0:T(8,128)(2,1)S(1)} collective-permute-done((bf16[1024,128]{1,0:T(8,128)(2,1)S(1)}, bf16[1024,128]{1,0:T(8,128)(2,1)S(1)}, u32[]{:S(2)}, u32[]{:S(2)}) %collective-permute-start.34) | collective-permute-done | bytes 262176 | tf_op jit(solution)/shard_map/ppermute | solution.py:54
  83.2 5.0 %collective-permute-done.21.refs_6_ = bf16[1024,128]{1,0:T(8,128)(2,1)S(1)} collective-permute-done((bf16[1024,128]{1,0:T(8,128)(2,1)S(1)}, bf16[1024,128]{1,0:T(8,128)(2,1)S(1)}, u32[]{:S(2)}, u32[]{:S(2)}) %collective-permute-start.21) | collective-permute-done | bytes 262176 | tf_op jit(solution)/shard_map/ppermute | solution.py:54
  92.4 4.1 %collective-permute-done.27 = f32[64,256]{1,0:T(8,128)S(1)} collective-permute-done((f32[64,256]{1,0:T(8,128)S(1)}, f32[64,256]{1,0:T(8,128)S(1)}, u32[]{:S(2)}, u32[]{:S(2)}) %collective-permute-start.27) | collective-permute-done | bytes 65568 | tf_op jit(solution)/shard_map/ppermute | solution.py:252
  96.5 2.5 %collective-permute-start.36 = (bf16[1024,128]{1,0:T(8,128)(2,1)S(1)}, bf16[1024,128]{1,0:T(8,128)(2,1)S(1)}, u32[]{:S(2)}, u32[]{:S(2)}) collective-permute-start(bf16[1024,128]{1,0:T(8,128)(2,1)S(1)} %collective-permute-done.35.refs_6_), channel_id=1, source_target_pairs={{8,0},{16,8},{24,16},{28,24},{20,28},{12,20},{4,12},{0,4},{9,1},{1... | collective-permute-start | bytes 786440 | tf_op jit(solution)/shard_map/ppermute | solution.py:54
  105.1 2.0 %collective-permute-start.33 = (bf16[1024,128]{1,0:T(8,128)(2,1)S(1)}, bf16[1024,128]{1,0:T(8,128)(2,1)S(1)}, u32[]{:S(2)}, u32[]{:S(2)}) collective-permute-start(bf16[1024,128]{1,0:T(8,128)(2,1)S(1)} %collective-permute-done.32.refs_2_), channel_id=1, source_target_pairs={{0,8},{8,16},{16,24},{24,28},{28,20},{20,12},{12,4},{4,0},{1,9},{9... | collective-permute-start | bytes 786440 | tf_op jit(solution)/shard_map/ppermute | solution.py:51
  121.0 11.1 %collective-permute-done.44.refs_2_ = f32[64,256]{1,0:T(8,128)S(1)} collective-permute-done((f32[64,256]{1,0:T(8,128)S(1)}, f32[64,256]{1,0:T(8,128)S(1)}, u32[]{:S(2)}, u32[]{:S(2)}) %collective-permute-start.44) | collective-permute-done | bytes 65568 | tf_op jit(solution)/shard_map/ppermute | solution.py:258
  (95 shorter events, 52.6 us)
Async XLA Ops:
  1.7 10.2 %collective-permute-start = (bf16[1024,128]{1,0:T(8,128)(2,1)S(1)}, bf16[1024,128]{1,0:T(8,128)(2,1)S(1)}, u32[]{:S(2)}, u32[]{:S(2)}) collective-permute-start(bf16[1024,128]{1,0:T(8,128)(2,1)S(1)} %get-tuple-element.92.refs_0_), channel_id=1, source_target_pairs={{0,8},{8,16},{16,24},{24,28},{28,20},{20,12},{12,4},{4,0},{1,9},{9... | collective-permute-start | bytes 786440 | tf_op jit(solution)/shard_map/ppermute | solution.py:51
  4.8 12.7 %collective-permute-start.9 = (bf16[1024,128]{1,0:T(8,128)(2,1)S(1)}, bf16[1024,128]{1,0:T(8,128)(2,1)S(1)}, u32[]{:S(2)}, u32[]{:S(2)}) collective-permute-start(bf16[1024,128]{1,0:T(8,128)(2,1)S(1)} %get-tuple-element.91.refs_0_), channel_id=1, source_target_pairs={{0,8},{8,16},{16,24},{24,28},{28,20},{20,12},{12,4},{4,0},{1,9},{9... | collective-permute-start | bytes 786440 | tf_op jit(solution)/shard_map/ppermute | solution.py:51
  6.4 11.1 %collective-permute-start.10 = (bf16[1024,128]{1,0:T(8,128)(2,1)S(1)}, bf16[1024,128]{1,0:T(8,128)(2,1)S(1)}, u32[]{:S(2)}, u32[]{:S(2)}) collective-permute-start(bf16[1024,128]{1,0:T(8,128)(2,1)S(1)} %get-tuple-element.91.refs_0_), channel_id=1, source_target_pairs={{8,0},{16,8},{24,16},{28,24},{20,28},{12,20},{4,12},{0,4},{9,1},{1... | collective-permute-start | bytes 786440 | tf_op jit(solution)/shard_map/ppermute | solution.py:54
  6.8 13.5 %collective-permute-start.4 = (bf16[1024,128]{1,0:T(8,128)(2,1)S(1)}, bf16[1024,128]{1,0:T(8,128)(2,1)S(1)}, u32[]{:S(2)}, u32[]{:S(2)}) collective-permute-start(bf16[1024,128]{1,0:T(8,128)(2,1)S(1)} %get-tuple-element.92.refs_0_), channel_id=1, source_target_pairs={{8,0},{16,8},{24,16},{28,24},{20,28},{12,20},{4,12},{0,4},{9,1},{1... | collective-permute-start | bytes 786440 | tf_op jit(solution)/shard_map/ppermute | solution.py:54
  11.9 10.4 %collective-permute-start.1 = (bf16[1024,128]{1,0:T(8,128)(2,1)S(1)}, bf16[1024,128]{1,0:T(8,128)(2,1)S(1)}, u32[]{:S(2)}, u32[]{:S(2)}) collective-permute-start(bf16[1024,128]{1,0:T(8,128)(2,1)S(1)} %collective-permute-done.refs_1_), channel_id=1, source_target_pairs={{0,8},{8,16},{16,24},{24,28},{28,20},{20,12},{12,4},{4,0},{1,9},{9... | collective-permute-start | bytes 786440 | tf_op jit(solution)/shard_map/ppermute | solution.py:51
  20.3 12.1 %collective-permute-start.5 = (bf16[1024,128]{1,0:T(8,128)(2,1)S(1)}, bf16[1024,128]{1,0:T(8,128)(2,1)S(1)}, u32[]{:S(2)}, u32[]{:S(2)}) collective-permute-start(bf16[1024,128]{1,0:T(8,128)(2,1)S(1)} %collective-permute-done.4.refs_7_), channel_id=1, source_target_pairs={{8,0},{16,8},{24,16},{28,24},{20,28},{12,20},{4,12},{0,4},{9,1},{1... | collective-permute-start | bytes 786440 | tf_op jit(solution)/shard_map/ppermute | solution.py:54
  22.3 12.1 %collective-permute-start.2 = (bf16[1024,128]{1,0:T(8,128)(2,1)S(1)}, bf16[1024,128]{1,0:T(8,128)(2,1)S(1)}, u32[]{:S(2)}, u32[]{:S(2)}) collective-permute-start(bf16[1024,128]{1,0:T(8,128)(2,1)S(1)} %collective-permute-done.1.refs_2_), channel_id=1, source_target_pairs={{0,8},{8,16},{16,24},{24,28},{28,20},{20,12},{12,4},{4,0},{1,9},{9... | collective-permute-start | bytes 786440 | tf_op jit(solution)/shard_map/ppermute | solution.py:51
  24.1 13.1 %collective-permute-start.11 = (bf16[1024,128]{1,0:T(8,128)(2,1)S(1)}, bf16[1024,128]{1,0:T(8,128)(2,1)S(1)}, u32[]{:S(2)}, u32[]{:S(2)}) collective-permute-start(bf16[1024,128]{1,0:T(8,128)(2,1)S(1)} %collective-permute-done.9.refs_1_), channel_id=1, source_target_pairs={{0,8},{8,16},{16,24},{24,28},{28,20},{20,12},{12,4},{4,0},{1,9},{9... | collective-permute-start | bytes 786440 | tf_op jit(solution)/shard_map/ppermute | solution.py:51
  26.8 12.1 %collective-permute-start.14 = (bf16[1024,128]{1,0:T(8,128)(2,1)S(1)}, bf16[1024,128]{1,0:T(8,128)(2,1)S(1)}, u32[]{:S(2)}, u32[]{:S(2)}) collective-permute-start(bf16[1024,128]{1,0:T(8,128)(2,1)S(1)} %collective-permute-done.13.refs_6_), channel_id=1, source_target_pairs={{8,0},{16,8},{24,16},{28,24},{20,28},{12,20},{4,12},{0,4},{9,1},{1... | collective-permute-start | bytes 786440 | tf_op jit(solution)/shard_map/ppermute | solution.py:54
  32.4 11.2 %collective-permute-start.6 = (bf16[1024,128]{1,0:T(8,128)(2,1)S(1)}, bf16[1024,128]{1,0:T(8,128)(2,1)S(1)}, u32[]{:S(2)}, u32[]{:S(2)}) collective-permute-start(bf16[1024,128]{1,0:T(8,128)(2,1)S(1)} %collective-permute-done.5.refs_6_), channel_id=1, source_target_pairs={{8,0},{16,8},{24,16},{28,24},{20,28},{12,20},{4,12},{0,4},{9,1},{1... | collective-permute-start | bytes 786440 | tf_op jit(solution)/shard_map/ppermute | solution.py:54
  37.1 9.9 %collective-permute-start.12 = (bf16[1024,128]{1,0:T(8,128)(2,1)S(1)}, bf16[1024,128]{1,0:T(8,128)(2,1)S(1)}, u32[]{:S(2)}, u32[]{:S(2)}) collective-permute-start(bf16[1024,128]{1,0:T(8,128)(2,1)S(1)} %collective-permute-done.11.refs_2_), channel_id=1, source_target_pairs={{0,8},{8,16},{16,24},{24,28},{28,20},{20,12},{12,4},{4,0},{1,9},{9... | collective-permute-start | bytes 786440 | tf_op jit(solution)/shard_map/ppermute | solution.py:51
  51.5 12.3 %collective-permute-start.17 = (bf16[1024,128]{1,0:T(8,128)(2,1)S(1)}, bf16[1024,128]{1,0:T(8,128)(2,1)S(1)}, u32[]{:S(2)}, u32[]{:S(2)}) collective-permute-start(bf16[1024,128]{1,0:T(8,128)(2,1)S(1)} %add_convert_fusion.2), channel_id=1, source_target_pairs={{0,2},{1,3},{2,0},{3,1},{4,6},{5,7},{6,4},{7,5},{8,10},{9,11},{10,... | collective-permute-start | bytes 786440 | tf_op jit(solution)/shard_map/ppermute | solution.py:102
  76.0 12.2 %collective-permute-start.21 = (bf16[1024,128]{1,0:T(8,128)(2,1)S(1)}, bf16[1024,128]{1,0:T(8,128)(2,1)S(1)}, u32[]{:S(2)}, u32[]{:S(2)}) collective-permute-start(bf16[1024,128]{1,0:T(8,128)(2,1)S(1)} %collective-permute-done.19.refs_7_), channel_id=1, source_target_pairs={{8,0},{16,8},{24,16},{28,24},{20,28},{12,20},{4,12},{0,4},{9,1},{1... | collective-permute-start | bytes 786440 | tf_op jit(solution)/shard_map/ppermute | solution.py:54
  76.2 14.6 %collective-permute-start.31 = (bf16[1024,128]{1,0:T(8,128)(2,1)S(1)}, bf16[1024,128]{1,0:T(8,128)(2,1)S(1)}, u32[]{:S(2)}, u32[]{:S(2)}) collective-permute-start(bf16[1024,128]{1,0:T(8,128)(2,1)S(1)} %get-tuple-element.79.refs_1_.refs_0_), channel_id=1, source_target_pairs={{0,8},{8,16},{16,24},{24,28},{28,20},{20,12},{12,4},{4,0},{1,9},{9... | collective-permute-start | bytes 786440 | tf_op jit(solution)/shard_map/ppermute | solution.py:51
  82.6 13.9 %collective-permute-start.35 = (bf16[1024,128]{1,0:T(8,128)(2,1)S(1)}, bf16[1024,128]{1,0:T(8,128)(2,1)S(1)}, u32[]{:S(2)}, u32[]{:S(2)}) collective-permute-start(bf16[1024,128]{1,0:T(8,128)(2,1)S(1)} %collective-permute-done.34.refs_7_), channel_id=1, source_target_pairs={{8,0},{16,8},{24,16},{28,24},{20,28},{12,20},{4,12},{0,4},{9,1},{1... | collective-permute-start | bytes 786440 | tf_op jit(solution)/shard_map/ppermute | solution.py:54
  88.2 10.8 %collective-permute-start.25 = (bf16[1024,128]{1,0:T(8,128)(2,1)S(1)}, bf16[1024,128]{1,0:T(8,128)(2,1)S(1)}, u32[]{:S(2)}, u32[]{:S(2)}) collective-permute-start(bf16[1024,128]{1,0:T(8,128)(2,1)S(1)} %collective-permute-done.20.refs_2_), channel_id=1, source_target_pairs={{0,8},{8,16},{16,24},{24,28},{28,20},{20,12},{12,4},{4,0},{1,9},{9... | collective-permute-start | bytes 786440 | tf_op jit(solution)/shard_map/ppermute | solution.py:51
  89.3 9.7 %collective-permute-start.26 = (bf16[1024,128]{1,0:T(8,128)(2,1)S(1)}, bf16[1024,128]{1,0:T(8,128)(2,1)S(1)}, u32[]{:S(2)}, u32[]{:S(2)}) collective-permute-start(bf16[1024,128]{1,0:T(8,128)(2,1)S(1)} %collective-permute-done.21.refs_6_), channel_id=1, source_target_pairs={{8,0},{16,8},{24,16},{28,24},{20,28},{12,20},{4,12},{0,4},{9,1},{1... | collective-permute-start | bytes 786440 | tf_op jit(solution)/shard_map/ppermute | solution.py:54
  90.8 12.4 %collective-permute-start.32 = (bf16[1024,128]{1,0:T(8,128)(2,1)S(1)}, bf16[1024,128]{1,0:T(8,128)(2,1)S(1)}, u32[]{:S(2)}, u32[]{:S(2)}) collective-permute-start(bf16[1024,128]{1,0:T(8,128)(2,1)S(1)} %collective-permute-done.31.refs_1_), channel_id=1, source_target_pairs={{0,8},{8,16},{16,24},{24,28},{28,20},{20,12},{12,4},{4,0},{1,9},{9... | collective-permute-start | bytes 786440 | tf_op jit(solution)/shard_map/ppermute | solution.py:51
  100.5 10.3 %collective-permute-start.39 = (f32[64,256]{1,0:T(8,128)S(1)}, f32[64,256]{1,0:T(8,128)S(1)}, u32[]{:S(2)}, u32[]{:S(2)}) collective-permute-start(f32[64,256]{1,0:T(8,128)S(1)} %add.71), channel_id=1, source_target_pairs={{0,16},{4,20},{8,24},{12,28},{16,0},{20,4},{24,8},{28,12},{1,17},{... | collective-permute-start | bytes 196616 | tf_op jit(solution)/shard_map/ppermute | solution.py:248
  101.9 9.4 %collective-permute-start.40 = (f32[64,256]{1,0:T(8,128)S(1)}, f32[64,256]{1,0:T(8,128)S(1)}, u32[]{:S(2)}, u32[]{:S(2)}) collective-permute-start(f32[64,256]{1,0:T(8,128)S(1)} %add.71), channel_id=1, source_target_pairs={{0,24},{4,28},{8,16},{12,20},{16,8},{20,12},{24,0},{28,4},{1,25},{... | collective-permute-start | bytes 196616 | tf_op jit(solution)/shard_map/ppermute | solution.py:248
  115.8 17.5 %collective-permute-start.30 = (bf16[1024,128]{1,0:T(8,128)(2,1)S(1)}, bf16[1024,128]{1,0:T(8,128)(2,1)S(1)}, u32[]{:S(2)}, u32[]{:S(2)}) collective-permute-start(bf16[1024,128]{1,0:T(8,128)(2,1)S(1)} %add_convert_fusion.1), channel_id=1, source_target_pairs={{0,2},{1,3},{2,0},{3,1},{4,6},{5,7},{6,4},{7,5},{8,10},{9,11},{10,... | collective-permute-start | bytes 786440 | tf_op jit(solution)/shard_map/ppermute | solution.py:102
  117.7 15.6 %collective-permute-start.42 = (bf16[1024,128]{1,0:T(8,128)(2,1)S(1)}, bf16[1024,128]{1,0:T(8,128)(2,1)S(1)}, u32[]{:S(2)}, u32[]{:S(2)}) collective-permute-start(bf16[1024,128]{1,0:T(8,128)(2,1)S(1)} %add_convert_fusion), channel_id=1, source_target_pairs={{0,2},{1,3},{2,0},{3,1},{4,6},{5,7},{6,4},{7,5},{8,10},{9,11},{10,... | collective-permute-start | bytes 786440 | tf_op jit(solution)/shard_map/ppermute | solution.py:102
  119.1 12.9 %collective-permute-start.44 = (f32[64,256]{1,0:T(8,128)S(1)}, f32[64,256]{1,0:T(8,128)S(1)}, u32[]{:S(2)}, u32[]{:S(2)}) collective-permute-start(f32[64,256]{1,0:T(8,128)S(1)} %add_add_fusion.refs_0_), channel_id=1, source_target_pairs={{0,2},{1,3},{2,0},{3,1},{4,6},{5,7},{6,4},{7,5},{8,10},{9,11},{10,... | collective-permute-start | bytes 196616 | tf_op jit(solution)/shard_map/ppermute | solution.py:258
  119.8 12.8 %collective-permute-start.45 = (f32[64,256]{1,0:T(8,128)S(1)}, f32[64,256]{1,0:T(8,128)S(1)}, u32[]{:S(2)}, u32[]{:S(2)}) collective-permute-start(f32[64,256]{1,0:T(8,128)S(1)} %add_add_fusion.refs_0_), channel_id=1, source_target_pairs={{0,3},{1,2},{2,1},{3,0},{4,7},{5,6},{6,5},{7,4},{8,11},{9,10},{10,... | collective-permute-start | bytes 196616 | tf_op jit(solution)/shard_map/ppermute | solution.py:258
  (26 other events, 228.7 us)

commit v3 on v2

--- a/solution.py
+++ b/solution.py
@@ -35,33 +35,20 @@
     return lax.optimization_barrier((arrays, other))[0]
 
 
-def gather_ring(chunks, n, beside=None):
+def ring_ways(n):
     order = ring_order(n)
     ahead = [(order[i], order[(i + 1) % n]) for i in range(n)]
-    behind = [(b, a) for a, b in ahead]
-    right, left = list(chunks), list(chunks)
-    pieces = [[c] + [None] * (n - 1) for c in chunks]
-    for step in range(1, n // 2 + 1):
-        for k in range(len(chunks)):
-            last = step == n // 2
-            if beside and (step, k) in beside:
-                right[k], left[k] = tie((right[k], left[k]), beside[step, k](before))
-            before = right[k]
-            if not last or k % 2 == 0:
-                right[k] = lax.ppermute(right[k], "rows", ahead)
-                pieces[k][step] = right[k]
-            if not last or k % 2 == 1:
-                left[k] = lax.ppermute(left[k], "rows", behind)
-                pieces[k][n - step] = left[k]
-    return pieces
-
-
-def blocks_kernel(n, own_blocks, block, scale, where_ref, rep_ref, vals_ref, *refs):
-    pieces, (send, keep_far, keep_near, pool) = refs[:n], refs[n:]
-    rows = own_blocks * block
-    for p in range(n):
-        piece = pieces[p][...]
-        pool[p * rows : (p + 1) * rows, :] = piece if scale is None else piece * jnp.asarray(scale, BF16)
+    return ahead, [(b, a) for a, b in ahead]
+
+
+def gather_kernel(n, own_blocks, block, scale, where_ref, rep_ref, vals_ref, *refs):
+    pieces, (send, keep_far, keep_near, pool) = refs[: n + 1], refs[n + 1 :]
+    rows, half = own_blocks * block, n // 2
+    starts = [p * rows for p in range(half + 1)] + [half * rows + rows // 2]
+    starts += [p * rows for p in range(half + 1, n)]
+    for start, ref in zip(starts, pieces):
+        piece = ref[...]
+        pool[start : start + piece.shape[0], :] = piece if scale is None else piece * jnp.asarray(scale, BF16)
     me = rep_ref[0]
     for mask, out, first in ((3, send, 0), (1, send, own_blocks), (2, keep_far, 0), (0, keep_near, 0)):
         base = lax.bitwise_xor(me, mask) * own_blocks
@@ -75,24 +62,128 @@
             out[(first + j) * block : (first + j + 1) * block, :] = total.astype(out.dtype)
 
 
-def apply_blocks(where, rep, vals, pieces, own_blocks, scale):
-    n, block = len(pieces), vals.shape[-1]
+def gather_blocks(where, rep, vals, pieces, n, own_blocks, scale):
+    block = vals.shape[-1]
     rows, width = pieces[0].shape
     shapes = [jax.ShapeDtypeStruct((2 * rows, width), BF16)]
     shapes += [jax.ShapeDtypeStruct((rows, width), F32)] * 2
     size = vals.size * 2 + 2 * n * rows * width * 2 + rows * width * 12
     return pl.pallas_call(
-        functools.partial(blocks_kernel, n, own_blocks, block, scale),
+        functools.partial(gather_kernel, n, own_blocks, block, scale),
         out_shape=shapes,
-        in_specs=[SMEM, SMEM, VMEM] + [VMEM] * n,
+        in_specs=[SMEM, SMEM, VMEM] + [VMEM] * (n + 1),
         out_specs=[VMEM] * 3,
         scratch_shapes=[pltpu.VMEM((n * rows, width), BF16)],
         compiler_params=pltpu.CompilerParams(vmem_limit_bytes=size + (8 << 20)),
         cost_estimate=pl.CostEstimate(
             flops=2 * vals.size * width, bytes_accessed=size, transcendentals=0
         ),
-        name="apply_blocks",
+        name="gather_blocks",
     )(where, rep, vals, *pieces)
+
+
+def scatter_kernel(own_blocks, block, scale, where_ref, rep_ref, vals_ref, *refs):
+    sources, (own_ref, out_ref) = refs[:4], refs[4:]
+    rows = own_blocks * block
+    out_ref[...] = jnp.zeros_like(out_ref)
+    me = rep_ref[0]
+    for mask in range(4):
+        base = lax.bitwise_xor(me, mask) * own_blocks
+        for j in range(own_blocks):
+            source = sources[mask][j * block : (j + 1) * block, :]
+            if scale is not None:
+                source = source * jnp.asarray(scale, BF16)
+            for s in range(2):
+                item = (base + j) * 2 + s
+                start = pl.multiple_of(where_ref[item] * block, block)
+                term = lax.dot_general(vals_ref[item], source, (((0,), (0,)), ((), ())), preferred_element_type=F32)
+                out_ref[pl.ds(start, block), :] += term
+    own_ref[...] = out_ref[:rows, :]
+
+
+def scatter_blocks(where, rep, vals, sources, n, own_blocks, scale):
+    block = vals.shape[-1]
+    rows, width = sources[0].shape
+    size = vals.size * 2 + 4 * rows * width * 2 + (n + 1) * rows * width * 4
+    return pl.pallas_call(
+        functools.partial(scatter_kernel, own_blocks, block, scale),
+        out_shape=[jax.ShapeDtypeStruct((rows, width), F32), jax.ShapeDtypeStruct((n * rows, width), F32)],
+        in_specs=[SMEM, SMEM, VMEM] + [VMEM] * 4,
+        out_specs=[VMEM] * 2,
+        compiler_params=pltpu.CompilerParams(vmem_limit_bytes=size + (4 << 20)),
+        cost_estimate=pl.CostEstimate(
+            flops=2 * vals.size * width, bytes_accessed=size, transcendentals=0
+        ),
+        name="scatter_blocks",
+    )(where, rep, vals, *sources)
+
+
+def near_kernel(vals_ref, out_ref):
+    out_ref[...] = vals_ref[0, :8, :]
+
+
+def brought_near(vals):
+    return pl.pallas_call(
+        near_kernel,
+        out_shape=jax.ShapeDtypeStruct((8, vals.shape[-1]), vals.dtype),
+        in_specs=[VMEM],
+        out_specs=VMEM,
+        compiler_params=pltpu.CompilerParams(vmem_limit_bytes=4 << 20),
+        name="brought_near",
+    )(vals)
+
+
+def add_terms(pair, terms, sent):
+    right, left = (array.astype(F32) for array in pair)
+    mid = terms[0].shape[0] // 2
+    if right.shape[0] == mid:
+        right = jnp.concatenate([terms[0][:mid] + right, terms[0][mid:]], 0)
+        left = jnp.concatenate([terms[1][:mid], terms[1][mid:] + left], 0)
+    else:
+        right, left = terms[0] + right, terms[1] + left
+    return right.astype(sent), left.astype(sent)
+
+
+def spread(first, second, n, own_blocks, numbers, vals, scale, hooks):
+    ahead, behind = ring_ways(n)
+    rows, half = first.shape[0], n // 2
+    mid = rows // 2
+    sent = BF16 if n <= 8 else F32
+    pairs = [[(i, i ^ mask) for i in range(4)] for mask in range(4)]
+    hook = lambda name, after: hooks[name](after) if name in hooks else ()
+    step = lambda pair: (lax.ppermute(pair[0], "rows", ahead), lax.ppermute(pair[1], "rows", behind))
+
+    across = lax.ppermute(second, "rep", pairs[2])
+    beside = lax.ppermute(tie(second, hook("beside", ())), "rep", pairs[1])
+    gathered = step((first, first))
+    pieces = [first] + [None] * n
+    pieces[1], pieces[n] = gathered
+    moving = None
+    for hop in range(2, half + 1):
+        if hop == 2:
+            gathered = tie(gathered, (across, hook("gather 2", across)))
+            far = lax.ppermute(across, "rep", pairs[1])
+        else:
+            gathered = tie(gathered, (moving, hook("gather %d" % hop, moving)))
+        if hop == half:
+            gathered = gathered[0][:mid], gathered[1][mid:]
+        behind_it = gathered
+        gathered = step(gathered)
+        pieces[hop], pieces[n + 1 - hop] = gathered
+        if hop == 2:
+            where, rep = numbers()
+            sources = tie([second, beside, across, far], behind_it)
+            own, partial = scatter_blocks(where, rep, vals, sources, n, own_blocks, scale)
+            term = lambda distance: partial[distance * rows : (distance + 1) * rows]
+            moving = term(half)[:mid].astype(sent), term(half)[mid:].astype(sent)
+        else:
+            moving = tie(add_terms(step(moving), (term(half + hop - 2), term(half - hop + 2)), sent), behind_it)
+    pieces = tie(pieces, (moving, hook("blocks", moving)))
+    *summed, crossing = reduce_rep(gather_blocks(where, rep, vals, pieces, n, own_blocks, scale))
+    moving = add_terms(step(moving), (term(n - 1), term(1)), sent)
+    moving = tie(moving, (crossing, hook("last", crossing)))
+    right, left = step(moving)
+    return [*summed, own, right, left], moving
 
 
 def reduce_rep(parts):
@@ -103,12 +194,11 @@
 
 
 def joined(refs):
-    halves = []
-    for h in range(len(refs) // 3):
-        near, got, cross = refs[3 * h : 3 * h + 3]
-        rows = near.shape[0]
-        halves.append(near[...] + got[rows:, :].astype(F32) + cross[...].astype(F32))
-    return jnp.concatenate(halves, axis=1)
+    near, got, cross, own, right, left = refs
+    rows = near.shape[0]
+    first = near[...] + got[rows:, :].astype(F32) + cross[...].astype(F32)
+    second = own[...] + (right[...].astype(F32) + left[...].astype(F32))
+    return jnp.concatenate([first, second], axis=1)
 
 
 def middle_kernel(rep_ref, weight_ref, grad_ref, *refs):
@@ -273,26 +363,19 @@
         cols = cols.reshape(-1)
         back_steps = (ring_place(my, n) - ring_place(cols // own_blocks, n) + n) % n
         ready["rep"], ready["where"] = rep, back_steps * own_blocks + cols % own_blocks
-        return ready["rep"], ready["where"]
-
-    sums = []
-    for pieces in gather_ring(chunks, n, {(2, 1): prepared}):
-        parts = apply_blocks(ready["where"], ready["rep"], vals, pieces, own_blocks, SCALE)
-        sums += reduce_rep(parts)[:3]
+        return ready["rep"], ready["where"], brought_near(vals)
+
+    numbers = lambda: (ready["where"], ready["rep"])
+    sums, _ = spread(*chunks, n, own_blocks, numbers, vals, SCALE, {"beside": prepared})
     rep = ready["rep"]
     activated, high, low, *masked = middle(rep, weight, out_grad, sums)
 
     node_total = own_rows * n * 4
     grad = GradientSum(rep, high, low, masked, n, 1.0 / (SCALE * math.sqrt(node_total)))
-    beside = {(2, 0): grad.start, (3, 0): grad.over_rep, (4, 0): lambda _: grad.over_rows([1])}
-    gathered = gather_ring(masked, n, beside)
-    gathered[1] = tie(gathered[1], grad.over_rows([1 << i for i in range(1, n.bit_length() - 1)]))
-    sums = []
-    for pieces in gathered:
-        parts = apply_blocks(ready["where"], rep, vals, pieces, own_blocks, None)
-        *parts, crossing = reduce_rep(parts)
-        sums += parts
-    weight_grad = grad.finish(crossing)
+    hooks = {"gather 2": grad.start, "gather 3": grad.over_rep, "gather 4": lambda _: grad.over_rows([1])}
+    hooks["last"] = lambda _: grad.over_rows([1 << i for i in range(1, n.bit_length() - 1)])
+    sums, moving = spread(*masked, n, own_blocks, numbers, vals, None, hooks)
+    weight_grad = grad.finish(moving)
     input_grad = last(weight, sums)
     return activated, input_grad, weight_grad
 

time: 135 us -> 121 us (0.90)
  waiting for transfers between devices: 66.3 us -> 56.4 us
  starting transfers between devices: 53 us -> 47.5 us
    ppermute x4 -> x2, waiting for transfers between devices: 10.8 us -> 0.17 us  [reduce_rep(): lax.ppermute(crossing, 'rep', [(i, i ^ 2) for i in range(4)])]
    ppermute x3, waiting for transfers between devices: 11.7 us -> 5.84 us  [finish(): lax.ppermute(self.value, 'rep', self.pairs[mask])]
    ppermute x1, waiting for transfers between devices: 4.08 us -> 9.29 us  [over_rows(): value = value + lax.ppermute(value, 'rows', pairs[step])]
    ppermute x4 -> x2, starting transfers between devices: 6.21 us -> 2.51 us  [reduce_rep(): lax.ppermute(crossing, 'rep', [(i, i ^ 2) for i in range(4)])]
    ppermute x28 -> x38, waiting for transfers between devices: 39 us -> 41 us  [the longest x16 21.9 us: spread(): lax.ppermute(pair[0], 'rows', ahead)]
    ppermute x28 -> x38, starting transfers between devices: 38.6 us -> 36.9 us  [the longest x16 19.5 us: spread(): lax.ppermute(pair[0], 'rows', ahead)]
    ppermute x2, starting transfers between devices: 2.72 us -> 4.37 us  [over_rows(): lax.ppermute(value, 'rows', pairs[step])]
  transfers between devices with their start and end apart: 46 -> 52, of which waited for: 24 -> 28; matrix products, arithmetic and copies ran while one was open for 1% -> 2% of each run, Pallas kernels for 6% -> 6%
where the time goes in v3:
time: 121 us; the launch traced here: 120 us
  waiting for transfers between devices  56.4 us (47%)
  starting transfers between devices  47.5 us (39%)
  Pallas kernels  10.6 us (9%)
  local copies, waits for them, and re-layouts  3.65 us (3%)
  other arithmetic  1.29 us (1%)
    ppermute x16, waiting for transfers between devices, spread(): lax.ppermute(pair[0], 'rows', ahead)  21.9 us
    ppermute x16, starting transfers between devices, spread(): lax.ppermute(pair[0], 'rows', ahead)  19.5 us
    ppermute x16, starting transfers between devices, spread(): lax.ppermute(pair[1], 'rows', behind)  13.2 us
    ppermute x16, waiting for transfers between devices, spread(): lax.ppermute(pair[1], 'rows', behind)  12.3 us
    ppermute x1, waiting for transfers between devices, over_rows(): value = value + lax.ppermute(value, 'rows', pairs[step])  9.29 us
    ppermute x2, waiting for transfers between devices, spread(): across = lax.ppermute(second, 'rep', pairs[2])  6.82 us
    ppermute x3, waiting for transfers between devices, finish(): lax.ppermute(self.value, 'rep', self.pairs[mask])  5.84 us
    ppermute x2, starting transfers between devices, over_rows(): lax.ppermute(value, 'rows', pairs[step])  4.37 us
  transfers between devices with their start and end apart: 52, of which 28 were waited for; matrix products, arithmetic and copies ran while one was open for 2% of the time, Pallas kernels for 6%

profile of v3, /device:TPU:0, one launch (start us, length us, event | category | flops | bytes accessed | tf_op | source)
XLA Modules:
  0.0 120.5 jit_solution(10490992873205083480)
XLA Ops:
  1.7 3.0 %collective-permute-start.2 = (bf16[1024,128]{1,0:T(8,128)(2,1)S(1)}, bf16[1024,128]{1,0:T(8,128)(2,1)S(1)}, u32[]{:S(2)}, u32[]{:S(2)}) collective-permute-start(bf16[1024,128]{1,0:T(8,128)(2,1)S(1)} %get-tuple-element.87.refs_0_), channel_id=1, source_target_pairs={{0,2},{1,3},{2,0},{3,1},{4,6},{5,7},{6,4},{7,5},{8,10},{9,11},{10,... | collective-permute-start | bytes 786440 | tf_op jit(solution)/shard_map/ppermute | solution.py:156
  4.7 1.6 %collective-permute-start = (bf16[1024,128]{1,0:T(8,128)(2,1)S(1)}, bf16[1024,128]{1,0:T(8,128)(2,1)S(1)}, u32[]{:S(2)}, u32[]{:S(2)}) collective-permute-start(bf16[1024,128]{1,0:T(8,128)(2,1)S(1)} %get-tuple-element.100.refs_0_), channel_id=1, source_target_pairs={{0,8},{8,16},{16,24},{24,28},{28,20},{20,12},{12,4},{4,0},{1,9},{9... | collective-permute-start | bytes 786440 | tf_op jit(solution)/shard_map/ppermute | solution.py:154
  7.7 3.3 %collective-permute-done.2.refs_2_ = bf16[1024,128]{1,0:T(8,128)(2,1)S(1)} collective-permute-done((bf16[1024,128]{1,0:T(8,128)(2,1)S(1)}, bf16[1024,128]{1,0:T(8,128)(2,1)S(1)}, u32[]{:S(2)}, u32[]{:S(2)}) %collective-permute-start.2) | collective-permute-done | bytes 262176 | tf_op jit(solution)/shard_map/ppermute | solution.py:156
  15.8 1.6 %copy-done = bf16[32,1,2,128,128]{4,3,2,1,0:T(8,128)(2,1)S(1)} copy-done((bf16[32,1,2,128,128]{4,3,2,1,0:T(8,128)(2,1)S(1)}, bf16[32,1,2,128,128]{4,3,2,1,0:T(8,128)(2,1)}, u32[]{:S(2)}) %copy-start) | copy-done | bytes 2097176
  17.4 1.6 %scatter_blocks.2 = (f32[1024,128]{1,0:T(8,128)S(1)}, f32[8192,128]{1,0:T(8,128)S(1)}) custom-call(s32[64]{0:T(128)S(1)} %fusion.where_ref, s32[1]{0:T(128)} %bitcast.rep_ref, bf16[64,128,128]{2,1,0:T(8,128)(2,1)S(1)} %bitcast.4, bf16[1024,128]{1,0:T(8,128)(2,1)S(1)} %get-tuple-element.87.refs_0_, bf16[1024,128]{1,0:T(8,128)(2,1)S(1)} %collective-permute-done.5.refs_1_, ...), custom_call_target="tpu_custom_call" | custom-call | flops 268435456 | bytes 7864320 | tf_op jit(solution)/shard_map/scatter_blocks/pallas_call | solution.py:108
  21.4 2.0 %collective-permute-done.4.refs_7_ = bf16[1024,128]{1,0:T(8,128)(2,1)S(1)} collective-permute-done((bf16[1024,128]{1,0:T(8,128)(2,1)S(1)}, bf16[1024,128]{1,0:T(8,128)(2,1)S(1)}, u32[]{:S(2)}, u32[]{:S(2)}) %collective-permute-start.4) | collective-permute-done | bytes 262176 | tf_op jit(solution)/shard_map/ppermute | solution.py:154
  26.4 1.6 %collective-permute-start.13 = (bf16[1024,128]{1,0:T(8,128)(2,1)S(1)}, bf16[1024,128]{1,0:T(8,128)(2,1)S(1)}, u32[]{:S(2)}, u32[]{:S(2)}) collective-permute-start(bf16[1024,128]{1,0:T(8,128)(2,1)S(1)} %get-tuple-element.94), channel_id=1, source_target_pairs={{0,8},{8,16},{16,24},{24,28},{28,20},{20,12},{12,4},{4,0},{1,9},{9... | collective-permute-start | bytes 786440 | tf_op jit(solution)/shard_map/ppermute | solution.py:154
  28.4 4.2 %collective-permute-done.7.refs_3_ = bf16[1024,128]{1,0:T(8,128)(2,1)S(1)} collective-permute-done((bf16[1024,128]{1,0:T(8,128)(2,1)S(1)}, bf16[1024,128]{1,0:T(8,128)(2,1)S(1)}, u32[]{:S(2)}, u32[]{:S(2)}) %collective-permute-start.7) | collective-permute-done | bytes 262176 | tf_op jit(solution)/shard_map/ppermute | solution.py:154
  41.4 1.7 %gather_blocks.2 = (bf16[2048,128]{1,0:T(8,128)(2,1)S(1)}, f32[1024,128]{1,0:T(8,128)S(1)}, f32[1024,128]{1,0:T(8,128)S(1)}) custom-call(s32[64]{0:T(128)S(1)} %fusion.where_ref, s32[1]{0:T(128)} %bitcast.rep_ref, bf16[64,128,128]{2,1,0:T(8,128)(2,1)S(1)} %bitcast.5, bf16[1024,128]{1,0:T(8,128)(2,1)S(1)} %get-tuple-element.100.refs_0_, ...), custom_call_target="tpu_custom_call" | custom-call | flops 268435456 | bytes 7864320 | tf_op jit(solution)/shard_map/gather_blocks/pallas_call | solution.py:71
  48.8 4.7 %collective-permute-done.19.refs_4_ = bf16[1024,128]{1,0:T(8,128)(2,1)S(1)} collective-permute-done((bf16[1024,128]{1,0:T(8,128)(2,1)S(1)}, bf16[1024,128]{1,0:T(8,128)(2,1)S(1)}, u32[]{:S(2)}, u32[]{:S(2)}) %collective-permute-start.19) | collective-permute-done | bytes 262176 | tf_op jit(solution)/shard_map/ppermute | solution.py:154
  57.7 1.7 %collective-permute-start.21 = (bf16[1024,128]{1,0:T(8,128)(2,1)S(1)}, bf16[1024,128]{1,0:T(8,128)(2,1)S(1)}, u32[]{:S(2)}, u32[]{:S(2)}) collective-permute-start(bf16[1024,128]{1,0:T(8,128)(2,1)S(1)} %get-tuple-element.143.refs_0_), channel_id=1, source_target_pairs={{0,8},{8,16},{16,24},{24,28},{28,20},{20,12},{12,4},{4,0},{1,9},{9... | collective-permute-start | bytes 786440 | tf_op jit(solution)/shard_map/ppermute | solution.py:154
  59.7 3.5 %collective-permute-done.23.refs_2_ = bf16[1024,128]{1,0:T(8,128)(2,1)S(1)} collective-permute-done((bf16[1024,128]{1,0:T(8,128)(2,1)S(1)}, bf16[1024,128]{1,0:T(8,128)(2,1)S(1)}, u32[]{:S(2)}, u32[]{:S(2)}) %collective-permute-start.23) | collective-permute-done | bytes 262176 | tf_op jit(solution)/shard_map/ppermute | solution.py:156
  68.1 1.6 %scatter_blocks.3 = (f32[1024,128]{1,0:T(8,128)S(1)}, f32[8192,128]{1,0:T(8,128)S(1)}) custom-call(s32[64]{0:T(128)S(1)} %fusion.where_ref, s32[1]{0:T(128)} %bitcast.rep_ref, bf16[64,128,128]{2,1,0:T(8,128)(2,1)S(1)} %bitcast.6, bf16[1024,128]{1,0:T(8,128)(2,1)S(1)} %get-tuple-element.130.refs_1_.refs_0_, ...), custom_call_target="tpu_custom_call" | custom-call | flops 268435456 | bytes 7864320 | tf_op jit(solution)/shard_map/scatter_blocks/pallas_call | solution.py:108
  72.1 3.1 %collective-permute-done.24.refs_2_ = bf16[1024,128]{1,0:T(8,128)(2,1)S(1)} collective-permute-done((bf16[1024,128]{1,0:T(8,128)(2,1)S(1)}, bf16[1024,128]{1,0:T(8,128)(2,1)S(1)}, u32[]{:S(2)}, u32[]{:S(2)}) %collective-permute-start.24) | collective-permute-done | bytes 262176 | tf_op jit(solution)/shard_map/ppermute | solution.py:154
  76.8 1.8 %collective-permute-start.32 = (bf16[1024,128]{1,0:T(8,128)(2,1)S(1)}, bf16[1024,128]{1,0:T(8,128)(2,1)S(1)}, u32[]{:S(2)}, u32[]{:S(2)}) collective-permute-start(bf16[1024,128]{1,0:T(8,128)(2,1)S(1)} %collective-permute-done.25.refs_7_), channel_id=1, source_target_pairs={{8,0},{16,8},{24,16},{28,24},{20,28},{12,20},{4,12},{0,4},{9,1},{1... | collective-permute-start | bytes 786440 | tf_op jit(solution)/shard_map/ppermute | solution.py:154
  79.7 1.8 %collective-permute-start.39 = (bf16[1024,128]{1,0:T(8,128)(2,1)S(1)}, bf16[1024,128]{1,0:T(8,128)(2,1)S(1)}, u32[]{:S(2)}, u32[]{:S(2)}) collective-permute-start(bf16[1024,128]{1,0:T(8,128)(2,1)S(1)} %pad_maximum_fusion.3), channel_id=1, source_target_pairs={{8,0},{16,8},{24,16},{28,24},{20,28},{12,20},{4,12},{0,4},{9,1},{1... | collective-permute-start | bytes 786440 | tf_op jit(solution)/shard_map/ppermute | solution.py:154
  81.7 9.3 %collective-permute-done.35 = f32[64,256]{1,0:T(8,128)S(1)} collective-permute-done((f32[64,256]{1,0:T(8,128)S(1)}, f32[64,256]{1,0:T(8,128)S(1)}, u32[]{:S(2)}, u32[]{:S(2)}) %collective-permute-start.35) | collective-permute-done | bytes 65568 | tf_op jit(solution)/shard_map/ppermute | solution.py:342
  91.1 2.6 %collective-permute-start.45 = (f32[64,256]{1,0:T(8,128)S(1)}, f32[64,256]{1,0:T(8,128)S(1)}, u32[]{:S(2)}, u32[]{:S(2)}) collective-permute-start(f32[64,256]{1,0:T(8,128)S(1)} %add.108), channel_id=1, source_target_pairs={{0,16},{4,20},{8,24},{12,28},{16,0},{20,4},{24,8},{28,12},{1,17},{... | collective-permute-start | bytes 196616 | tf_op jit(solution)/shard_map/ppermute | solution.py:338
  93.8 1.7 %collective-permute-start.46 = (f32[64,256]{1,0:T(8,128)S(1)}, f32[64,256]{1,0:T(8,128)S(1)}, u32[]{:S(2)}, u32[]{:S(2)}) collective-permute-start(f32[64,256]{1,0:T(8,128)S(1)} %add.108), channel_id=1, source_target_pairs={{0,24},{4,28},{8,16},{12,20},{16,8},{20,12},{24,0},{28,4},{1,25},{... | collective-permute-start | bytes 196616 | tf_op jit(solution)/shard_map/ppermute | solution.py:338
  95.6 2.0 %collective-permute-start.37 = (bf16[512,128]{1,0:T(8,128)(2,1)S(1)}, bf16[512,128]{1,0:T(8,128)(2,1)S(1)}, u32[]{:S(2)}, u32[]{:S(2)}) collective-permute-start(bf16[512,128]{1,0:T(8,128)(2,1)S(1)} %slice.134), channel_id=1, source_target_pairs={{8,0},{16,8},{24,16},{28,24},{20,28},{12,20},{4,12},{0,4},{9,1},{1... | collective-permute-start | bytes 393224 | tf_op jit(solution)/shard_map/ppermute | solution.py:154
  97.7 2.8 %collective-permute-done.36.refs_4_ = bf16[512,128]{1,0:T(8,128)(2,1)S(1)} collective-permute-done((bf16[512,128]{1,0:T(8,128)(2,1)S(1)}, bf16[512,128]{1,0:T(8,128)(2,1)S(1)}, u32[]{:S(2)}, u32[]{:S(2)}) %collective-permute-start.36) | collective-permute-done | bytes 131104 | tf_op jit(solution)/shard_map/ppermute | solution.py:154
  104.1 2.8 %collective-permute-done.42 = bf16[1024,128]{1,0:T(8,128)(2,1)S(1)} collective-permute-done((bf16[1024,128]{1,0:T(8,128)(2,1)S(1)}, bf16[1024,128]{1,0:T(8,128)(2,1)S(1)}, u32[]{:S(2)}, u32[]{:S(2)}) %collective-permute-start.42) | collective-permute-done | bytes 262176 | tf_op jit(solution)/shard_map/ppermute | solution.py:154
  107.9 2.0 %collective-permute-start.47 = (bf16[1024,128]{1,0:T(8,128)(2,1)S(1)}, bf16[1024,128]{1,0:T(8,128)(2,1)S(1)}, u32[]{:S(2)}, u32[]{:S(2)}) collective-permute-start(bf16[1024,128]{1,0:T(8,128)(2,1)S(1)} %get-tuple-element.156), channel_id=1, source_target_pairs={{0,8},{8,16},{16,24},{24,28},{28,20},{20,12},{12,4},{4,0},{1,9},{9... | collective-permute-start | bytes 786440 | tf_op jit(solution)/shard_map/ppermute | solution.py:154
  113.2 5.2 %collective-permute-done.50.refs_2_ = f32[64,256]{1,0:T(8,128)S(1)} collective-permute-done((f32[64,256]{1,0:T(8,128)S(1)}, f32[64,256]{1,0:T(8,128)S(1)}, u32[]{:S(2)}, u32[]{:S(2)}) %collective-permute-start.50) | collective-permute-done | bytes 65568 | tf_op jit(solution)/shard_map/ppermute | solution.py:348
  (122 shorter events, 52.1 us)
Async XLA Ops:
  1.7 9.3 %collective-permute-start.2 = (bf16[1024,128]{1,0:T(8,128)(2,1)S(1)}, bf16[1024,128]{1,0:T(8,128)(2,1)S(1)}, u32[]{:S(2)}, u32[]{:S(2)}) collective-permute-start(bf16[1024,128]{1,0:T(8,128)(2,1)S(1)} %get-tuple-element.87.refs_0_), channel_id=1, source_target_pairs={{0,2},{1,3},{2,0},{3,1},{4,6},{5,7},{6,4},{7,5},{8,10},{9,11},{10,... | collective-permute-start | bytes 786440 | tf_op jit(solution)/shard_map/ppermute | solution.py:156
  4.7 7.8 %collective-permute-start = (bf16[1024,128]{1,0:T(8,128)(2,1)S(1)}, bf16[1024,128]{1,0:T(8,128)(2,1)S(1)}, u32[]{:S(2)}, u32[]{:S(2)}) collective-permute-start(bf16[1024,128]{1,0:T(8,128)(2,1)S(1)} %get-tuple-element.100.refs_0_), channel_id=1, source_target_pairs={{0,8},{8,16},{16,24},{24,28},{28,20},{20,12},{12,4},{4,0},{1,9},{9... | collective-permute-start | bytes 786440 | tf_op jit(solution)/shard_map/ppermute | solution.py:154
  7.6 8.2 %collective-permute-start.5 = (bf16[1024,128]{1,0:T(8,128)(2,1)S(1)}, bf16[1024,128]{1,0:T(8,128)(2,1)S(1)}, u32[]{:S(2)}, u32[]{:S(2)}) collective-permute-start(bf16[1024,128]{1,0:T(8,128)(2,1)S(1)} %get-tuple-element.87.refs_0_), channel_id=1, source_target_pairs={{0,1},{1,0},{2,3},{3,2},{4,5},{5,4},{6,7},{7,6},{8,9},{9,8},{10,11... | collective-permute-start | bytes 786440 | tf_op jit(solution)/shard_map/ppermute | solution.py:157
  15.3 8.0 %collective-permute-start.4 = (bf16[1024,128]{1,0:T(8,128)(2,1)S(1)}, bf16[1024,128]{1,0:T(8,128)(2,1)S(1)}, u32[]{:S(2)}, u32[]{:S(2)}) collective-permute-start(bf16[1024,128]{1,0:T(8,128)(2,1)S(1)} %collective-permute-done.1.refs_8_), channel_id=1, source_target_pairs={{8,0},{16,8},{24,16},{28,24},{20,28},{12,20},{4,12},{0,4},{9,1},{1... | collective-permute-start | bytes 786440 | tf_op jit(solution)/shard_map/ppermute | solution.py:154
  23.4 9.2 %collective-permute-start.7 = (bf16[1024,128]{1,0:T(8,128)(2,1)S(1)}, bf16[1024,128]{1,0:T(8,128)(2,1)S(1)}, u32[]{:S(2)}, u32[]{:S(2)}) collective-permute-start(bf16[1024,128]{1,0:T(8,128)(2,1)S(1)} %collective-permute-done.3.refs_2_), channel_id=1, source_target_pairs={{0,8},{8,16},{16,24},{24,28},{28,20},{20,12},{12,4},{4,0},{1,9},{9... | collective-permute-start | bytes 786440 | tf_op jit(solution)/shard_map/ppermute | solution.py:154
  24.9 9.2 %collective-permute-start.8 = (bf16[1024,128]{1,0:T(8,128)(2,1)S(1)}, bf16[1024,128]{1,0:T(8,128)(2,1)S(1)}, u32[]{:S(2)}, u32[]{:S(2)}) collective-permute-start(bf16[1024,128]{1,0:T(8,128)(2,1)S(1)} %collective-permute-done.4.refs_7_), channel_id=1, source_target_pairs={{8,0},{16,8},{24,16},{28,24},{20,28},{12,20},{4,12},{0,4},{9,1},{1... | collective-permute-start | bytes 786440 | tf_op jit(solution)/shard_map/ppermute | solution.py:154
  26.4 11.1 %collective-permute-start.13 = (bf16[1024,128]{1,0:T(8,128)(2,1)S(1)}, bf16[1024,128]{1,0:T(8,128)(2,1)S(1)}, u32[]{:S(2)}, u32[]{:S(2)}) collective-permute-start(bf16[1024,128]{1,0:T(8,128)(2,1)S(1)} %get-tuple-element.94), channel_id=1, source_target_pairs={{0,8},{8,16},{16,24},{24,28},{28,20},{20,12},{12,4},{4,0},{1,9},{9... | collective-permute-start | bytes 786440 | tf_op jit(solution)/shard_map/ppermute | solution.py:154
  28.0 10.0 %collective-permute-start.14 = (bf16[1024,128]{1,0:T(8,128)(2,1)S(1)}, bf16[1024,128]{1,0:T(8,128)(2,1)S(1)}, u32[]{:S(2)}, u32[]{:S(2)}) collective-permute-start(bf16[1024,128]{1,0:T(8,128)(2,1)S(1)} %get-tuple-element.95), channel_id=1, source_target_pairs={{8,0},{16,8},{24,16},{28,24},{20,28},{12,20},{4,12},{0,4},{9,1},{1... | collective-permute-start | bytes 786440 | tf_op jit(solution)/shard_map/ppermute | solution.py:154
  45.6 7.9 %collective-permute-start.19 = (bf16[1024,128]{1,0:T(8,128)(2,1)S(1)}, bf16[1024,128]{1,0:T(8,128)(2,1)S(1)}, u32[]{:S(2)}, u32[]{:S(2)}) collective-permute-start(bf16[1024,128]{1,0:T(8,128)(2,1)S(1)} %get-tuple-element.113), channel_id=1, source_target_pairs={{0,8},{8,16},{16,24},{24,28},{28,20},{20,12},{12,4},{4,0},{1,9},{9... | collective-permute-start | bytes 786440 | tf_op jit(solution)/shard_map/ppermute | solution.py:154
  66.0 9.2 %collective-permute-start.24 = (bf16[1024,128]{1,0:T(8,128)(2,1)S(1)}, bf16[1024,128]{1,0:T(8,128)(2,1)S(1)}, u32[]{:S(2)}, u32[]{:S(2)}) collective-permute-start(bf16[1024,128]{1,0:T(8,128)(2,1)S(1)} %collective-permute-done.21.refs_1_), channel_id=1, source_target_pairs={{0,8},{8,16},{16,24},{24,28},{28,20},{20,12},{12,4},{4,0},{1,9},{9... | collective-permute-start | bytes 786440 | tf_op jit(solution)/shard_map/ppermute | solution.py:154
  67.5 9.1 %collective-permute-start.25 = (bf16[1024,128]{1,0:T(8,128)(2,1)S(1)}, bf16[1024,128]{1,0:T(8,128)(2,1)S(1)}, u32[]{:S(2)}, u32[]{:S(2)}) collective-permute-start(bf16[1024,128]{1,0:T(8,128)(2,1)S(1)} %collective-permute-done.22.refs_8_), channel_id=1, source_target_pairs={{8,0},{16,8},{24,16},{28,24},{20,28},{12,20},{4,12},{0,4},{9,1},{1... | collective-permute-start | bytes 786440 | tf_op jit(solution)/shard_map/ppermute | solution.py:154
  70.0 8.7 %collective-permute-start.33 = (bf16[512,128]{1,0:T(8,128)(2,1)S(1)}, bf16[512,128]{1,0:T(8,128)(2,1)S(1)}, u32[]{:S(2)}, u32[]{:S(2)}) collective-permute-start(bf16[512,128]{1,0:T(8,128)(2,1)S(1)} %get-tuple-element.174), channel_id=1, source_target_pairs={{0,8},{8,16},{16,24},{24,28},{28,20},{20,12},{12,4},{4,0},{1,9},{9... | collective-permute-start | bytes 393224 | tf_op jit(solution)/shard_map/ppermute | solution.py:154
  71.5 7.8 %collective-permute-start.34 = (bf16[512,128]{1,0:T(8,128)(2,1)S(1)}, bf16[512,128]{1,0:T(8,128)(2,1)S(1)}, u32[]{:S(2)}, u32[]{:S(2)}) collective-permute-start(bf16[512,128]{1,0:T(8,128)(2,1)S(1)} %get-tuple-element.173), channel_id=1, source_target_pairs={{8,0},{16,8},{24,16},{28,24},{20,28},{12,20},{4,12},{0,4},{9,1},{1... | collective-permute-start | bytes 393224 | tf_op jit(solution)/shard_map/ppermute | solution.py:154
  76.6 14.5 %collective-permute-start.31 = (bf16[1024,128]{1,0:T(8,128)(2,1)S(1)}, bf16[1024,128]{1,0:T(8,128)(2,1)S(1)}, u32[]{:S(2)}, u32[]{:S(2)}) collective-permute-start(bf16[1024,128]{1,0:T(8,128)(2,1)S(1)} %collective-permute-done.24.refs_2_), channel_id=1, source_target_pairs={{0,8},{8,16},{16,24},{24,28},{28,20},{20,12},{12,4},{4,0},{1,9},{9... | collective-permute-start | bytes 786440 | tf_op jit(solution)/shard_map/ppermute | solution.py:154
  76.8 17.0 %collective-permute-start.32 = (bf16[1024,128]{1,0:T(8,128)(2,1)S(1)}, bf16[1024,128]{1,0:T(8,128)(2,1)S(1)}, u32[]{:S(2)}, u32[]{:S(2)}) collective-permute-start(bf16[1024,128]{1,0:T(8,128)(2,1)S(1)} %collective-permute-done.25.refs_7_), channel_id=1, source_target_pairs={{8,0},{16,8},{24,16},{28,24},{20,28},{12,20},{4,12},{0,4},{9,1},{1... | collective-permute-start | bytes 786440 | tf_op jit(solution)/shard_map/ppermute | solution.py:154
  79.4 16.1 %collective-permute-start.38 = (bf16[1024,128]{1,0:T(8,128)(2,1)S(1)}, bf16[1024,128]{1,0:T(8,128)(2,1)S(1)}, u32[]{:S(2)}, u32[]{:S(2)}) collective-permute-start(bf16[1024,128]{1,0:T(8,128)(2,1)S(1)} %pad_maximum_fusion.2), channel_id=1, source_target_pairs={{0,8},{8,16},{16,24},{24,28},{28,20},{20,12},{12,4},{4,0},{1,9},{9... | collective-permute-start | bytes 786440 | tf_op jit(solution)/shard_map/ppermute | solution.py:154
  79.7 16.0 %collective-permute-start.39 = (bf16[1024,128]{1,0:T(8,128)(2,1)S(1)}, bf16[1024,128]{1,0:T(8,128)(2,1)S(1)}, u32[]{:S(2)}, u32[]{:S(2)}) collective-permute-start(bf16[1024,128]{1,0:T(8,128)(2,1)S(1)} %pad_maximum_fusion.3), channel_id=1, source_target_pairs={{8,0},{16,8},{24,16},{28,24},{20,28},{12,20},{4,12},{0,4},{9,1},{1... | collective-permute-start | bytes 786440 | tf_op jit(solution)/shard_map/ppermute | solution.py:154
  81.5 9.6 %collective-permute-start.35 = (f32[64,256]{1,0:T(8,128)S(1)}, f32[64,256]{1,0:T(8,128)S(1)}, u32[]{:S(2)}, u32[]{:S(2)}) collective-permute-start(f32[64,256]{1,0:T(8,128)S(1)} %add_add_fusion.1), channel_id=1, source_target_pairs={{0,4},{4,0},{8,12},{12,8},{16,20},{20,16},{24,28},{28,24},{1,5},{5... | collective-permute-start | bytes 196616 | tf_op jit(solution)/shard_map/ppermute | solution.py:342
  91.0 12.9 %collective-permute-start.44 = (f32[64,256]{1,0:T(8,128)S(1)}, f32[64,256]{1,0:T(8,128)S(1)}, u32[]{:S(2)}, u32[]{:S(2)}) collective-permute-start(f32[64,256]{1,0:T(8,128)S(1)} %add.108), channel_id=1, source_target_pairs={{0,8},{4,12},{8,0},{12,4},{16,24},{20,28},{24,16},{28,20},{1,9},{5... | collective-permute-start | bytes 196616 | tf_op jit(solution)/shard_map/ppermute | solution.py:337
  91.1 12.9 %collective-permute-start.45 = (f32[64,256]{1,0:T(8,128)S(1)}, f32[64,256]{1,0:T(8,128)S(1)}, u32[]{:S(2)}, u32[]{:S(2)}) collective-permute-start(f32[64,256]{1,0:T(8,128)S(1)} %add.108), channel_id=1, source_target_pairs={{0,16},{4,20},{8,24},{12,28},{16,0},{20,4},{24,8},{28,12},{1,17},{... | collective-permute-start | bytes 196616 | tf_op jit(solution)/shard_map/ppermute | solution.py:338
  93.8 10.3 %collective-permute-start.46 = (f32[64,256]{1,0:T(8,128)S(1)}, f32[64,256]{1,0:T(8,128)S(1)}, u32[]{:S(2)}, u32[]{:S(2)}) collective-permute-start(f32[64,256]{1,0:T(8,128)S(1)} %add.108), channel_id=1, source_target_pairs={{0,24},{4,28},{8,16},{12,20},{16,8},{20,12},{24,0},{28,4},{1,25},{... | collective-permute-start | bytes 196616 | tf_op jit(solution)/shard_map/ppermute | solution.py:338
  107.9 11.3 %collective-permute-start.47 = (bf16[1024,128]{1,0:T(8,128)(2,1)S(1)}, bf16[1024,128]{1,0:T(8,128)(2,1)S(1)}, u32[]{:S(2)}, u32[]{:S(2)}) collective-permute-start(bf16[1024,128]{1,0:T(8,128)(2,1)S(1)} %get-tuple-element.156), channel_id=1, source_target_pairs={{0,8},{8,16},{16,24},{24,28},{28,20},{20,12},{12,4},{4,0},{1,9},{9... | collective-permute-start | bytes 786440 | tf_op jit(solution)/shard_map/ppermute | solution.py:154
  109.9 9.3 %collective-permute-start.48 = (bf16[1024,128]{1,0:T(8,128)(2,1)S(1)}, bf16[1024,128]{1,0:T(8,128)(2,1)S(1)}, u32[]{:S(2)}, u32[]{:S(2)}) collective-permute-start(bf16[1024,128]{1,0:T(8,128)(2,1)S(1)} %get-tuple-element.157), channel_id=1, source_target_pairs={{8,0},{16,8},{24,16},{28,24},{20,28},{12,20},{4,12},{0,4},{9,1},{1... | collective-permute-start | bytes 786440 | tf_op jit(solution)/shard_map/ppermute | solution.py:154
  110.0 9.2 %collective-permute-start.41 = (bf16[1024,128]{1,0:T(8,128)(2,1)S(1)}, bf16[1024,128]{1,0:T(8,128)(2,1)S(1)}, u32[]{:S(2)}, u32[]{:S(2)}) collective-permute-start(bf16[1024,128]{1,0:T(8,128)(2,1)S(1)} %add_convert_fusion.2), channel_id=1, source_target_pairs={{0,2},{1,3},{2,0},{3,1},{4,6},{5,7},{6,4},{7,5},{8,10},{9,11},{10,... | collective-permute-start | bytes 786440 | tf_op jit(solution)/shard_map/ppermute | solution.py:193
  (32 other events, 224.1 us)

commit v4 on v3

--- a/solution.py
+++ b/solution.py
@@ -47,7 +47,7 @@
     starts = [p * rows for p in range(half + 1)] + [half * rows + rows // 2]
     starts += [p * rows for p in range(half + 1, n)]
     for start, ref in zip(starts, pieces):
-        piece = ref[...]
+        piece = ref[: min(ref.shape[0], rows), :]
         pool[start : start + piece.shape[0], :] = piece if scale is None else piece * jnp.asarray(scale, BF16)
     me = rep_ref[0]
     for mask, out, first in ((3, send, 0), (1, send, own_blocks), (2, keep_far, 0), (0, keep_near, 0)):
@@ -76,7 +76,7 @@
         scratch_shapes=[pltpu.VMEM((n * rows, width), BF16)],
         compiler_params=pltpu.CompilerParams(vmem_limit_bytes=size + (8 << 20)),
         cost_estimate=pl.CostEstimate(
-            flops=2 * vals.size * width, bytes_accessed=size, transcendentals=0
+            flops=200 * vals.size * width, bytes_accessed=size, transcendentals=0
         ),
         name="gather_blocks",
     )(where, rep, vals, *pieces)
@@ -118,30 +118,20 @@
     )(where, rep, vals, *sources)
 
 
-def near_kernel(vals_ref, out_ref):
-    out_ref[...] = vals_ref[0, :8, :]
-
-
-def brought_near(vals):
-    return pl.pallas_call(
-        near_kernel,
-        out_shape=jax.ShapeDtypeStruct((8, vals.shape[-1]), vals.dtype),
-        in_specs=[VMEM],
-        out_specs=VMEM,
-        compiler_params=pltpu.CompilerParams(vmem_limit_bytes=4 << 20),
-        name="brought_near",
-    )(vals)
-
-
-def add_terms(pair, terms, sent):
-    right, left = (array.astype(F32) for array in pair)
-    mid = terms[0].shape[0] // 2
-    if right.shape[0] == mid:
+def add_terms(pair, terms, sent, riders):
+    rows = terms[0].shape[0]
+    mid = rows // 2
+    size = pair[0].shape[0] - riders
+    right, left = (array[:size].astype(F32) for array in pair)
+    if size == mid:
         right = jnp.concatenate([terms[0][:mid] + right, terms[0][mid:]], 0)
         left = jnp.concatenate([terms[1][:mid], terms[1][mid:] + left], 0)
     else:
         right, left = terms[0] + right, terms[1] + left
-    return right.astype(sent), left.astype(sent)
+    return tuple(
+        jnp.concatenate([array.astype(sent), came[size:]], 0) if riders else array.astype(sent)
+        for array, came in zip((right, left), pair)
+    )
 
 
 def spread(first, second, n, own_blocks, numbers, vals, scale, hooks):
@@ -158,7 +148,7 @@
     gathered = step((first, first))
     pieces = [first] + [None] * n
     pieces[1], pieces[n] = gathered
-    moving = None
+    moving, riders, arrived = None, 0, []
     for hop in range(2, half + 1):
         if hop == 2:
             gathered = tie(gathered, (across, hook("gather 2", across)))
@@ -166,7 +156,9 @@
         else:
             gathered = tie(gathered, (moving, hook("gather %d" % hop, moving)))
         if hop == half:
-            gathered = gathered[0][:mid], gathered[1][mid:]
+            gathered = gathered[0][:mid], gathered[1][mid:rows]
+        elif riders:
+            gathered = tuple(jnp.concatenate([array[:rows], rider.astype(array.dtype)], 0) for array in gathered)
         behind_it = gathered
         gathered = step(gathered)
         pieces[hop], pieces[n + 1 - hop] = gathered
@@ -176,14 +168,26 @@
             own, partial = scatter_blocks(where, rep, vals, sources, n, own_blocks, scale)
             term = lambda distance: partial[distance * rows : (distance + 1) * rows]
             moving = term(half)[:mid].astype(sent), term(half)[mid:].astype(sent)
+            if "riders" in hooks:
+                rider = hooks["riders"](behind_it).astype(sent)
+                riders = rider.shape[0]
+                moving = tuple(jnp.concatenate([array, rider], 0) for array in moving)
         else:
-            moving = tie(add_terms(step(moving), (term(half + hop - 2), term(half - hop + 2)), sent), behind_it)
-    pieces = tie(pieces, (moving, hook("blocks", moving)))
+            came = step(moving)
+            arrived.append(came)
+            moving = add_terms(came, (term(half + hop - 2), term(half - hop + 2)), sent, riders)
+            moving = tie(moving, behind_it)
+    pieces = tie(pieces, moving)
     *summed, crossing = reduce_rep(gather_blocks(where, rep, vals, pieces, n, own_blocks, scale))
-    moving = add_terms(step(moving), (term(n - 1), term(1)), sent)
-    moving = tie(moving, (crossing, hook("last", crossing)))
+    came = step(moving)
+    arrived.append(came)
+    moving = add_terms([array[:rows] for array in came], (term(n - 1), term(1)), sent, 0)
+    if riders:
+        moving = jnp.concatenate([moving[0], came[0][rows:]], 0), moving[1]
+    moving = tie(moving, crossing)
     right, left = step(moving)
-    return [*summed, own, right, left], moving
+    arrived.append((right, None))
+    return [*summed, own, right, left], arrived
 
 
 def reduce_rep(parts):
@@ -197,7 +201,7 @@
     near, got, cross, own, right, left = refs
     rows = near.shape[0]
     first = near[...] + got[rows:, :].astype(F32) + cross[...].astype(F32)
-    second = own[...] + (right[...].astype(F32) + left[...].astype(F32))
+    second = own[...] + (right[:rows, :].astype(F32) + left[...].astype(F32))
     return jnp.concatenate([first, second], axis=1)
 
 
@@ -270,21 +274,22 @@
         for held in (high_ref, low_ref):
             term = lax.dot_general(held[...], ref[...], (((0,), (0,)), ((), ())), preferred_element_type=F32)
             part = term if part is None else part + term
-        total[:, h * HALF : (h + 1) * HALF] = part
-    rows = outs[0].shape[0]
+        total[h] = part
+    rows = outs[0].shape[0] // 2
     for mask, out in enumerate(outs):
         start = pl.multiple_of(lax.bitwise_xor(rep_ref[0], mask) * rows, rows)
-        out[...] = total[pl.ds(start, rows), :]
+        for h in range(2):
+            out[h * rows : (h + 1) * rows, :] = total[h, pl.ds(start, rows), :]
 
 
 def local_grad(rep, high, low, masked):
     rows, width = high.shape
     return pl.pallas_call(
         local_kernel,
-        out_shape=[jax.ShapeDtypeStruct((width // 4, width), F32)] * 4,
+        out_shape=[jax.ShapeDtypeStruct((width // 2, HALF), F32)] * 4,
         in_specs=[SMEM] + [VMEM] * 4,
         out_specs=[VMEM] * 4,
-        scratch_shapes=[pltpu.VMEM((width, width), F32)],
+        scratch_shapes=[pltpu.VMEM((2, width, HALF), F32)],
         compiler_params=pltpu.CompilerParams(vmem_limit_bytes=16 << 20),
         cost_estimate=pl.CostEstimate(
             flops=4 * rows * width * width, bytes_accessed=rows * width * 6, transcendentals=0
@@ -293,18 +298,44 @@
     )(rep, high, low, *masked)
 
 
+def round_kernel(n, spot_ref, *refs):
+    held, out_ref, slots = refs[:n], refs[n], refs[n + 1]
+    rows = out_ref.shape[0]
+    for distance, ref in enumerate(held):
+        slots[lax.rem(spot_ref[0] + distance, n)] = ref[ref.shape[0] - rows :, :].astype(F32)
+    total = slots[0]
+    for i in range(1, n):
+        total = total + slots[i]
+    out_ref[...] = total
+
+
+def round_sum(spot, held):
+    n, shape = len(held), held[0].shape
+    return pl.pallas_call(
+        functools.partial(round_kernel, n),
+        out_shape=jax.ShapeDtypeStruct(shape, F32),
+        in_specs=[SMEM] + [VMEM] * n,
+        out_specs=VMEM,
+        scratch_shapes=[pltpu.VMEM((n, *shape), F32)],
+        compiler_params=pltpu.CompilerParams(vmem_limit_bytes=(2 * n + 8) << 17),
+        name="round_sum",
+    )(spot, *held)
+
+
 def whole_kernel(scale, rep_ref, *refs):
-    rows = refs[0].shape[0]
+    rows = refs[0].shape[0] // 2
     for mask in range(4):
         start = pl.multiple_of(lax.bitwise_xor(rep_ref[0], mask) * rows, rows)
-        refs[4][pl.ds(start, rows), :] = refs[mask][...] * scale
+        for h in range(2):
+            part = refs[mask][h * rows : (h + 1) * rows, :] * scale
+            refs[4][pl.ds(start, rows), h * HALF : (h + 1) * HALF] = part
 
 
 def whole_grad(rep, quarters, scale):
-    rows, width = quarters[0].shape
+    size = 2 * quarters[0].shape[0]
     return pl.pallas_call(
         functools.partial(whole_kernel, scale),
-        out_shape=jax.ShapeDtypeStruct((4 * rows, width), F32),
+        out_shape=jax.ShapeDtypeStruct((size, 2 * HALF), F32),
         in_specs=[SMEM] + [VMEM] * 4,
         out_specs=VMEM,
         compiler_params=pltpu.CompilerParams(vmem_limit_bytes=4 << 20),
@@ -313,8 +344,8 @@
 
 
 class GradientSum:
-    def __init__(self, rep, high, low, masked, n, scale):
-        self.rep, self.local, self.n, self.scale = rep, (high, low, masked), n, scale
+    def __init__(self, rep, spot, high, low, masked, n, scale):
+        self.rep, self.spot, self.local, self.n, self.scale = rep, spot, (high, low, masked), n, scale
         self.pairs = [[(i, i ^ mask) for i in range(4)] for mask in range(4)]
 
     def start(self, after):
@@ -322,31 +353,22 @@
         self.quarters = local_grad(self.rep, high, low, masked)
         return self.quarters
 
-    def over_rep(self, after):
+    def riders(self, after):
         value = self.quarters[0]
         for mask in (1, 2, 3):
             value = value + lax.ppermute(self.quarters[mask], "rep", self.pairs[mask])
-        self.value = value
-        return value
-
-    def over_rows(self, strides):
-        value = self.value
-        pairs = [[(i, i ^ step) for i in range(self.n)] for step in range(self.n)]
-        if len(strides) == 2:
-            low, high = strides
-            near = value + lax.ppermute(value, "rows", pairs[low])
-            far = [lax.ppermute(value, "rows", pairs[step]) for step in (high, high + low)]
-            self.value = near + (far[0] + far[1])
-        else:
-            for step in strides:
-                value = value + lax.ppermute(value, "rows", pairs[step])
-            self.value = value
+        self.value = value.astype(BF16)
         return self.value
 
-    def finish(self, after):
-        self.value = tie(self.value, after)
-        others = [lax.ppermute(self.value, "rep", self.pairs[mask]) for mask in (1, 2, 3)]
-        return whole_grad(self.rep, [self.value, *others], self.scale)
+    def finish(self, arrived):
+        held = [self.value] + [None] * (self.n - 1)
+        for hop, (right, left) in enumerate(arrived, 1):
+            held[self.n - hop] = right
+            if left is not None:
+                held[hop] = left
+        value = round_sum(self.spot, held)
+        others = [lax.ppermute(value, "rep", self.pairs[mask]) for mask in (1, 2, 3)]
+        return whole_grad(self.rep, [value, *others], self.scale)
 
 
 def on_device(n, features, weight, block_cols, block_vals, out_grad):
@@ -362,8 +384,9 @@
         my, rep, cols = tie((me.astype(jnp.int32), layer.astype(jnp.int32).reshape(1), block_cols), after)
         cols = cols.reshape(-1)
         back_steps = (ring_place(my, n) - ring_place(cols // own_blocks, n) + n) % n
+        ready["spot"] = ring_place(my, n).reshape(1)
         ready["rep"], ready["where"] = rep, back_steps * own_blocks + cols % own_blocks
-        return ready["rep"], ready["where"], brought_near(vals)
+        return ready["rep"], ready["where"], ready["spot"]
 
     numbers = lambda: (ready["where"], ready["rep"])
     sums, _ = spread(*chunks, n, own_blocks, numbers, vals, SCALE, {"beside": prepared})
@@ -371,11 +394,9 @@
     activated, high, low, *masked = middle(rep, weight, out_grad, sums)
 
     node_total = own_rows * n * 4
-    grad = GradientSum(rep, high, low, masked, n, 1.0 / (SCALE * math.sqrt(node_total)))
-    hooks = {"gather 2": grad.start, "gather 3": grad.over_rep, "gather 4": lambda _: grad.over_rows([1])}
-    hooks["last"] = lambda _: grad.over_rows([1 << i for i in range(1, n.bit_length() - 1)])
-    sums, moving = spread(*masked, n, own_blocks, numbers, vals, None, hooks)
-    weight_grad = grad.finish(moving)
+    grad = GradientSum(rep, ready["spot"], high, low, masked, n, 1.0 / (SCALE * math.sqrt(node_total)))
+    sums, arrived = spread(*masked, n, own_blocks, numbers, vals, None, {"gather 2": grad.start, "riders": grad.riders})
+    weight_grad = grad.finish(arrived)
     input_grad = last(weight, sums)
     return activated, input_grad, weight_grad
 

time: 121 us -> 116 us (0.959)
  starting transfers between devices: 47.5 us -> 44.6 us
  waiting for transfers between devices: 56.4 us -> 54.8 us
    ppermute x10 -> x6, waiting for transfers between devices: 15.2 us -> 3.97 us  [the longest x3 2.5 us: finish(): lax.ppermute(value, 'rep', self.pairs[mask])]
    ppermute x16, waiting for transfers between devices: 12.3 us -> 18.4 us  [spread(): lax.ppermute(pair[1], 'rows', behind)]
    ppermute x10 -> x6, starting transfers between devices: 7.95 us -> 3.87 us  [the longest x3 1.93 us: riders(): value = value + lax.ppermute(self.quarters[mask], 'rep', self.pairs[mask])]
    ppermute x16, starting transfers between devices: 19.5 us -> 23.5 us  [spread(): lax.ppermute(pair[0], 'rows', ahead)]
    ppermute x16, waiting for transfers between devices: 21.9 us -> 25.5 us  [spread(): lax.ppermute(pair[0], 'rows', ahead)]
    ppermute x16, starting transfers between devices: 13.2 us -> 9.89 us  [spread(): lax.ppermute(pair[1], 'rows', behind)]
  transfers between devices with their start and end apart: 52 -> 48, of which waited for: 28 -> 31; matrix products, arithmetic and copies ran while one was open for 2% -> 2% of each run, Pallas kernels for 6% -> 7%
where the time goes in v4:
time: 116 us
  waiting for transfers between devices  54.8 us (47%)
  starting transfers between devices  44.6 us (38%)
  Pallas kernels  10.7 us (9%)
  local copies, waits for them, and re-layouts  3.67 us (3%)
  other arithmetic  1.39 us (1%)
    ppermute x16, waiting for transfers between devices, spread(): lax.ppermute(pair[0], 'rows', ahead)  25.5 us
    ppermute x16, starting transfers between devices, spread(): lax.ppermute(pair[0], 'rows', ahead)  23.5 us
    ppermute x16, waiting for transfers between devices, spread(): lax.ppermute(pair[1], 'rows', behind)  18.4 us
    ppermute x16, starting transfers between devices, spread(): lax.ppermute(pair[1], 'rows', behind)  9.89 us
    ppermute x2, waiting for transfers between devices, spread(): across = lax.ppermute(second, 'rep', pairs[2])  6.83 us
    ppermute x2, starting transfers between devices, spread(): across = lax.ppermute(second, 'rep', pairs[2])  4.14 us
    pallas_call x2, Pallas kernels, scatter_blocks(): pl.pallas_call(functools.partial(scatter_kernel, own_blocks, block, scale...  3.27 us
    pallas_call x2, Pallas kernels, gather_blocks(): pl.pallas_call(functools.partial(gather_kernel, n, own_blocks, block, sca...  3.04 us
  transfers between devices with their start and end apart: 48, of which 31 were waited for; matrix products, arithmetic and copies ran while one was open for 2% of the time, Pallas kernels for 7%

profile of v4, /device:TPU:0, one launch (start us, length us, event | category | flops | bytes accessed | tf_op | source)
XLA Modules:
  0.0 116.3 jit_solution(18044630446389869189)
XLA Ops:
  1.7 3.0 %collective-permute-start.2 = (bf16[1024,128]{1,0:T(8,128)(2,1)S(1)}, bf16[1024,128]{1,0:T(8,128)(2,1)S(1)}, u32[]{:S(2)}, u32[]{:S(2)}) collective-permute-start(bf16[1024,128]{1,0:T(8,128)(2,1)S(1)} %get-tuple-element.86.refs_0_), channel_id=1, source_target_pairs={{0,2},{1,3},{2,0},{3,1},{4,6},{5,7},{6,4},{7,5},{8,10},{9,11},{10,... | collective-permute-start | bytes 786440 | tf_op jit(solution)/shard_map/ppermute | solution.py:146
  7.7 3.3 %collective-permute-done.2.refs_2_ = bf16[1024,128]{1,0:T(8,128)(2,1)S(1)} collective-permute-done((bf16[1024,128]{1,0:T(8,128)(2,1)S(1)}, bf16[1024,128]{1,0:T(8,128)(2,1)S(1)}, u32[]{:S(2)}, u32[]{:S(2)}) %collective-permute-start.2) | collective-permute-done | bytes 262176 | tf_op jit(solution)/shard_map/ppermute | solution.py:146
  15.8 1.6 %copy-done = bf16[32,1,2,128,128]{4,3,2,1,0:T(8,128)(2,1)S(1)} copy-done((bf16[32,1,2,128,128]{4,3,2,1,0:T(8,128)(2,1)S(1)}, bf16[32,1,2,128,128]{4,3,2,1,0:T(8,128)(2,1)}, u32[]{:S(2)}) %copy-start) | copy-done | bytes 2097176
  17.4 1.6 %scatter_blocks.2 = (f32[1024,128]{1,0:T(8,128)S(1)}, f32[8192,128]{1,0:T(8,128)S(1)}) custom-call(s32[64]{0:T(128)S(1)} %fusion.where_ref, s32[1]{0:T(128)} %bitcast.rep_ref, bf16[64,128,128]{2,1,0:T(8,128)(2,1)S(1)} %bitcast.5, bf16[1024,128]{1,0:T(8,128)(2,1)S(1)} %get-tuple-element.86.refs_0_, bf16[1024,128]{1,0:T(8,128)(2,1)S(1)} %collective-permute-done.5.refs_1_, ...), custom_call_target="tpu_custom_call" | custom-call | flops 268435456 | bytes 7864320 | tf_op jit(solution)/shard_map/scatter_blocks/pallas_call | solution.py:108
  21.4 2.0 %collective-permute-done.4.refs_7_ = bf16[1024,128]{1,0:T(8,128)(2,1)S(1)} collective-permute-done((bf16[1024,128]{1,0:T(8,128)(2,1)S(1)}, bf16[1024,128]{1,0:T(8,128)(2,1)S(1)}, u32[]{:S(2)}, u32[]{:S(2)}) %collective-permute-start.4) | collective-permute-done | bytes 262176 | tf_op jit(solution)/shard_map/ppermute | solution.py:144
  26.4 1.6 %collective-permute-start.13 = (bf16[1024,128]{1,0:T(8,128)(2,1)S(1)}, bf16[1024,128]{1,0:T(8,128)(2,1)S(1)}, u32[]{:S(2)}, u32[]{:S(2)}) collective-permute-start(bf16[1024,128]{1,0:T(8,128)(2,1)S(1)} %get-tuple-element.93), channel_id=1, source_target_pairs={{0,8},{8,16},{16,24},{24,28},{28,20},{20,12},{12,4},{4,0},{1,9},{9... | collective-permute-start | bytes 786440 | tf_op jit(solution)/shard_map/ppermute | solution.py:144
  28.4 4.2 %collective-permute-done.7.refs_3_ = bf16[1024,128]{1,0:T(8,128)(2,1)S(1)} collective-permute-done((bf16[1024,128]{1,0:T(8,128)(2,1)S(1)}, bf16[1024,128]{1,0:T(8,128)(2,1)S(1)}, u32[]{:S(2)}, u32[]{:S(2)}) %collective-permute-start.7) | collective-permute-done | bytes 262176 | tf_op jit(solution)/shard_map/ppermute | solution.py:144
  41.4 1.7 %gather_blocks.2 = (bf16[2048,128]{1,0:T(8,128)(2,1)S(1)}, f32[1024,128]{1,0:T(8,128)S(1)}, f32[1024,128]{1,0:T(8,128)S(1)}) custom-call(s32[64]{0:T(128)S(1)} %fusion.where_ref, s32[1]{0:T(128)} %bitcast.rep_ref, bf16[64,128,128]{2,1,0:T(8,128)(2,1)S(1)} %bitcast.6, bf16[1024,128]{1,0:T(8,128)(2,1)S(1)} %get-tuple-element.99.refs_0_, ...), custom_call_target="tpu_custom_call" | custom-call | flops 26843545600 | bytes 7864320 | tf_op jit(solution)/shard_map/gather_blocks/pallas_call | solution.py:71
  48.8 4.7 %collective-permute-done.19.refs_4_ = bf16[1024,128]{1,0:T(8,128)(2,1)S(1)} collective-permute-done((bf16[1024,128]{1,0:T(8,128)(2,1)S(1)}, bf16[1024,128]{1,0:T(8,128)(2,1)S(1)}, u32[]{:S(2)}, u32[]{:S(2)}) %collective-permute-start.19) | collective-permute-done | bytes 262176 | tf_op jit(solution)/shard_map/ppermute | solution.py:144
  57.7 1.7 %collective-permute-start.21 = (bf16[1024,128]{1,0:T(8,128)(2,1)S(1)}, bf16[1024,128]{1,0:T(8,128)(2,1)S(1)}, u32[]{:S(2)}, u32[]{:S(2)}) collective-permute-start(bf16[1024,128]{1,0:T(8,128)(2,1)S(1)} %get-tuple-element.142.refs_0_), channel_id=1, source_target_pairs={{0,8},{8,16},{16,24},{24,28},{28,20},{20,12},{12,4},{4,0},{1,9},{9... | collective-permute-start | bytes 786440 | tf_op jit(solution)/shard_map/ppermute | solution.py:144
  59.7 3.5 %collective-permute-done.23.refs_2_ = bf16[1024,128]{1,0:T(8,128)(2,1)S(1)} collective-permute-done((bf16[1024,128]{1,0:T(8,128)(2,1)S(1)}, bf16[1024,128]{1,0:T(8,128)(2,1)S(1)}, u32[]{:S(2)}, u32[]{:S(2)}) %collective-permute-start.23) | collective-permute-done | bytes 262176 | tf_op jit(solution)/shard_map/ppermute | solution.py:146
  69.7 1.6 %scatter_blocks.3 = (f32[1024,128]{1,0:T(8,128)S(1)}, f32[8192,128]{1,0:T(8,128)S(1)}) custom-call(s32[64]{0:T(128)S(1)} %fusion.where_ref, s32[1]{0:T(128)} %bitcast.rep_ref, bf16[64,128,128]{2,1,0:T(8,128)(2,1)S(1)} %bitcast.7, bf16[1024,128]{1,0:T(8,128)(2,1)S(1)} %get-tuple-element.129.refs_1_.refs_0_, ...), custom_call_target="tpu_custom_call" | custom-call | flops 268435456 | bytes 7864320 | tf_op jit(solution)/shard_map/scatter_blocks/pallas_call | solution.py:108
  73.7 1.8 %collective-permute-done.24.refs_2_ = bf16[1024,128]{1,0:T(8,128)(2,1)S(1)} collective-permute-done((bf16[1024,128]{1,0:T(8,128)(2,1)S(1)}, bf16[1024,128]{1,0:T(8,128)(2,1)S(1)}, u32[]{:S(2)}, u32[]{:S(2)}) %collective-permute-start.24) | collective-permute-done | bytes 262176 | tf_op jit(solution)/shard_map/ppermute | solution.py:144
  75.6 1.7 %collective-permute-done.25.refs_7_ = bf16[1024,128]{1,0:T(8,128)(2,1)S(1)} collective-permute-done((bf16[1024,128]{1,0:T(8,128)(2,1)S(1)}, bf16[1024,128]{1,0:T(8,128)(2,1)S(1)}, u32[]{:S(2)}, u32[]{:S(2)}) %collective-permute-start.25) | collective-permute-done | bytes 262176 | tf_op jit(solution)/shard_map/ppermute | solution.py:144
  77.3 2.4 %collective-permute-start.31 = (bf16[1152,128]{1,0:T(8,128)(2,1)S(1)}, bf16[1152,128]{1,0:T(8,128)(2,1)S(1)}, u32[]{:S(2)}, u32[]{:S(2)}) collective-permute-start(bf16[1152,128]{1,0:T(8,128)(2,1)S(1)} %get-tuple-element.180), channel_id=1, source_target_pairs={{0,8},{8,16},{16,24},{24,28},{28,20},{20,12},{12,4},{4,0},{1,9},{9... | collective-permute-start | bytes 884744 | tf_op jit(solution)/shard_map/ppermute | solution.py:144
  81.0 2.3 %collective-permute-start.37 = (bf16[1152,128]{1,0:T(8,128)(2,1)S(1)}, bf16[1152,128]{1,0:T(8,128)(2,1)S(1)}, u32[]{:S(2)}, u32[]{:S(2)}) collective-permute-start(bf16[1152,128]{1,0:T(8,128)(2,1)S(1)} %pad_maximum_fusion.2), channel_id=1, source_target_pairs={{0,8},{8,16},{16,24},{24,28},{28,20},{20,12},{12,4},{4,0},{1,9},{9... | collective-permute-start | bytes 884744 | tf_op jit(solution)/shard_map/ppermute | solution.py:144
  83.4 3.9 %collective-permute-done.31.refs_3_ = bf16[1152,128]{1,0:T(8,128)(2,1)S(1)} collective-permute-done((bf16[1152,128]{1,0:T(8,128)(2,1)S(1)}, bf16[1152,128]{1,0:T(8,128)(2,1)S(1)}, u32[]{:S(2)}, u32[]{:S(2)}) %collective-permute-start.31) | collective-permute-done | bytes 294944 | tf_op jit(solution)/shard_map/ppermute | solution.py:144
  87.3 2.3 %collective-permute-done.32.refs_6_ = bf16[1152,128]{1,0:T(8,128)(2,1)S(1)} collective-permute-done((bf16[1152,128]{1,0:T(8,128)(2,1)S(1)}, bf16[1152,128]{1,0:T(8,128)(2,1)S(1)}, u32[]{:S(2)}, u32[]{:S(2)}) %collective-permute-start.32) | collective-permute-done | bytes 294944 | tf_op jit(solution)/shard_map/ppermute | solution.py:144
  89.8 2.0 %collective-permute-start.36 = (bf16[512,128]{1,0:T(8,128)(2,1)S(1)}, bf16[512,128]{1,0:T(8,128)(2,1)S(1)}, u32[]{:S(2)}, u32[]{:S(2)}) collective-permute-start(bf16[512,128]{1,0:T(8,128)(2,1)S(1)} %slice.171), channel_id=1, source_target_pairs={{8,0},{16,8},{24,16},{28,24},{20,28},{12,20},{4,12},{0,4},{9,1},{1... | collective-permute-start | bytes 393224 | tf_op jit(solution)/shard_map/ppermute | solution.py:144
  91.7 2.3 %collective-permute-done.38.refs_2_ = bf16[1152,128]{1,0:T(8,128)(2,1)S(1)} collective-permute-done((bf16[1152,128]{1,0:T(8,128)(2,1)S(1)}, bf16[1152,128]{1,0:T(8,128)(2,1)S(1)}, u32[]{:S(2)}, u32[]{:S(2)}) %collective-permute-start.38) | collective-permute-done | bytes 294944 | tf_op jit(solution)/shard_map/ppermute | solution.py:144
  94.2 1.8 %collective-permute-start.41 = (bf16[1152,128]{1,0:T(8,128)(2,1)S(1)}, bf16[1152,128]{1,0:T(8,128)(2,1)S(1)}, u32[]{:S(2)}, u32[]{:S(2)}) collective-permute-start(bf16[1152,128]{1,0:T(8,128)(2,1)S(1)} %pad_maximum_fusion.4), channel_id=1, source_target_pairs={{0,8},{8,16},{16,24},{24,28},{28,20},{20,12},{12,4},{4,0},{1,9},{9... | collective-permute-start | bytes 884744 | tf_op jit(solution)/shard_map/ppermute | solution.py:144
  97.8 3.2 %collective-permute-done.41.refs_5_ = bf16[1152,128]{1,0:T(8,128)(2,1)S(1)} collective-permute-done((bf16[1152,128]{1,0:T(8,128)(2,1)S(1)}, bf16[1152,128]{1,0:T(8,128)(2,1)S(1)}, u32[]{:S(2)}, u32[]{:S(2)}) %collective-permute-start.41) | collective-permute-done | bytes 294944 | tf_op jit(solution)/shard_map/ppermute | solution.py:144
  101.0 1.7 %collective-permute-done.42.refs_3_ = bf16[1152,128]{1,0:T(8,128)(2,1)S(1)} collective-permute-done((bf16[1152,128]{1,0:T(8,128)(2,1)S(1)}, bf16[1152,128]{1,0:T(8,128)(2,1)S(1)}, u32[]{:S(2)}, u32[]{:S(2)}) %collective-permute-start.42) | collective-permute-done | bytes 294944 | tf_op jit(solution)/shard_map/ppermute | solution.py:144
  106.4 3.3 %collective-permute-done.43.refs_4_ = bf16[1152,128]{1,0:T(8,128)(2,1)S(1)} collective-permute-done((bf16[1152,128]{1,0:T(8,128)(2,1)S(1)}, bf16[1152,128]{1,0:T(8,128)(2,1)S(1)}, u32[]{:S(2)}, u32[]{:S(2)}) %collective-permute-start.43) | collective-permute-done | bytes 294944 | tf_op jit(solution)/shard_map/ppermute | solution.py:144
  (123 shorter events, 55.9 us)
Async XLA Ops:
  1.7 9.3 %collective-permute-start.2 = (bf16[1024,128]{1,0:T(8,128)(2,1)S(1)}, bf16[1024,128]{1,0:T(8,128)(2,1)S(1)}, u32[]{:S(2)}, u32[]{:S(2)}) collective-permute-start(bf16[1024,128]{1,0:T(8,128)(2,1)S(1)} %get-tuple-element.86.refs_0_), channel_id=1, source_target_pairs={{0,2},{1,3},{2,0},{3,1},{4,6},{5,7},{6,4},{7,5},{8,10},{9,11},{10,... | collective-permute-start | bytes 786440 | tf_op jit(solution)/shard_map/ppermute | solution.py:146
  4.7 7.8 %collective-permute-start = (bf16[1024,128]{1,0:T(8,128)(2,1)S(1)}, bf16[1024,128]{1,0:T(8,128)(2,1)S(1)}, u32[]{:S(2)}, u32[]{:S(2)}) collective-permute-start(bf16[1024,128]{1,0:T(8,128)(2,1)S(1)} %get-tuple-element.99.refs_0_), channel_id=1, source_target_pairs={{0,8},{8,16},{16,24},{24,28},{28,20},{20,12},{12,4},{4,0},{1,9},{9... | collective-permute-start | bytes 786440 | tf_op jit(solution)/shard_map/ppermute | solution.py:144
  6.3 7.5 %collective-permute-start.1 = (bf16[1024,128]{1,0:T(8,128)(2,1)S(1)}, bf16[1024,128]{1,0:T(8,128)(2,1)S(1)}, u32[]{:S(2)}, u32[]{:S(2)}) collective-permute-start(bf16[1024,128]{1,0:T(8,128)(2,1)S(1)} %get-tuple-element.99.refs_0_), channel_id=1, source_target_pairs={{8,0},{16,8},{24,16},{28,24},{20,28},{12,20},{4,12},{0,4},{9,1},{1... | collective-permute-start | bytes 786440 | tf_op jit(solution)/shard_map/ppermute | solution.py:144
  7.6 8.2 %collective-permute-start.5 = (bf16[1024,128]{1,0:T(8,128)(2,1)S(1)}, bf16[1024,128]{1,0:T(8,128)(2,1)S(1)}, u32[]{:S(2)}, u32[]{:S(2)}) collective-permute-start(bf16[1024,128]{1,0:T(8,128)(2,1)S(1)} %get-tuple-element.86.refs_0_), channel_id=1, source_target_pairs={{0,1},{1,0},{2,3},{3,2},{4,5},{5,4},{6,7},{7,6},{8,9},{9,8},{10,11... | collective-permute-start | bytes 786440 | tf_op jit(solution)/shard_map/ppermute | solution.py:147
  13.8 7.6 %collective-permute-start.3 = (bf16[1024,128]{1,0:T(8,128)(2,1)S(1)}, bf16[1024,128]{1,0:T(8,128)(2,1)S(1)}, u32[]{:S(2)}, u32[]{:S(2)}) collective-permute-start(bf16[1024,128]{1,0:T(8,128)(2,1)S(1)} %collective-permute-done.refs_1_), channel_id=1, source_target_pairs={{0,8},{8,16},{16,24},{24,28},{28,20},{20,12},{12,4},{4,0},{1,9},{9... | collective-permute-start | bytes 786440 | tf_op jit(solution)/shard_map/ppermute | solution.py:144
  15.3 8.0 %collective-permute-start.4 = (bf16[1024,128]{1,0:T(8,128)(2,1)S(1)}, bf16[1024,128]{1,0:T(8,128)(2,1)S(1)}, u32[]{:S(2)}, u32[]{:S(2)}) collective-permute-start(bf16[1024,128]{1,0:T(8,128)(2,1)S(1)} %collective-permute-done.1.refs_8_), channel_id=1, source_target_pairs={{8,0},{16,8},{24,16},{28,24},{20,28},{12,20},{4,12},{0,4},{9,1},{1... | collective-permute-start | bytes 786440 | tf_op jit(solution)/shard_map/ppermute | solution.py:144
  23.4 9.2 %collective-permute-start.7 = (bf16[1024,128]{1,0:T(8,128)(2,1)S(1)}, bf16[1024,128]{1,0:T(8,128)(2,1)S(1)}, u32[]{:S(2)}, u32[]{:S(2)}) collective-permute-start(bf16[1024,128]{1,0:T(8,128)(2,1)S(1)} %collective-permute-done.3.refs_2_), channel_id=1, source_target_pairs={{0,8},{8,16},{16,24},{24,28},{28,20},{20,12},{12,4},{4,0},{1,9},{9... | collective-permute-start | bytes 786440 | tf_op jit(solution)/shard_map/ppermute | solution.py:144
  24.9 9.2 %collective-permute-start.8 = (bf16[1024,128]{1,0:T(8,128)(2,1)S(1)}, bf16[1024,128]{1,0:T(8,128)(2,1)S(1)}, u32[]{:S(2)}, u32[]{:S(2)}) collective-permute-start(bf16[1024,128]{1,0:T(8,128)(2,1)S(1)} %collective-permute-done.4.refs_7_), channel_id=1, source_target_pairs={{8,0},{16,8},{24,16},{28,24},{20,28},{12,20},{4,12},{0,4},{9,1},{1... | collective-permute-start | bytes 786440 | tf_op jit(solution)/shard_map/ppermute | solution.py:144
  26.4 11.1 %collective-permute-start.13 = (bf16[1024,128]{1,0:T(8,128)(2,1)S(1)}, bf16[1024,128]{1,0:T(8,128)(2,1)S(1)}, u32[]{:S(2)}, u32[]{:S(2)}) collective-permute-start(bf16[1024,128]{1,0:T(8,128)(2,1)S(1)} %get-tuple-element.93), channel_id=1, source_target_pairs={{0,8},{8,16},{16,24},{24,28},{28,20},{20,12},{12,4},{4,0},{1,9},{9... | collective-permute-start | bytes 786440 | tf_op jit(solution)/shard_map/ppermute | solution.py:144
  28.0 10.0 %collective-permute-start.14 = (bf16[1024,128]{1,0:T(8,128)(2,1)S(1)}, bf16[1024,128]{1,0:T(8,128)(2,1)S(1)}, u32[]{:S(2)}, u32[]{:S(2)}) collective-permute-start(bf16[1024,128]{1,0:T(8,128)(2,1)S(1)} %get-tuple-element.94), channel_id=1, source_target_pairs={{8,0},{16,8},{24,16},{28,24},{20,28},{12,20},{4,12},{0,4},{9,1},{1... | collective-permute-start | bytes 786440 | tf_op jit(solution)/shard_map/ppermute | solution.py:144
  45.6 7.9 %collective-permute-start.19 = (bf16[1024,128]{1,0:T(8,128)(2,1)S(1)}, bf16[1024,128]{1,0:T(8,128)(2,1)S(1)}, u32[]{:S(2)}, u32[]{:S(2)}) collective-permute-start(bf16[1024,128]{1,0:T(8,128)(2,1)S(1)} %get-tuple-element.112), channel_id=1, source_target_pairs={{0,8},{8,16},{16,24},{24,28},{28,20},{20,12},{12,4},{4,0},{1,9},{9... | collective-permute-start | bytes 786440 | tf_op jit(solution)/shard_map/ppermute | solution.py:144
  47.1 7.7 %collective-permute-start.20 = (bf16[1024,128]{1,0:T(8,128)(2,1)S(1)}, bf16[1024,128]{1,0:T(8,128)(2,1)S(1)}, u32[]{:S(2)}, u32[]{:S(2)}) collective-permute-start(bf16[1024,128]{1,0:T(8,128)(2,1)S(1)} %get-tuple-element.113), channel_id=1, source_target_pairs={{8,0},{16,8},{24,16},{28,24},{20,28},{12,20},{4,12},{0,4},{9,1},{1... | collective-permute-start | bytes 786440 | tf_op jit(solution)/shard_map/ppermute | solution.py:144
  47.7 7.3 %collective-permute-start.16 = (bf16[1024,128]{1,0:T(8,128)(2,1)S(1)}, bf16[1024,128]{1,0:T(8,128)(2,1)S(1)}, u32[]{:S(2)}, u32[]{:S(2)}) collective-permute-start(bf16[1024,128]{1,0:T(8,128)(2,1)S(1)} %add_convert_fusion.7), channel_id=1, source_target_pairs={{0,2},{1,3},{2,0},{3,1},{4,6},{5,7},{6,4},{7,5},{8,10},{9,11},{10,... | collective-permute-start | bytes 786440 | tf_op jit(solution)/shard_map/ppermute | solution.py:197
  57.7 8.3 %collective-permute-start.21 = (bf16[1024,128]{1,0:T(8,128)(2,1)S(1)}, bf16[1024,128]{1,0:T(8,128)(2,1)S(1)}, u32[]{:S(2)}, u32[]{:S(2)}) collective-permute-start(bf16[1024,128]{1,0:T(8,128)(2,1)S(1)} %get-tuple-element.142.refs_0_), channel_id=1, source_target_pairs={{0,8},{8,16},{16,24},{24,28},{28,20},{20,12},{12,4},{4,0},{1,9},{9... | collective-permute-start | bytes 786440 | tf_op jit(solution)/shard_map/ppermute | solution.py:144
  59.4 6.9 %collective-permute-start.22 = (bf16[1024,128]{1,0:T(8,128)(2,1)S(1)}, bf16[1024,128]{1,0:T(8,128)(2,1)S(1)}, u32[]{:S(2)}, u32[]{:S(2)}) collective-permute-start(bf16[1024,128]{1,0:T(8,128)(2,1)S(1)} %get-tuple-element.142.refs_0_), channel_id=1, source_target_pairs={{8,0},{16,8},{24,16},{28,24},{20,28},{12,20},{4,12},{0,4},{9,1},{1... | collective-permute-start | bytes 786440 | tf_op jit(solution)/shard_map/ppermute | solution.py:144
  66.5 9.1 %collective-permute-start.24 = (bf16[1024,128]{1,0:T(8,128)(2,1)S(1)}, bf16[1024,128]{1,0:T(8,128)(2,1)S(1)}, u32[]{:S(2)}, u32[]{:S(2)}) collective-permute-start(bf16[1024,128]{1,0:T(8,128)(2,1)S(1)} %collective-permute-done.21.refs_1_), channel_id=1, source_target_pairs={{0,8},{8,16},{16,24},{24,28},{28,20},{20,12},{12,4},{4,0},{1,9},{9... | collective-permute-start | bytes 786440 | tf_op jit(solution)/shard_map/ppermute | solution.py:144
  68.9 8.4 %collective-permute-start.25 = (bf16[1024,128]{1,0:T(8,128)(2,1)S(1)}, bf16[1024,128]{1,0:T(8,128)(2,1)S(1)}, u32[]{:S(2)}, u32[]{:S(2)}) collective-permute-start(bf16[1024,128]{1,0:T(8,128)(2,1)S(1)} %collective-permute-done.22.refs_8_), channel_id=1, source_target_pairs={{8,0},{16,8},{24,16},{28,24},{20,28},{12,20},{4,12},{0,4},{9,1},{1... | collective-permute-start | bytes 786440 | tf_op jit(solution)/shard_map/ppermute | solution.py:144
  71.7 9.1 %collective-permute-start.33 = (bf16[640,128]{1,0:T(8,128)(2,1)S(1)}, bf16[640,128]{1,0:T(8,128)(2,1)S(1)}, u32[]{:S(2)}, u32[]{:S(2)}) collective-permute-start(bf16[640,128]{1,0:T(8,128)(2,1)S(1)} %get-tuple-element.182), channel_id=1, source_target_pairs={{0,8},{8,16},{16,24},{24,28},{28,20},{20,12},{12,4},{4,0},{1,9},{9... | collective-permute-start | bytes 491528 | tf_op jit(solution)/shard_map/ppermute | solution.py:144
  73.2 7.6 %collective-permute-start.34 = (bf16[640,128]{1,0:T(8,128)(2,1)S(1)}, bf16[640,128]{1,0:T(8,128)(2,1)S(1)}, u32[]{:S(2)}, u32[]{:S(2)}) collective-permute-start(bf16[640,128]{1,0:T(8,128)(2,1)S(1)} %get-tuple-element.181), channel_id=1, source_target_pairs={{8,0},{16,8},{24,16},{28,24},{20,28},{12,20},{4,12},{0,4},{9,1},{1... | collective-permute-start | bytes 491528 | tf_op jit(solution)/shard_map/ppermute | solution.py:144
  77.3 10.0 %collective-permute-start.31 = (bf16[1152,128]{1,0:T(8,128)(2,1)S(1)}, bf16[1152,128]{1,0:T(8,128)(2,1)S(1)}, u32[]{:S(2)}, u32[]{:S(2)}) collective-permute-start(bf16[1152,128]{1,0:T(8,128)(2,1)S(1)} %get-tuple-element.180), channel_id=1, source_target_pairs={{0,8},{8,16},{16,24},{24,28},{28,20},{20,12},{12,4},{4,0},{1,9},{9... | collective-permute-start | bytes 884744 | tf_op jit(solution)/shard_map/ppermute | solution.py:144
  79.7 9.9 %collective-permute-start.32 = (bf16[1152,128]{1,0:T(8,128)(2,1)S(1)}, bf16[1152,128]{1,0:T(8,128)(2,1)S(1)}, u32[]{:S(2)}, u32[]{:S(2)}) collective-permute-start(bf16[1152,128]{1,0:T(8,128)(2,1)S(1)} %get-tuple-element.179), channel_id=1, source_target_pairs={{8,0},{16,8},{24,16},{28,24},{20,28},{12,20},{4,12},{0,4},{9,1},{1... | collective-permute-start | bytes 884744 | tf_op jit(solution)/shard_map/ppermute | solution.py:144
  80.9 13.1 %collective-permute-start.38 = (bf16[1152,128]{1,0:T(8,128)(2,1)S(1)}, bf16[1152,128]{1,0:T(8,128)(2,1)S(1)}, u32[]{:S(2)}, u32[]{:S(2)}) collective-permute-start(bf16[1152,128]{1,0:T(8,128)(2,1)S(1)} %pad_maximum_fusion.3), channel_id=1, source_target_pairs={{8,0},{16,8},{24,16},{28,24},{20,28},{12,20},{4,12},{0,4},{9,1},{1... | collective-permute-start | bytes 884744 | tf_op jit(solution)/shard_map/ppermute | solution.py:144
  81.0 13.0 %collective-permute-start.37 = (bf16[1152,128]{1,0:T(8,128)(2,1)S(1)}, bf16[1152,128]{1,0:T(8,128)(2,1)S(1)}, u32[]{:S(2)}, u32[]{:S(2)}) collective-permute-start(bf16[1152,128]{1,0:T(8,128)(2,1)S(1)} %pad_maximum_fusion.2), channel_id=1, source_target_pairs={{0,8},{8,16},{16,24},{24,28},{28,20},{20,12},{12,4},{4,0},{1,9},{9... | collective-permute-start | bytes 884744 | tf_op jit(solution)/shard_map/ppermute | solution.py:144
  103.5 8.2 %collective-permute-start.44 = (bf16[1024,128]{1,0:T(8,128)(2,1)S(1)}, bf16[1024,128]{1,0:T(8,128)(2,1)S(1)}, u32[]{:S(2)}, u32[]{:S(2)}) collective-permute-start(bf16[1024,128]{1,0:T(8,128)(2,1)S(1)} %get-tuple-element.156), channel_id=1, source_target_pairs={{8,0},{16,8},{24,16},{28,24},{20,28},{12,20},{4,12},{0,4},{9,1},{1... | collective-permute-start | bytes 786440 | tf_op jit(solution)/shard_map/ppermute | solution.py:144
  (28 other events, 180.8 us)

commit v5 on v4

--- a/solution.py
+++ b/solution.py
@@ -118,6 +118,24 @@
     )(where, rep, vals, *sources)
 
 
+def near_kernel(vals_ref, out_ref, sem):
+    copy = pltpu.make_async_copy(vals_ref, out_ref, sem)
+    copy.start()
+    copy.wait()
+
+
+def brought_near(vals):
+    return pl.pallas_call(
+        near_kernel,
+        out_shape=jax.ShapeDtypeStruct(vals.shape, vals.dtype),
+        in_specs=[pl.BlockSpec(memory_space=pl.ANY)],
+        out_specs=VMEM,
+        scratch_shapes=[pltpu.SemaphoreType.DMA],
+        compiler_params=pltpu.CompilerParams(vmem_limit_bytes=4 << 20),
+        name="brought_near",
+    )(vals)
+
+
 def add_terms(pair, terms, sent, riders):
     rows = terms[0].shape[0]
     mid = rows // 2
@@ -134,7 +152,7 @@
     )
 
 
-def spread(first, second, n, own_blocks, numbers, vals, scale, hooks):
+def spread(first, second, n, own_blocks, numbers, scale, hooks):
     ahead, behind = ring_ways(n)
     rows, half = first.shape[0], n // 2
     mid = rows // 2
@@ -163,7 +181,7 @@
         gathered = step(gathered)
         pieces[hop], pieces[n + 1 - hop] = gathered
         if hop == 2:
-            where, rep = numbers()
+            where, rep, vals = numbers()
             sources = tie([second, beside, across, far], behind_it)
             own, partial = scatter_blocks(where, rep, vals, sources, n, own_blocks, scale)
             term = lambda distance: partial[distance * rows : (distance + 1) * rows]
@@ -386,16 +404,17 @@
         back_steps = (ring_place(my, n) - ring_place(cols // own_blocks, n) + n) % n
         ready["spot"] = ring_place(my, n).reshape(1)
         ready["rep"], ready["where"] = rep, back_steps * own_blocks + cols % own_blocks
-        return ready["rep"], ready["where"], ready["spot"]
-
-    numbers = lambda: (ready["where"], ready["rep"])
-    sums, _ = spread(*chunks, n, own_blocks, numbers, vals, SCALE, {"beside": prepared})
+        ready["vals"] = brought_near(vals)
+        return ready["rep"], ready["where"], ready["spot"], ready["vals"]
+
+    numbers = lambda: (ready["where"], ready["rep"], ready["vals"])
+    sums, _ = spread(*chunks, n, own_blocks, numbers, SCALE, {"beside": prepared})
     rep = ready["rep"]
     activated, high, low, *masked = middle(rep, weight, out_grad, sums)
 
     node_total = own_rows * n * 4
     grad = GradientSum(rep, ready["spot"], high, low, masked, n, 1.0 / (SCALE * math.sqrt(node_total)))
-    sums, arrived = spread(*masked, n, own_blocks, numbers, vals, None, {"gather 2": grad.start, "riders": grad.riders})
+    sums, arrived = spread(*masked, n, own_blocks, numbers, None, {"gather 2": grad.start, "riders": grad.riders})
     weight_grad = grad.finish(arrived)
     input_grad = last(weight, sums)
     return activated, input_grad, weight_grad

time: 116 us -> 116 us (level)
    ppermute x16, starting transfers between devices: 9.89 us -> 7.69 us  [spread(): lax.ppermute(pair[1], 'rows', behind)]
    ppermute x16, waiting for transfers between devices: 18.4 us -> 20.6 us  [spread(): lax.ppermute(pair[1], 'rows', behind)]
    ppermute x2, waiting for transfers between devices: 6.83 us -> 4.73 us  [spread(): across = lax.ppermute(second, 'rep', pairs[2])]
    ppermute x16, starting transfers between devices: 23.5 us -> 25.5 us  [spread(): lax.ppermute(pair[0], 'rows', ahead)]
where the time goes in v5:
time: 116 us
  waiting for transfers between devices  55.2 us (48%)
  starting transfers between devices  43.9 us (38%)
  Pallas kernels  10.8 us (9%)
  local copies, waits for them, and re-layouts  3.66 us (3%)
  other arithmetic  1.34 us (1%)
    ppermute x16, waiting for transfers between devices, spread(): lax.ppermute(pair[0], 'rows', ahead)  26.2 us
    ppermute x16, starting transfers between devices, spread(): lax.ppermute(pair[0], 'rows', ahead)  25.5 us
    ppermute x16, waiting for transfers between devices, spread(): lax.ppermute(pair[1], 'rows', behind)  20.6 us
    ppermute x16, starting transfers between devices, spread(): lax.ppermute(pair[1], 'rows', behind)  7.69 us
    ppermute x2, waiting for transfers between devices, spread(): across = lax.ppermute(second, 'rep', pairs[2])  4.73 us
    ppermute x2, starting transfers between devices, spread(): across = lax.ppermute(second, 'rep', pairs[2])  4.22 us
    pallas_call x2, Pallas kernels, scatter_blocks(): pl.pallas_call(functools.partial(scatter_kernel, own_blocks, block, scale...  3.27 us
    pallas_call x2, Pallas kernels, gather_blocks(): pl.pallas_call(functools.partial(gather_kernel, n, own_blocks, block, sca...  3.04 us
  transfers between devices with their start and end apart: 48, of which 31 were waited for; matrix products, arithmetic and copies ran while one was open for 2% of the time, Pallas kernels for 7%

profile of v5, /device:TPU:0, one launch (start us, length us, event | category | flops | bytes accessed | tf_op | source)
XLA Modules:
  0.0 115.9 jit_solution(16520923562146359918)
XLA Ops:
  1.7 3.0 %collective-permute-start.2 = (bf16[1024,128]{1,0:T(8,128)(2,1)S(1)}, bf16[1024,128]{1,0:T(8,128)(2,1)S(1)}, u32[]{:S(2)}, u32[]{:S(2)}) collective-permute-start(bf16[1024,128]{1,0:T(8,128)(2,1)S(1)} %get-tuple-element.86.refs_0_), channel_id=1, source_target_pairs={{0,2},{1,3},{2,0},{3,1},{4,6},{5,7},{6,4},{7,5},{8,10},{9,11},{10,... | collective-permute-start | bytes 786440 | tf_op jit(solution)/shard_map/ppermute | solution.py:164
  15.8 1.6 %scatter_blocks.2 = (f32[1024,128]{1,0:T(8,128)S(1)}, f32[8192,128]{1,0:T(8,128)S(1)}) custom-call(s32[64]{0:T(128)S(1)} %fusion.where_ref, s32[1]{0:T(128)} %bitcast.rep_ref, bf16[64,128,128]{2,1,0:T(8,128)(2,1)S(1)} %brought_near.1.vals_ref, bf16[1024,128]{1,0:T(8,128)(2,1)S(1)} %get-tuple-element.86.refs_0_, ...), custom_call_target="tpu_custom_call" | custom-call | flops 268435456 | bytes 7864320 | tf_op jit(solution)/shard_map/scatter_blocks/pallas_call | solution.py:108
  19.8 1.8 %collective-permute-done.3.refs_2_ = bf16[1024,128]{1,0:T(8,128)(2,1)S(1)} collective-permute-done((bf16[1024,128]{1,0:T(8,128)(2,1)S(1)}, bf16[1024,128]{1,0:T(8,128)(2,1)S(1)}, u32[]{:S(2)}, u32[]{:S(2)}) %collective-permute-start.3) | collective-permute-done | bytes 262176 | tf_op jit(solution)/shard_map/ppermute | solution.py:162
  21.5 1.6 %collective-permute-done.4.refs_7_ = bf16[1024,128]{1,0:T(8,128)(2,1)S(1)} collective-permute-done((bf16[1024,128]{1,0:T(8,128)(2,1)S(1)}, bf16[1024,128]{1,0:T(8,128)(2,1)S(1)}, u32[]{:S(2)}, u32[]{:S(2)}) %collective-permute-start.4) | collective-permute-done | bytes 262176 | tf_op jit(solution)/shard_map/ppermute | solution.py:162
  28.2 4.2 %collective-permute-done.7.refs_3_ = bf16[1024,128]{1,0:T(8,128)(2,1)S(1)} collective-permute-done((bf16[1024,128]{1,0:T(8,128)(2,1)S(1)}, bf16[1024,128]{1,0:T(8,128)(2,1)S(1)}, u32[]{:S(2)}, u32[]{:S(2)}) %collective-permute-start.7) | collective-permute-done | bytes 262176 | tf_op jit(solution)/shard_map/ppermute | solution.py:162
  38.1 1.6 %collective-permute-start.17 = (bf16[1024,128]{1,0:T(8,128)(2,1)S(1)}, bf16[1024,128]{1,0:T(8,128)(2,1)S(1)}, u32[]{:S(2)}, u32[]{:S(2)}) collective-permute-start(bf16[1024,128]{1,0:T(8,128)(2,1)S(1)} %get-tuple-element.97), channel_id=1, source_target_pairs={{0,8},{8,16},{16,24},{24,28},{28,20},{20,12},{12,4},{4,0},{1,9},{9... | collective-permute-start | bytes 786440 | tf_op jit(solution)/shard_map/ppermute | solution.py:162
  41.3 1.7 %gather_blocks.2 = (bf16[2048,128]{1,0:T(8,128)(2,1)S(1)}, f32[1024,128]{1,0:T(8,128)S(1)}, f32[1024,128]{1,0:T(8,128)S(1)}) custom-call(s32[64]{0:T(128)S(1)} %fusion.where_ref, s32[1]{0:T(128)} %bitcast.rep_ref, bf16[64,128,128]{2,1,0:T(8,128)(2,1)S(1)} %brought_near.1.vals_ref, bf16[1024,128]{1,0:T(8,128)(2,1)S(1)} %get-tuple-element.99.refs_0_, ...), custom_call_target="tpu_custom_call" | custom-call | flops 26843545600 | bytes 7864320 | tf_op jit(solution)/shard_map/gather_blocks/pallas_call | solution.py:71
  48.6 4.8 %collective-permute-done.19.refs_4_ = bf16[1024,128]{1,0:T(8,128)(2,1)S(1)} collective-permute-done((bf16[1024,128]{1,0:T(8,128)(2,1)S(1)}, bf16[1024,128]{1,0:T(8,128)(2,1)S(1)}, u32[]{:S(2)}, u32[]{:S(2)}) %collective-permute-start.19) | collective-permute-done | bytes 262176 | tf_op jit(solution)/shard_map/ppermute | solution.py:162
  57.7 1.7 %collective-permute-start.21 = (bf16[1024,128]{1,0:T(8,128)(2,1)S(1)}, bf16[1024,128]{1,0:T(8,128)(2,1)S(1)}, u32[]{:S(2)}, u32[]{:S(2)}) collective-permute-start(bf16[1024,128]{1,0:T(8,128)(2,1)S(1)} %get-tuple-element.142.refs_0_), channel_id=1, source_target_pairs={{0,8},{8,16},{16,24},{24,28},{28,20},{20,12},{12,4},{4,0},{1,9},{9... | collective-permute-start | bytes 786440 | tf_op jit(solution)/shard_map/ppermute | solution.py:162
  59.7 3.2 %collective-permute-done.23.refs_2_ = bf16[1024,128]{1,0:T(8,128)(2,1)S(1)} collective-permute-done((bf16[1024,128]{1,0:T(8,128)(2,1)S(1)}, bf16[1024,128]{1,0:T(8,128)(2,1)S(1)}, u32[]{:S(2)}, u32[]{:S(2)}) %collective-permute-start.23) | collective-permute-done | bytes 262176 | tf_op jit(solution)/shard_map/ppermute | solution.py:164
  69.4 1.6 %scatter_blocks.3 = (f32[1024,128]{1,0:T(8,128)S(1)}, f32[8192,128]{1,0:T(8,128)S(1)}) custom-call(s32[64]{0:T(128)S(1)} %fusion.where_ref, s32[1]{0:T(128)} %bitcast.rep_ref, bf16[64,128,128]{2,1,0:T(8,128)(2,1)S(1)} %brought_near.1.vals_ref, bf16[1024,128]{1,0:T(8,128)(2,1)S(1)} %get-tuple-element.129.refs_1_.refs_0_, ...), custom_call_target="tpu_custom_call" | custom-call | flops 268435456 | bytes 7864320 | tf_op jit(solution)/shard_map/scatter_blocks/pallas_call | solution.py:108
  71.3 1.7 %collective-permute-start.33 = (bf16[640,128]{1,0:T(8,128)(2,1)S(1)}, bf16[640,128]{1,0:T(8,128)(2,1)S(1)}, u32[]{:S(2)}, u32[]{:S(2)}) collective-permute-start(bf16[640,128]{1,0:T(8,128)(2,1)S(1)} %get-tuple-element.182), channel_id=1, source_target_pairs={{0,8},{8,16},{16,24},{24,28},{28,20},{20,12},{12,4},{4,0},{1,9},{9... | collective-permute-start | bytes 491528 | tf_op jit(solution)/shard_map/ppermute | solution.py:162
  73.4 1.8 %collective-permute-done.24.refs_2_ = bf16[1024,128]{1,0:T(8,128)(2,1)S(1)} collective-permute-done((bf16[1024,128]{1,0:T(8,128)(2,1)S(1)}, bf16[1024,128]{1,0:T(8,128)(2,1)S(1)}, u32[]{:S(2)}, u32[]{:S(2)}) %collective-permute-start.24) | collective-permute-done | bytes 262176 | tf_op jit(solution)/shard_map/ppermute | solution.py:162
  76.8 1.7 %collective-permute-start.31 = (bf16[1152,128]{1,0:T(8,128)(2,1)S(1)}, bf16[1152,128]{1,0:T(8,128)(2,1)S(1)}, u32[]{:S(2)}, u32[]{:S(2)}) collective-permute-start(bf16[1152,128]{1,0:T(8,128)(2,1)S(1)} %get-tuple-element.180), channel_id=1, source_target_pairs={{0,8},{8,16},{16,24},{24,28},{28,20},{20,12},{12,4},{4,0},{1,9},{9... | collective-permute-start | bytes 884744 | tf_op jit(solution)/shard_map/ppermute | solution.py:162
  82.5 4.3 %collective-permute-done.31.refs_3_ = bf16[1152,128]{1,0:T(8,128)(2,1)S(1)} collective-permute-done((bf16[1152,128]{1,0:T(8,128)(2,1)S(1)}, bf16[1152,128]{1,0:T(8,128)(2,1)S(1)}, u32[]{:S(2)}, u32[]{:S(2)}) %collective-permute-start.31) | collective-permute-done | bytes 294944 | tf_op jit(solution)/shard_map/ppermute | solution.py:162
  86.8 1.7 %collective-permute-done.32.refs_6_ = bf16[1152,128]{1,0:T(8,128)(2,1)S(1)} collective-permute-done((bf16[1152,128]{1,0:T(8,128)(2,1)S(1)}, bf16[1152,128]{1,0:T(8,128)(2,1)S(1)}, u32[]{:S(2)}, u32[]{:S(2)}) %collective-permute-start.32) | collective-permute-done | bytes 294944 | tf_op jit(solution)/shard_map/ppermute | solution.py:162
  88.5 1.9 %collective-permute-start.35 = (bf16[512,128]{1,0:T(8,128)(2,1)S(1)}, bf16[512,128]{1,0:T(8,128)(2,1)S(1)}, u32[]{:S(2)}, u32[]{:S(2)}) collective-permute-start(bf16[512,128]{1,0:T(8,128)(2,1)S(1)} %slice.170), channel_id=1, source_target_pairs={{0,8},{8,16},{16,24},{24,28},{28,20},{20,12},{12,4},{4,0},{1,9},{9... | collective-permute-start | bytes 393224 | tf_op jit(solution)/shard_map/ppermute | solution.py:162
  90.6 3.1 %collective-permute-done.38.refs_2_ = bf16[1152,128]{1,0:T(8,128)(2,1)S(1)} collective-permute-done((bf16[1152,128]{1,0:T(8,128)(2,1)S(1)}, bf16[1152,128]{1,0:T(8,128)(2,1)S(1)}, u32[]{:S(2)}, u32[]{:S(2)}) %collective-permute-start.38) | collective-permute-done | bytes 294944 | tf_op jit(solution)/shard_map/ppermute | solution.py:162
  93.9 1.7 %collective-permute-start.41 = (bf16[1152,128]{1,0:T(8,128)(2,1)S(1)}, bf16[1152,128]{1,0:T(8,128)(2,1)S(1)}, u32[]{:S(2)}, u32[]{:S(2)}) collective-permute-start(bf16[1152,128]{1,0:T(8,128)(2,1)S(1)} %pad_maximum_fusion.4), channel_id=1, source_target_pairs={{0,8},{8,16},{16,24},{24,28},{28,20},{20,12},{12,4},{4,0},{1,9},{9... | collective-permute-start | bytes 884744 | tf_op jit(solution)/shard_map/ppermute | solution.py:162
  98.2 2.5 %collective-permute-done.41.refs_5_ = bf16[1152,128]{1,0:T(8,128)(2,1)S(1)} collective-permute-done((bf16[1152,128]{1,0:T(8,128)(2,1)S(1)}, bf16[1152,128]{1,0:T(8,128)(2,1)S(1)}, u32[]{:S(2)}, u32[]{:S(2)}) %collective-permute-start.41) | collective-permute-done | bytes 294944 | tf_op jit(solution)/shard_map/ppermute | solution.py:162
  100.6 1.7 %collective-permute-done.42.refs_3_ = bf16[1152,128]{1,0:T(8,128)(2,1)S(1)} collective-permute-done((bf16[1152,128]{1,0:T(8,128)(2,1)S(1)}, bf16[1152,128]{1,0:T(8,128)(2,1)S(1)}, u32[]{:S(2)}, u32[]{:S(2)}) %collective-permute-start.42) | collective-permute-done | bytes 294944 | tf_op jit(solution)/shard_map/ppermute | solution.py:162
  104.6 1.6 %collective-permute-start.40 = (bf16[1024,128]{1,0:T(8,128)(2,1)S(1)}, bf16[1024,128]{1,0:T(8,128)(2,1)S(1)}, u32[]{:S(2)}, u32[]{:S(2)}) collective-permute-start(bf16[1024,128]{1,0:T(8,128)(2,1)S(1)} %add_convert_fusion.2), channel_id=1, source_target_pairs={{0,2},{1,3},{2,0},{3,1},{4,6},{5,7},{6,4},{7,5},{8,10},{9,11},{10,... | collective-permute-start | bytes 786440 | tf_op jit(solution)/shard_map/ppermute | solution.py:215
  106.2 3.1 %collective-permute-done.43.refs_4_ = bf16[1152,128]{1,0:T(8,128)(2,1)S(1)} collective-permute-done((bf16[1152,128]{1,0:T(8,128)(2,1)S(1)}, bf16[1152,128]{1,0:T(8,128)(2,1)S(1)}, u32[]{:S(2)}, u32[]{:S(2)}) %collective-permute-start.43) | collective-permute-done | bytes 294944 | tf_op jit(solution)/shard_map/ppermute | solution.py:162
  109.5 1.7 %collective-permute-start.46 = (f32[128,128]{1,0:T(8,128)S(1)}, f32[128,128]{1,0:T(8,128)S(1)}, u32[]{:S(2)}, u32[]{:S(2)}) collective-permute-start(f32[128,128]{1,0:T(8,128)S(1)} %round_sum.1.refs_0_), channel_id=1, source_target_pairs={{0,2},{1,3},{2,0},{3,1},{4,6},{5,7},{6,4},{7,5},{8,10},{9,11},{10,... | collective-permute-start | bytes 196616 | tf_op jit(solution)/shard_map/ppermute | solution.py:388
  (122 shorter events, 59.6 us)
Async XLA Ops:
  1.7 9.3 %collective-permute-start.2 = (bf16[1024,128]{1,0:T(8,128)(2,1)S(1)}, bf16[1024,128]{1,0:T(8,128)(2,1)S(1)}, u32[]{:S(2)}, u32[]{:S(2)}) collective-permute-start(bf16[1024,128]{1,0:T(8,128)(2,1)S(1)} %get-tuple-element.86.refs_0_), channel_id=1, source_target_pairs={{0,2},{1,3},{2,0},{3,1},{4,6},{5,7},{6,4},{7,5},{8,10},{9,11},{10,... | collective-permute-start | bytes 786440 | tf_op jit(solution)/shard_map/ppermute | solution.py:164
  4.7 7.8 %collective-permute-start = (bf16[1024,128]{1,0:T(8,128)(2,1)S(1)}, bf16[1024,128]{1,0:T(8,128)(2,1)S(1)}, u32[]{:S(2)}, u32[]{:S(2)}) collective-permute-start(bf16[1024,128]{1,0:T(8,128)(2,1)S(1)} %get-tuple-element.99.refs_0_), channel_id=1, source_target_pairs={{0,8},{8,16},{16,24},{24,28},{28,20},{20,12},{12,4},{4,0},{1,9},{9... | collective-permute-start | bytes 786440 | tf_op jit(solution)/shard_map/ppermute | solution.py:162
  6.3 7.5 %collective-permute-start.1 = (bf16[1024,128]{1,0:T(8,128)(2,1)S(1)}, bf16[1024,128]{1,0:T(8,128)(2,1)S(1)}, u32[]{:S(2)}, u32[]{:S(2)}) collective-permute-start(bf16[1024,128]{1,0:T(8,128)(2,1)S(1)} %get-tuple-element.99.refs_0_), channel_id=1, source_target_pairs={{8,0},{16,8},{24,16},{28,24},{20,28},{12,20},{4,12},{0,4},{9,1},{1... | collective-permute-start | bytes 786440 | tf_op jit(solution)/shard_map/ppermute | solution.py:162
  13.8 7.8 %collective-permute-start.3 = (bf16[1024,128]{1,0:T(8,128)(2,1)S(1)}, bf16[1024,128]{1,0:T(8,128)(2,1)S(1)}, u32[]{:S(2)}, u32[]{:S(2)}) collective-permute-start(bf16[1024,128]{1,0:T(8,128)(2,1)S(1)} %collective-permute-done.refs_1_), channel_id=1, source_target_pairs={{0,8},{8,16},{16,24},{24,28},{28,20},{20,12},{12,4},{4,0},{1,9},{9... | collective-permute-start | bytes 786440 | tf_op jit(solution)/shard_map/ppermute | solution.py:162
  15.3 7.8 %collective-permute-start.4 = (bf16[1024,128]{1,0:T(8,128)(2,1)S(1)}, bf16[1024,128]{1,0:T(8,128)(2,1)S(1)}, u32[]{:S(2)}, u32[]{:S(2)}) collective-permute-start(bf16[1024,128]{1,0:T(8,128)(2,1)S(1)} %collective-permute-done.1.refs_8_), channel_id=1, source_target_pairs={{8,0},{16,8},{24,16},{28,24},{20,28},{12,20},{4,12},{0,4},{9,1},{1... | collective-permute-start | bytes 786440 | tf_op jit(solution)/shard_map/ppermute | solution.py:162
  17.7 8.3 %collective-permute-start.10 = (bf16[512,128]{1,0:T(8,128)(2,1)S(1)}, bf16[512,128]{1,0:T(8,128)(2,1)S(1)}, u32[]{:S(2)}, u32[]{:S(2)}) collective-permute-start(bf16[512,128]{1,0:T(8,128)(2,1)S(1)} %get-tuple-element.175), channel_id=1, source_target_pairs={{8,0},{16,8},{24,16},{28,24},{20,28},{12,20},{4,12},{0,4},{9,1},{1... | collective-permute-start | bytes 393224 | tf_op jit(solution)/shard_map/ppermute | solution.py:162
  18.2 7.8 %collective-permute-start.9 = (bf16[512,128]{1,0:T(8,128)(2,1)S(1)}, bf16[512,128]{1,0:T(8,128)(2,1)S(1)}, u32[]{:S(2)}, u32[]{:S(2)}) collective-permute-start(bf16[512,128]{1,0:T(8,128)(2,1)S(1)} %get-tuple-element.176), channel_id=1, source_target_pairs={{0,8},{8,16},{16,24},{24,28},{28,20},{20,12},{12,4},{4,0},{1,9},{9... | collective-permute-start | bytes 393224 | tf_op jit(solution)/shard_map/ppermute | solution.py:162
  23.2 9.2 %collective-permute-start.7 = (bf16[1024,128]{1,0:T(8,128)(2,1)S(1)}, bf16[1024,128]{1,0:T(8,128)(2,1)S(1)}, u32[]{:S(2)}, u32[]{:S(2)}) collective-permute-start(bf16[1024,128]{1,0:T(8,128)(2,1)S(1)} %collective-permute-done.3.refs_2_), channel_id=1, source_target_pairs={{0,8},{8,16},{16,24},{24,28},{28,20},{20,12},{12,4},{4,0},{1,9},{9... | collective-permute-start | bytes 786440 | tf_op jit(solution)/shard_map/ppermute | solution.py:162
  24.7 9.2 %collective-permute-start.8 = (bf16[1024,128]{1,0:T(8,128)(2,1)S(1)}, bf16[1024,128]{1,0:T(8,128)(2,1)S(1)}, u32[]{:S(2)}, u32[]{:S(2)}) collective-permute-start(bf16[1024,128]{1,0:T(8,128)(2,1)S(1)} %collective-permute-done.4.refs_7_), channel_id=1, source_target_pairs={{8,0},{16,8},{24,16},{28,24},{20,28},{12,20},{4,12},{0,4},{9,1},{1... | collective-permute-start | bytes 786440 | tf_op jit(solution)/shard_map/ppermute | solution.py:162
  26.1 10.7 %collective-permute-start.13 = (bf16[1024,128]{1,0:T(8,128)(2,1)S(1)}, bf16[1024,128]{1,0:T(8,128)(2,1)S(1)}, u32[]{:S(2)}, u32[]{:S(2)}) collective-permute-start(bf16[1024,128]{1,0:T(8,128)(2,1)S(1)} %get-tuple-element.93), channel_id=1, source_target_pairs={{0,8},{8,16},{16,24},{24,28},{28,20},{20,12},{12,4},{4,0},{1,9},{9... | collective-permute-start | bytes 786440 | tf_op jit(solution)/shard_map/ppermute | solution.py:162
  27.7 10.3 %collective-permute-start.14 = (bf16[1024,128]{1,0:T(8,128)(2,1)S(1)}, bf16[1024,128]{1,0:T(8,128)(2,1)S(1)}, u32[]{:S(2)}, u32[]{:S(2)}) collective-permute-start(bf16[1024,128]{1,0:T(8,128)(2,1)S(1)} %get-tuple-element.94), channel_id=1, source_target_pairs={{8,0},{16,8},{24,16},{28,24},{20,28},{12,20},{4,12},{0,4},{9,1},{1... | collective-permute-start | bytes 786440 | tf_op jit(solution)/shard_map/ppermute | solution.py:162
  46.3 7.1 %collective-permute-start.19 = (bf16[1024,128]{1,0:T(8,128)(2,1)S(1)}, bf16[1024,128]{1,0:T(8,128)(2,1)S(1)}, u32[]{:S(2)}, u32[]{:S(2)}) collective-permute-start(bf16[1024,128]{1,0:T(8,128)(2,1)S(1)} %get-tuple-element.112), channel_id=1, source_target_pairs={{0,8},{8,16},{16,24},{24,28},{28,20},{20,12},{12,4},{4,0},{1,9},{9... | collective-permute-start | bytes 786440 | tf_op jit(solution)/shard_map/ppermute | solution.py:162
  47.7 7.0 %collective-permute-start.20 = (bf16[1024,128]{1,0:T(8,128)(2,1)S(1)}, bf16[1024,128]{1,0:T(8,128)(2,1)S(1)}, u32[]{:S(2)}, u32[]{:S(2)}) collective-permute-start(bf16[1024,128]{1,0:T(8,128)(2,1)S(1)} %get-tuple-element.113), channel_id=1, source_target_pairs={{8,0},{16,8},{24,16},{28,24},{20,28},{12,20},{4,12},{0,4},{9,1},{1... | collective-permute-start | bytes 786440 | tf_op jit(solution)/shard_map/ppermute | solution.py:162
  57.7 7.9 %collective-permute-start.21 = (bf16[1024,128]{1,0:T(8,128)(2,1)S(1)}, bf16[1024,128]{1,0:T(8,128)(2,1)S(1)}, u32[]{:S(2)}, u32[]{:S(2)}) collective-permute-start(bf16[1024,128]{1,0:T(8,128)(2,1)S(1)} %get-tuple-element.142.refs_0_), channel_id=1, source_target_pairs={{0,8},{8,16},{16,24},{24,28},{28,20},{20,12},{12,4},{4,0},{1,9},{9... | collective-permute-start | bytes 786440 | tf_op jit(solution)/shard_map/ppermute | solution.py:162
  66.1 9.1 %collective-permute-start.24 = (bf16[1024,128]{1,0:T(8,128)(2,1)S(1)}, bf16[1024,128]{1,0:T(8,128)(2,1)S(1)}, u32[]{:S(2)}, u32[]{:S(2)}) collective-permute-start(bf16[1024,128]{1,0:T(8,128)(2,1)S(1)} %collective-permute-done.21.refs_1_), channel_id=1, source_target_pairs={{0,8},{8,16},{16,24},{24,28},{28,20},{20,12},{12,4},{4,0},{1,9},{9... | collective-permute-start | bytes 786440 | tf_op jit(solution)/shard_map/ppermute | solution.py:162
  68.2 8.5 %collective-permute-start.25 = (bf16[1024,128]{1,0:T(8,128)(2,1)S(1)}, bf16[1024,128]{1,0:T(8,128)(2,1)S(1)}, u32[]{:S(2)}, u32[]{:S(2)}) collective-permute-start(bf16[1024,128]{1,0:T(8,128)(2,1)S(1)} %collective-permute-done.22.refs_8_), channel_id=1, source_target_pairs={{8,0},{16,8},{24,16},{28,24},{20,28},{12,20},{4,12},{0,4},{9,1},{1... | collective-permute-start | bytes 786440 | tf_op jit(solution)/shard_map/ppermute | solution.py:162
  71.3 9.0 %collective-permute-start.33 = (bf16[640,128]{1,0:T(8,128)(2,1)S(1)}, bf16[640,128]{1,0:T(8,128)(2,1)S(1)}, u32[]{:S(2)}, u32[]{:S(2)}) collective-permute-start(bf16[640,128]{1,0:T(8,128)(2,1)S(1)} %get-tuple-element.182), channel_id=1, source_target_pairs={{0,8},{8,16},{16,24},{24,28},{28,20},{20,12},{12,4},{4,0},{1,9},{9... | collective-permute-start | bytes 491528 | tf_op jit(solution)/shard_map/ppermute | solution.py:162
  73.0 7.3 %collective-permute-start.34 = (bf16[640,128]{1,0:T(8,128)(2,1)S(1)}, bf16[640,128]{1,0:T(8,128)(2,1)S(1)}, u32[]{:S(2)}, u32[]{:S(2)}) collective-permute-start(bf16[640,128]{1,0:T(8,128)(2,1)S(1)} %get-tuple-element.181), channel_id=1, source_target_pairs={{8,0},{16,8},{24,16},{28,24},{20,28},{12,20},{4,12},{0,4},{9,1},{1... | collective-permute-start | bytes 491528 | tf_op jit(solution)/shard_map/ppermute | solution.py:162
  76.8 10.0 %collective-permute-start.31 = (bf16[1152,128]{1,0:T(8,128)(2,1)S(1)}, bf16[1152,128]{1,0:T(8,128)(2,1)S(1)}, u32[]{:S(2)}, u32[]{:S(2)}) collective-permute-start(bf16[1152,128]{1,0:T(8,128)(2,1)S(1)} %get-tuple-element.180), channel_id=1, source_target_pairs={{0,8},{8,16},{16,24},{24,28},{28,20},{20,12},{12,4},{4,0},{1,9},{9... | collective-permute-start | bytes 884744 | tf_op jit(solution)/shard_map/ppermute | solution.py:162
  78.5 9.9 %collective-permute-start.32 = (bf16[1152,128]{1,0:T(8,128)(2,1)S(1)}, bf16[1152,128]{1,0:T(8,128)(2,1)S(1)}, u32[]{:S(2)}, u32[]{:S(2)}) collective-permute-start(bf16[1152,128]{1,0:T(8,128)(2,1)S(1)} %get-tuple-element.179), channel_id=1, source_target_pairs={{8,0},{16,8},{24,16},{28,24},{20,28},{12,20},{4,12},{0,4},{9,1},{1... | collective-permute-start | bytes 884744 | tf_op jit(solution)/shard_map/ppermute | solution.py:162
  80.4 13.3 %collective-permute-start.38 = (bf16[1152,128]{1,0:T(8,128)(2,1)S(1)}, bf16[1152,128]{1,0:T(8,128)(2,1)S(1)}, u32[]{:S(2)}, u32[]{:S(2)}) collective-permute-start(bf16[1152,128]{1,0:T(8,128)(2,1)S(1)} %pad_maximum_fusion.3), channel_id=1, source_target_pairs={{8,0},{16,8},{24,16},{28,24},{20,28},{12,20},{4,12},{0,4},{9,1},{1... | collective-permute-start | bytes 884744 | tf_op jit(solution)/shard_map/ppermute | solution.py:162
  81.0 12.7 %collective-permute-start.37 = (bf16[1152,128]{1,0:T(8,128)(2,1)S(1)}, bf16[1152,128]{1,0:T(8,128)(2,1)S(1)}, u32[]{:S(2)}, u32[]{:S(2)}) collective-permute-start(bf16[1152,128]{1,0:T(8,128)(2,1)S(1)} %pad_maximum_fusion.2), channel_id=1, source_target_pairs={{0,8},{8,16},{16,24},{24,28},{28,20},{20,12},{12,4},{4,0},{1,9},{9... | collective-permute-start | bytes 884744 | tf_op jit(solution)/shard_map/ppermute | solution.py:162
  88.5 7.4 %collective-permute-start.35 = (bf16[512,128]{1,0:T(8,128)(2,1)S(1)}, bf16[512,128]{1,0:T(8,128)(2,1)S(1)}, u32[]{:S(2)}, u32[]{:S(2)}) collective-permute-start(bf16[512,128]{1,0:T(8,128)(2,1)S(1)} %slice.170), channel_id=1, source_target_pairs={{0,8},{8,16},{16,24},{24,28},{28,20},{20,12},{12,4},{4,0},{1,9},{9... | collective-permute-start | bytes 393224 | tf_op jit(solution)/shard_map/ppermute | solution.py:162
  104.0 7.3 %collective-permute-start.44 = (bf16[1024,128]{1,0:T(8,128)(2,1)S(1)}, bf16[1024,128]{1,0:T(8,128)(2,1)S(1)}, u32[]{:S(2)}, u32[]{:S(2)}) collective-permute-start(bf16[1024,128]{1,0:T(8,128)(2,1)S(1)} %get-tuple-element.156), channel_id=1, source_target_pairs={{8,0},{16,8},{24,16},{28,24},{20,28},{12,20},{4,12},{0,4},{9,1},{1... | collective-permute-start | bytes 786440 | tf_op jit(solution)/shard_map/ppermute | solution.py:162
  (27 other events, 156.8 us)

commit v6 on v5

--- a/solution.py
+++ b/solution.py
@@ -297,14 +297,14 @@
     for mask, out in enumerate(outs):
         start = pl.multiple_of(lax.bitwise_xor(rep_ref[0], mask) * rows, rows)
         for h in range(2):
-            out[h * rows : (h + 1) * rows, :] = total[h, pl.ds(start, rows), :]
+            out[h * rows : (h + 1) * rows, :] = total[h, pl.ds(start, rows), :].astype(out.dtype)
 
 
 def local_grad(rep, high, low, masked):
     rows, width = high.shape
     return pl.pallas_call(
         local_kernel,
-        out_shape=[jax.ShapeDtypeStruct((width // 2, HALF), F32)] * 4,
+        out_shape=[jax.ShapeDtypeStruct((width // 2, HALF), t) for t in (F32, BF16, BF16, BF16)],
         in_specs=[SMEM] + [VMEM] * 4,
         out_specs=[VMEM] * 4,
         scratch_shapes=[pltpu.VMEM((2, width, HALF), F32)],
@@ -324,14 +324,14 @@
     total = slots[0]
     for i in range(1, n):
         total = total + slots[i]
-    out_ref[...] = total
+    out_ref[...] = total.astype(BF16)
 
 
 def round_sum(spot, held):
     n, shape = len(held), held[0].shape
     return pl.pallas_call(
         functools.partial(round_kernel, n),
-        out_shape=jax.ShapeDtypeStruct(shape, F32),
+        out_shape=jax.ShapeDtypeStruct(shape, BF16),
         in_specs=[SMEM] + [VMEM] * n,
         out_specs=VMEM,
         scratch_shapes=[pltpu.VMEM((n, *shape), F32)],
@@ -345,7 +345,7 @@
     for mask in range(4):
         start = pl.multiple_of(lax.bitwise_xor(rep_ref[0], mask) * rows, rows)
         for h in range(2):
-            part = refs[mask][h * rows : (h + 1) * rows, :] * scale
+            part = refs[mask][h * rows : (h + 1) * rows, :].astype(F32) * scale
             refs[4][pl.ds(start, rows), h * HALF : (h + 1) * HALF] = part
 
 
@@ -374,7 +374,7 @@
     def riders(self, after):
         value = self.quarters[0]
         for mask in (1, 2, 3):
-            value = value + lax.ppermute(self.quarters[mask], "rep", self.pairs[mask])
+            value = value + lax.ppermute(self.quarters[mask], "rep", self.pairs[mask]).astype(F32)
         self.value = value.astype(BF16)
         return self.value
 

time: 116 us -> 115 us (level)
  starting transfers between devices: 43.9 us -> 42.2 us
    ppermute x3, waiting for transfers between devices: 2.59 us -> 1.16 us  [finish(): lax.ppermute(value, 'rep', self.pairs[mask])]
    ppermute x16, waiting for transfers between devices: 26.2 us -> 27.3 us  [spread(): lax.ppermute(pair[0], 'rows', ahead)]
  transfers between devices with their start and end apart: 48 -> 48, of which waited for: 31 -> 30; matrix products, arithmetic and copies ran while one was open for 2% -> 2% of each run, Pallas kernels for 7% -> 8%
where the time goes in v6:
time: 115 us; the launch traced here: 114 us
  waiting for transfers between devices  55.4 us (48%)
  starting transfers between devices  42.2 us (37%)
  Pallas kernels  10.9 us (9%)
  local copies, waits for them, and re-layouts  3.66 us (3%)
  other arithmetic  1.34 us (1%)
    ppermute x16, waiting for transfers between devices, spread(): lax.ppermute(pair[0], 'rows', ahead)  27.3 us
    ppermute x16, starting transfers between devices, spread(): lax.ppermute(pair[0], 'rows', ahead)  24.4 us
    ppermute x16, waiting for transfers between devices, spread(): lax.ppermute(pair[1], 'rows', behind)  20.3 us
    ppermute x16, starting transfers between devices, spread(): lax.ppermute(pair[1], 'rows', behind)  8.59 us
    ppermute x2, waiting for transfers between devices, spread(): across = lax.ppermute(second, 'rep', pairs[2])  4.72 us
    ppermute x2, starting transfers between devices, spread(): across = lax.ppermute(second, 'rep', pairs[2])  4.22 us
    pallas_call x2, Pallas kernels, scatter_blocks(): pl.pallas_call(functools.partial(scatter_kernel, own_blocks, block, scale...  3.27 us
    pallas_call x2, Pallas kernels, gather_blocks(): pl.pallas_call(functools.partial(gather_kernel, n, own_blocks, block, sca...  3.04 us
  transfers between devices with their start and end apart: 48, of which 30 were waited for; matrix products, arithmetic and copies ran while one was open for 2% of the time, Pallas kernels for 8%

profile of v6, /device:TPU:0, one launch (start us, length us, event | category | flops | bytes accessed | tf_op | source)
XLA Modules:
  0.0 114.4 jit_solution(7506947026341148187)
XLA Ops:
  1.7 3.0 %collective-permute-start.2 = (bf16[1024,128]{1,0:T(8,128)(2,1)S(1)}, bf16[1024,128]{1,0:T(8,128)(2,1)S(1)}, u32[]{:S(2)}, u32[]{:S(2)}) collective-permute-start(bf16[1024,128]{1,0:T(8,128)(2,1)S(1)} %get-tuple-element.86.refs_0_), channel_id=1, source_target_pairs={{0,2},{1,3},{2,0},{3,1},{4,6},{5,7},{6,4},{7,5},{8,10},{9,11},{10,... | collective-permute-start | bytes 786440 | tf_op jit(solution)/shard_map/ppermute | solution.py:164
  4.7 1.6 %collective-permute-start = (bf16[1024,128]{1,0:T(8,128)(2,1)S(1)}, bf16[1024,128]{1,0:T(8,128)(2,1)S(1)}, u32[]{:S(2)}, u32[]{:S(2)}) collective-permute-start(bf16[1024,128]{1,0:T(8,128)(2,1)S(1)} %get-tuple-element.99.refs_0_), channel_id=1, source_target_pairs={{0,8},{8,16},{16,24},{24,28},{28,20},{20,12},{12,4},{4,0},{1,9},{9... | collective-permute-start | bytes 786440 | tf_op jit(solution)/shard_map/ppermute | solution.py:162
  7.7 1.6 %copy-done.1 = bf16[32,1,2,128,128]{4,3,2,1,0:T(8,128)(2,1)S(1)} copy-done((bf16[32,1,2,128,128]{4,3,2,1,0:T(8,128)(2,1)S(1)}, bf16[32,1,2,128,128]{4,3,2,1,0:T(8,128)(2,1)}, u32[]{:S(2)}) %copy-start.1) | copy-done | bytes 2097176
  13.8 1.6 %collective-permute-start.3 = (bf16[1024,128]{1,0:T(8,128)(2,1)S(1)}, bf16[1024,128]{1,0:T(8,128)(2,1)S(1)}, u32[]{:S(2)}, u32[]{:S(2)}) collective-permute-start(bf16[1024,128]{1,0:T(8,128)(2,1)S(1)} %collective-permute-done.refs_1_), channel_id=1, source_target_pairs={{0,8},{8,16},{16,24},{24,28},{28,20},{20,12},{12,4},{4,0},{1,9},{9... | collective-permute-start | bytes 786440 | tf_op jit(solution)/shard_map/ppermute | solution.py:162
  15.8 1.6 %scatter_blocks.2 = (f32[1024,128]{1,0:T(8,128)S(1)}, f32[8192,128]{1,0:T(8,128)S(1)}) custom-call(s32[64]{0:T(128)S(1)} %fusion.where_ref, s32[1]{0:T(128)} %bitcast.rep_ref, bf16[64,128,128]{2,1,0:T(8,128)(2,1)S(1)} %brought_near.1.vals_ref, bf16[1024,128]{1,0:T(8,128)(2,1)S(1)} %get-tuple-element.86.refs_0_, ...), custom_call_target="tpu_custom_call" | custom-call | flops 268435456 | bytes 7864320 | tf_op jit(solution)/shard_map/scatter_blocks/pallas_call | solution.py:108
  19.8 1.8 %collective-permute-done.3.refs_2_ = bf16[1024,128]{1,0:T(8,128)(2,1)S(1)} collective-permute-done((bf16[1024,128]{1,0:T(8,128)(2,1)S(1)}, bf16[1024,128]{1,0:T(8,128)(2,1)S(1)}, u32[]{:S(2)}, u32[]{:S(2)}) %collective-permute-start.3) | collective-permute-done | bytes 262176 | tf_op jit(solution)/shard_map/ppermute | solution.py:162
  21.5 1.6 %collective-permute-done.4.refs_7_ = bf16[1024,128]{1,0:T(8,128)(2,1)S(1)} collective-permute-done((bf16[1024,128]{1,0:T(8,128)(2,1)S(1)}, bf16[1024,128]{1,0:T(8,128)(2,1)S(1)}, u32[]{:S(2)}, u32[]{:S(2)}) %collective-permute-start.4) | collective-permute-done | bytes 262176 | tf_op jit(solution)/shard_map/ppermute | solution.py:162
  28.2 4.2 %collective-permute-done.7.refs_3_ = bf16[1024,128]{1,0:T(8,128)(2,1)S(1)} collective-permute-done((bf16[1024,128]{1,0:T(8,128)(2,1)S(1)}, bf16[1024,128]{1,0:T(8,128)(2,1)S(1)}, u32[]{:S(2)}, u32[]{:S(2)}) %collective-permute-start.7) | collective-permute-done | bytes 262176 | tf_op jit(solution)/shard_map/ppermute | solution.py:162
  38.1 1.6 %collective-permute-start.17 = (bf16[1024,128]{1,0:T(8,128)(2,1)S(1)}, bf16[1024,128]{1,0:T(8,128)(2,1)S(1)}, u32[]{:S(2)}, u32[]{:S(2)}) collective-permute-start(bf16[1024,128]{1,0:T(8,128)(2,1)S(1)} %get-tuple-element.97), channel_id=1, source_target_pairs={{0,8},{8,16},{16,24},{24,28},{28,20},{20,12},{12,4},{4,0},{1,9},{9... | collective-permute-start | bytes 786440 | tf_op jit(solution)/shard_map/ppermute | solution.py:162
  41.3 1.7 %gather_blocks.2 = (bf16[2048,128]{1,0:T(8,128)(2,1)S(1)}, f32[1024,128]{1,0:T(8,128)S(1)}, f32[1024,128]{1,0:T(8,128)S(1)}) custom-call(s32[64]{0:T(128)S(1)} %fusion.where_ref, s32[1]{0:T(128)} %bitcast.rep_ref, bf16[64,128,128]{2,1,0:T(8,128)(2,1)S(1)} %brought_near.1.vals_ref, bf16[1024,128]{1,0:T(8,128)(2,1)S(1)} %get-tuple-element.99.refs_0_, ...), custom_call_target="tpu_custom_call" | custom-call | flops 26843545600 | bytes 7864320 | tf_op jit(solution)/shard_map/gather_blocks/pallas_call | solution.py:71
  44.5 1.6 %collective-permute-done.18 = bf16[1024,128]{1,0:T(8,128)(2,1)S(1)} collective-permute-done((bf16[1024,128]{1,0:T(8,128)(2,1)S(1)}, bf16[1024,128]{1,0:T(8,128)(2,1)S(1)}, u32[]{:S(2)}, u32[]{:S(2)}) %collective-permute-start.18) | collective-permute-done | bytes 262176 | tf_op jit(solution)/shard_map/ppermute | solution.py:162
  48.6 4.8 %collective-permute-done.19.refs_4_ = bf16[1024,128]{1,0:T(8,128)(2,1)S(1)} collective-permute-done((bf16[1024,128]{1,0:T(8,128)(2,1)S(1)}, bf16[1024,128]{1,0:T(8,128)(2,1)S(1)}, u32[]{:S(2)}, u32[]{:S(2)}) %collective-permute-start.19) | collective-permute-done | bytes 262176 | tf_op jit(solution)/shard_map/ppermute | solution.py:162
  57.7 1.7 %collective-permute-start.21 = (bf16[1024,128]{1,0:T(8,128)(2,1)S(1)}, bf16[1024,128]{1,0:T(8,128)(2,1)S(1)}, u32[]{:S(2)}, u32[]{:S(2)}) collective-permute-start(bf16[1024,128]{1,0:T(8,128)(2,1)S(1)} %get-tuple-element.142.refs_0_), channel_id=1, source_target_pairs={{0,8},{8,16},{16,24},{24,28},{28,20},{20,12},{12,4},{4,0},{1,9},{9... | collective-permute-start | bytes 786440 | tf_op jit(solution)/shard_map/ppermute | solution.py:162
  59.7 3.2 %collective-permute-done.23.refs_2_ = bf16[1024,128]{1,0:T(8,128)(2,1)S(1)} collective-permute-done((bf16[1024,128]{1,0:T(8,128)(2,1)S(1)}, bf16[1024,128]{1,0:T(8,128)(2,1)S(1)}, u32[]{:S(2)}, u32[]{:S(2)}) %collective-permute-start.23) | collective-permute-done | bytes 262176 | tf_op jit(solution)/shard_map/ppermute | solution.py:164
  69.4 1.6 %scatter_blocks.3 = (f32[1024,128]{1,0:T(8,128)S(1)}, f32[8192,128]{1,0:T(8,128)S(1)}) custom-call(s32[64]{0:T(128)S(1)} %fusion.where_ref, s32[1]{0:T(128)} %bitcast.rep_ref, bf16[64,128,128]{2,1,0:T(8,128)(2,1)S(1)} %brought_near.1.vals_ref, bf16[1024,128]{1,0:T(8,128)(2,1)S(1)} %get-tuple-element.129.refs_1_.refs_0_, ...), custom_call_target="tpu_custom_call" | custom-call | flops 268435456 | bytes 7864320 | tf_op jit(solution)/shard_map/scatter_blocks/pallas_call | solution.py:108
  75.0 1.8 %collective-permute-done.25.refs_7_ = bf16[1024,128]{1,0:T(8,128)(2,1)S(1)} collective-permute-done((bf16[1024,128]{1,0:T(8,128)(2,1)S(1)}, bf16[1024,128]{1,0:T(8,128)(2,1)S(1)}, u32[]{:S(2)}, u32[]{:S(2)}) %collective-permute-start.25) | collective-permute-done | bytes 262176 | tf_op jit(solution)/shard_map/ppermute | solution.py:162
  76.8 1.8 %collective-permute-start.31 = (bf16[1152,128]{1,0:T(8,128)(2,1)S(1)}, bf16[1152,128]{1,0:T(8,128)(2,1)S(1)}, u32[]{:S(2)}, u32[]{:S(2)}) collective-permute-start(bf16[1152,128]{1,0:T(8,128)(2,1)S(1)} %get-tuple-element.180), channel_id=1, source_target_pairs={{0,8},{8,16},{16,24},{24,28},{28,20},{20,12},{12,4},{4,0},{1,9},{9... | collective-permute-start | bytes 884744 | tf_op jit(solution)/shard_map/ppermute | solution.py:162
  82.5 4.3 %collective-permute-done.31.refs_3_ = bf16[1152,128]{1,0:T(8,128)(2,1)S(1)} collective-permute-done((bf16[1152,128]{1,0:T(8,128)(2,1)S(1)}, bf16[1152,128]{1,0:T(8,128)(2,1)S(1)}, u32[]{:S(2)}, u32[]{:S(2)}) %collective-permute-start.31) | collective-permute-done | bytes 294944 | tf_op jit(solution)/shard_map/ppermute | solution.py:162
  86.8 1.8 %collective-permute-done.32.refs_6_ = bf16[1152,128]{1,0:T(8,128)(2,1)S(1)} collective-permute-done((bf16[1152,128]{1,0:T(8,128)(2,1)S(1)}, bf16[1152,128]{1,0:T(8,128)(2,1)S(1)}, u32[]{:S(2)}, u32[]{:S(2)}) %collective-permute-start.32) | collective-permute-done | bytes 294944 | tf_op jit(solution)/shard_map/ppermute | solution.py:162
  90.7 2.9 %collective-permute-done.38.refs_2_ = bf16[1152,128]{1,0:T(8,128)(2,1)S(1)} collective-permute-done((bf16[1152,128]{1,0:T(8,128)(2,1)S(1)}, bf16[1152,128]{1,0:T(8,128)(2,1)S(1)}, u32[]{:S(2)}, u32[]{:S(2)}) %collective-permute-start.38) | collective-permute-done | bytes 294944 | tf_op jit(solution)/shard_map/ppermute | solution.py:162
  93.8 1.7 %collective-permute-start.41 = (bf16[1152,128]{1,0:T(8,128)(2,1)S(1)}, bf16[1152,128]{1,0:T(8,128)(2,1)S(1)}, u32[]{:S(2)}, u32[]{:S(2)}) collective-permute-start(bf16[1152,128]{1,0:T(8,128)(2,1)S(1)} %pad_maximum_fusion.4), channel_id=1, source_target_pairs={{0,8},{8,16},{16,24},{24,28},{28,20},{20,12},{12,4},{4,0},{1,9},{9... | collective-permute-start | bytes 884744 | tf_op jit(solution)/shard_map/ppermute | solution.py:162
  97.7 2.8 %collective-permute-done.41.refs_5_ = bf16[1152,128]{1,0:T(8,128)(2,1)S(1)} collective-permute-done((bf16[1152,128]{1,0:T(8,128)(2,1)S(1)}, bf16[1152,128]{1,0:T(8,128)(2,1)S(1)}, u32[]{:S(2)}, u32[]{:S(2)}) %collective-permute-start.41) | collective-permute-done | bytes 294944 | tf_op jit(solution)/shard_map/ppermute | solution.py:162
  100.6 1.6 %collective-permute-done.42.refs_3_ = bf16[1152,128]{1,0:T(8,128)(2,1)S(1)} collective-permute-done((bf16[1152,128]{1,0:T(8,128)(2,1)S(1)}, bf16[1152,128]{1,0:T(8,128)(2,1)S(1)}, u32[]{:S(2)}, u32[]{:S(2)}) %collective-permute-start.42) | collective-permute-done | bytes 294944 | tf_op jit(solution)/shard_map/ppermute | solution.py:162
  105.0 4.2 %collective-permute-done.43.refs_4_ = bf16[1152,128]{1,0:T(8,128)(2,1)S(1)} collective-permute-done((bf16[1152,128]{1,0:T(8,128)(2,1)S(1)}, bf16[1152,128]{1,0:T(8,128)(2,1)S(1)}, u32[]{:S(2)}, u32[]{:S(2)}) %collective-permute-start.43) | collective-permute-done | bytes 294944 | tf_op jit(solution)/shard_map/ppermute | solution.py:162
  (122 shorter events, 57.2 us)
Async XLA Ops:
  1.7 9.3 %collective-permute-start.2 = (bf16[1024,128]{1,0:T(8,128)(2,1)S(1)}, bf16[1024,128]{1,0:T(8,128)(2,1)S(1)}, u32[]{:S(2)}, u32[]{:S(2)}) collective-permute-start(bf16[1024,128]{1,0:T(8,128)(2,1)S(1)} %get-tuple-element.86.refs_0_), channel_id=1, source_target_pairs={{0,2},{1,3},{2,0},{3,1},{4,6},{5,7},{6,4},{7,5},{8,10},{9,11},{10,... | collective-permute-start | bytes 786440 | tf_op jit(solution)/shard_map/ppermute | solution.py:164
  4.7 7.8 %collective-permute-start = (bf16[1024,128]{1,0:T(8,128)(2,1)S(1)}, bf16[1024,128]{1,0:T(8,128)(2,1)S(1)}, u32[]{:S(2)}, u32[]{:S(2)}) collective-permute-start(bf16[1024,128]{1,0:T(8,128)(2,1)S(1)} %get-tuple-element.99.refs_0_), channel_id=1, source_target_pairs={{0,8},{8,16},{16,24},{24,28},{28,20},{20,12},{12,4},{4,0},{1,9},{9... | collective-permute-start | bytes 786440 | tf_op jit(solution)/shard_map/ppermute | solution.py:162
  6.3 7.5 %collective-permute-start.1 = (bf16[1024,128]{1,0:T(8,128)(2,1)S(1)}, bf16[1024,128]{1,0:T(8,128)(2,1)S(1)}, u32[]{:S(2)}, u32[]{:S(2)}) collective-permute-start(bf16[1024,128]{1,0:T(8,128)(2,1)S(1)} %get-tuple-element.99.refs_0_), channel_id=1, source_target_pairs={{8,0},{16,8},{24,16},{28,24},{20,28},{12,20},{4,12},{0,4},{9,1},{1... | collective-permute-start | bytes 786440 | tf_op jit(solution)/shard_map/ppermute | solution.py:162
  13.8 7.8 %collective-permute-start.3 = (bf16[1024,128]{1,0:T(8,128)(2,1)S(1)}, bf16[1024,128]{1,0:T(8,128)(2,1)S(1)}, u32[]{:S(2)}, u32[]{:S(2)}) collective-permute-start(bf16[1024,128]{1,0:T(8,128)(2,1)S(1)} %collective-permute-done.refs_1_), channel_id=1, source_target_pairs={{0,8},{8,16},{16,24},{24,28},{28,20},{20,12},{12,4},{4,0},{1,9},{9... | collective-permute-start | bytes 786440 | tf_op jit(solution)/shard_map/ppermute | solution.py:162
  15.3 7.8 %collective-permute-start.4 = (bf16[1024,128]{1,0:T(8,128)(2,1)S(1)}, bf16[1024,128]{1,0:T(8,128)(2,1)S(1)}, u32[]{:S(2)}, u32[]{:S(2)}) collective-permute-start(bf16[1024,128]{1,0:T(8,128)(2,1)S(1)} %collective-permute-done.1.refs_8_), channel_id=1, source_target_pairs={{8,0},{16,8},{24,16},{28,24},{20,28},{12,20},{4,12},{0,4},{9,1},{1... | collective-permute-start | bytes 786440 | tf_op jit(solution)/shard_map/ppermute | solution.py:162
  17.7 8.3 %collective-permute-start.10 = (bf16[512,128]{1,0:T(8,128)(2,1)S(1)}, bf16[512,128]{1,0:T(8,128)(2,1)S(1)}, u32[]{:S(2)}, u32[]{:S(2)}) collective-permute-start(bf16[512,128]{1,0:T(8,128)(2,1)S(1)} %get-tuple-element.175), channel_id=1, source_target_pairs={{8,0},{16,8},{24,16},{28,24},{20,28},{12,20},{4,12},{0,4},{9,1},{1... | collective-permute-start | bytes 393224 | tf_op jit(solution)/shard_map/ppermute | solution.py:162
  18.2 7.8 %collective-permute-start.9 = (bf16[512,128]{1,0:T(8,128)(2,1)S(1)}, bf16[512,128]{1,0:T(8,128)(2,1)S(1)}, u32[]{:S(2)}, u32[]{:S(2)}) collective-permute-start(bf16[512,128]{1,0:T(8,128)(2,1)S(1)} %get-tuple-element.176), channel_id=1, source_target_pairs={{0,8},{8,16},{16,24},{24,28},{28,20},{20,12},{12,4},{4,0},{1,9},{9... | collective-permute-start | bytes 393224 | tf_op jit(solution)/shard_map/ppermute | solution.py:162
  23.2 9.2 %collective-permute-start.7 = (bf16[1024,128]{1,0:T(8,128)(2,1)S(1)}, bf16[1024,128]{1,0:T(8,128)(2,1)S(1)}, u32[]{:S(2)}, u32[]{:S(2)}) collective-permute-start(bf16[1024,128]{1,0:T(8,128)(2,1)S(1)} %collective-permute-done.3.refs_2_), channel_id=1, source_target_pairs={{0,8},{8,16},{16,24},{24,28},{28,20},{20,12},{12,4},{4,0},{1,9},{9... | collective-permute-start | bytes 786440 | tf_op jit(solution)/shard_map/ppermute | solution.py:162
  24.7 9.2 %collective-permute-start.8 = (bf16[1024,128]{1,0:T(8,128)(2,1)S(1)}, bf16[1024,128]{1,0:T(8,128)(2,1)S(1)}, u32[]{:S(2)}, u32[]{:S(2)}) collective-permute-start(bf16[1024,128]{1,0:T(8,128)(2,1)S(1)} %collective-permute-done.4.refs_7_), channel_id=1, source_target_pairs={{8,0},{16,8},{24,16},{28,24},{20,28},{12,20},{4,12},{0,4},{9,1},{1... | collective-permute-start | bytes 786440 | tf_op jit(solution)/shard_map/ppermute | solution.py:162
  26.1 10.7 %collective-permute-start.13 = (bf16[1024,128]{1,0:T(8,128)(2,1)S(1)}, bf16[1024,128]{1,0:T(8,128)(2,1)S(1)}, u32[]{:S(2)}, u32[]{:S(2)}) collective-permute-start(bf16[1024,128]{1,0:T(8,128)(2,1)S(1)} %get-tuple-element.93), channel_id=1, source_target_pairs={{0,8},{8,16},{16,24},{24,28},{28,20},{20,12},{12,4},{4,0},{1,9},{9... | collective-permute-start | bytes 786440 | tf_op jit(solution)/shard_map/ppermute | solution.py:162
  27.7 10.3 %collective-permute-start.14 = (bf16[1024,128]{1,0:T(8,128)(2,1)S(1)}, bf16[1024,128]{1,0:T(8,128)(2,1)S(1)}, u32[]{:S(2)}, u32[]{:S(2)}) collective-permute-start(bf16[1024,128]{1,0:T(8,128)(2,1)S(1)} %get-tuple-element.94), channel_id=1, source_target_pairs={{8,0},{16,8},{24,16},{28,24},{20,28},{12,20},{4,12},{0,4},{9,1},{1... | collective-permute-start | bytes 786440 | tf_op jit(solution)/shard_map/ppermute | solution.py:162
  46.3 7.1 %collective-permute-start.19 = (bf16[1024,128]{1,0:T(8,128)(2,1)S(1)}, bf16[1024,128]{1,0:T(8,128)(2,1)S(1)}, u32[]{:S(2)}, u32[]{:S(2)}) collective-permute-start(bf16[1024,128]{1,0:T(8,128)(2,1)S(1)} %get-tuple-element.112), channel_id=1, source_target_pairs={{0,8},{8,16},{16,24},{24,28},{28,20},{20,12},{12,4},{4,0},{1,9},{9... | collective-permute-start | bytes 786440 | tf_op jit(solution)/shard_map/ppermute | solution.py:162
  47.7 7.0 %collective-permute-start.20 = (bf16[1024,128]{1,0:T(8,128)(2,1)S(1)}, bf16[1024,128]{1,0:T(8,128)(2,1)S(1)}, u32[]{:S(2)}, u32[]{:S(2)}) collective-permute-start(bf16[1024,128]{1,0:T(8,128)(2,1)S(1)} %get-tuple-element.113), channel_id=1, source_target_pairs={{8,0},{16,8},{24,16},{28,24},{20,28},{12,20},{4,12},{0,4},{9,1},{1... | collective-permute-start | bytes 786440 | tf_op jit(solution)/shard_map/ppermute | solution.py:162
  59.7 9.7 %collective-permute-start.26 = (bf16[1024,128]{1,0:T(8,128)(2,1)S(1)}, bf16[1024,128]{1,0:T(8,128)(2,1)S(1)}, u32[]{:S(2)}, u32[]{:S(2)}) collective-permute-start(bf16[1024,128]{1,0:T(8,128)(2,1)S(1)} %get-tuple-element.129.refs_1_.refs_0_), channel_id=1, source_target_pairs={{0,1},{1,0},{2,3},{3,2},{4,5},{5,4},{6,7},{7,6},{8,9},{9,8},{10,11... | collective-permute-start | bytes 786440 | tf_op jit(solution)/shard_map/ppermute | solution.py:165
  65.7 9.2 %collective-permute-start.24 = (bf16[1024,128]{1,0:T(8,128)(2,1)S(1)}, bf16[1024,128]{1,0:T(8,128)(2,1)S(1)}, u32[]{:S(2)}, u32[]{:S(2)}) collective-permute-start(bf16[1024,128]{1,0:T(8,128)(2,1)S(1)} %collective-permute-done.21.refs_1_), channel_id=1, source_target_pairs={{0,8},{8,16},{16,24},{24,28},{28,20},{20,12},{12,4},{4,0},{1,9},{9... | collective-permute-start | bytes 786440 | tf_op jit(solution)/shard_map/ppermute | solution.py:162
  68.1 8.6 %collective-permute-start.25 = (bf16[1024,128]{1,0:T(8,128)(2,1)S(1)}, bf16[1024,128]{1,0:T(8,128)(2,1)S(1)}, u32[]{:S(2)}, u32[]{:S(2)}) collective-permute-start(bf16[1024,128]{1,0:T(8,128)(2,1)S(1)} %collective-permute-done.22.refs_8_), channel_id=1, source_target_pairs={{8,0},{16,8},{24,16},{28,24},{20,28},{12,20},{4,12},{0,4},{9,1},{1... | collective-permute-start | bytes 786440 | tf_op jit(solution)/shard_map/ppermute | solution.py:162
  71.4 8.9 %collective-permute-start.33 = (bf16[640,128]{1,0:T(8,128)(2,1)S(1)}, bf16[640,128]{1,0:T(8,128)(2,1)S(1)}, u32[]{:S(2)}, u32[]{:S(2)}) collective-permute-start(bf16[640,128]{1,0:T(8,128)(2,1)S(1)} %get-tuple-element.182), channel_id=1, source_target_pairs={{0,8},{8,16},{16,24},{24,28},{28,20},{20,12},{12,4},{4,0},{1,9},{9... | collective-permute-start | bytes 491528 | tf_op jit(solution)/shard_map/ppermute | solution.py:162
  72.9 7.4 %collective-permute-start.34 = (bf16[640,128]{1,0:T(8,128)(2,1)S(1)}, bf16[640,128]{1,0:T(8,128)(2,1)S(1)}, u32[]{:S(2)}, u32[]{:S(2)}) collective-permute-start(bf16[640,128]{1,0:T(8,128)(2,1)S(1)} %get-tuple-element.181), channel_id=1, source_target_pairs={{8,0},{16,8},{24,16},{28,24},{20,28},{12,20},{4,12},{0,4},{9,1},{1... | collective-permute-start | bytes 491528 | tf_op jit(solution)/shard_map/ppermute | solution.py:162
  76.8 10.0 %collective-permute-start.31 = (bf16[1152,128]{1,0:T(8,128)(2,1)S(1)}, bf16[1152,128]{1,0:T(8,128)(2,1)S(1)}, u32[]{:S(2)}, u32[]{:S(2)}) collective-permute-start(bf16[1152,128]{1,0:T(8,128)(2,1)S(1)} %get-tuple-element.180), channel_id=1, source_target_pairs={{0,8},{8,16},{16,24},{24,28},{28,20},{20,12},{12,4},{4,0},{1,9},{9... | collective-permute-start | bytes 884744 | tf_op jit(solution)/shard_map/ppermute | solution.py:162
  78.6 9.9 %collective-permute-start.32 = (bf16[1152,128]{1,0:T(8,128)(2,1)S(1)}, bf16[1152,128]{1,0:T(8,128)(2,1)S(1)}, u32[]{:S(2)}, u32[]{:S(2)}) collective-permute-start(bf16[1152,128]{1,0:T(8,128)(2,1)S(1)} %get-tuple-element.179), channel_id=1, source_target_pairs={{8,0},{16,8},{24,16},{28,24},{20,28},{12,20},{4,12},{0,4},{9,1},{1... | collective-permute-start | bytes 884744 | tf_op jit(solution)/shard_map/ppermute | solution.py:162
  80.4 13.2 %collective-permute-start.38 = (bf16[1152,128]{1,0:T(8,128)(2,1)S(1)}, bf16[1152,128]{1,0:T(8,128)(2,1)S(1)}, u32[]{:S(2)}, u32[]{:S(2)}) collective-permute-start(bf16[1152,128]{1,0:T(8,128)(2,1)S(1)} %pad_maximum_fusion.3), channel_id=1, source_target_pairs={{8,0},{16,8},{24,16},{28,24},{20,28},{12,20},{4,12},{0,4},{9,1},{1... | collective-permute-start | bytes 884744 | tf_op jit(solution)/shard_map/ppermute | solution.py:162
  80.9 12.7 %collective-permute-start.37 = (bf16[1152,128]{1,0:T(8,128)(2,1)S(1)}, bf16[1152,128]{1,0:T(8,128)(2,1)S(1)}, u32[]{:S(2)}, u32[]{:S(2)}) collective-permute-start(bf16[1152,128]{1,0:T(8,128)(2,1)S(1)} %pad_maximum_fusion.2), channel_id=1, source_target_pairs={{0,8},{8,16},{16,24},{24,28},{28,20},{20,12},{12,4},{4,0},{1,9},{9... | collective-permute-start | bytes 884744 | tf_op jit(solution)/shard_map/ppermute | solution.py:162
  88.6 7.3 %collective-permute-start.35 = (bf16[512,128]{1,0:T(8,128)(2,1)S(1)}, bf16[512,128]{1,0:T(8,128)(2,1)S(1)}, u32[]{:S(2)}, u32[]{:S(2)}) collective-permute-start(bf16[512,128]{1,0:T(8,128)(2,1)S(1)} %slice.170), channel_id=1, source_target_pairs={{0,8},{8,16},{16,24},{24,28},{28,20},{20,12},{12,4},{4,0},{1,9},{9... | collective-permute-start | bytes 393224 | tf_op jit(solution)/shard_map/ppermute | solution.py:162
  103.4 7.8 %collective-permute-start.44 = (bf16[1024,128]{1,0:T(8,128)(2,1)S(1)}, bf16[1024,128]{1,0:T(8,128)(2,1)S(1)}, u32[]{:S(2)}, u32[]{:S(2)}) collective-permute-start(bf16[1024,128]{1,0:T(8,128)(2,1)S(1)} %get-tuple-element.156), channel_id=1, source_target_pairs={{8,0},{16,8},{24,16},{28,24},{20,28},{12,20},{4,12},{0,4},{9,1},{1... | collective-permute-start | bytes 786440 | tf_op jit(solution)/shard_map/ppermute | solution.py:162
  (27 other events, 160.2 us)

commit v7 on v6

--- a/solution.py
+++ b/solution.py
@@ -83,7 +83,7 @@
 
 
 def scatter_kernel(own_blocks, block, scale, where_ref, rep_ref, vals_ref, *refs):
-    sources, (own_ref, out_ref) = refs[:4], refs[4:]
+    sources, (own_ref, out_ref, ahead_ref, behind_ref) = refs[:4], refs[4:]
     rows = own_blocks * block
     out_ref[...] = jnp.zeros_like(out_ref)
     me = rep_ref[0]
@@ -99,17 +99,21 @@
                 term = lax.dot_general(vals_ref[item], source, (((0,), (0,)), ((), ())), preferred_element_type=F32)
                 out_ref[pl.ds(start, block), :] += term
     own_ref[...] = out_ref[:rows, :]
-
-
-def scatter_blocks(where, rep, vals, sources, n, own_blocks, scale):
+    first, mid = out_ref.shape[0] // 2, rows // 2
+    ahead_ref[...] = out_ref[first : first + mid, :].astype(ahead_ref.dtype)
+    behind_ref[...] = out_ref[first + mid : first + rows, :].astype(behind_ref.dtype)
+
+
+def scatter_blocks(where, rep, vals, sources, n, own_blocks, scale, sent):
     block = vals.shape[-1]
     rows, width = sources[0].shape
     size = vals.size * 2 + 4 * rows * width * 2 + (n + 1) * rows * width * 4
     return pl.pallas_call(
         functools.partial(scatter_kernel, own_blocks, block, scale),
-        out_shape=[jax.ShapeDtypeStruct((rows, width), F32), jax.ShapeDtypeStruct((n * rows, width), F32)],
+        out_shape=[jax.ShapeDtypeStruct((size_of * rows, width), F32) for size_of in (1, n)]
+        + [jax.ShapeDtypeStruct((rows // 2, width), sent)] * 2,
         in_specs=[SMEM, SMEM, VMEM] + [VMEM] * 4,
-        out_specs=[VMEM] * 2,
+        out_specs=[VMEM] * 4,
         compiler_params=pltpu.CompilerParams(vmem_limit_bytes=size + (4 << 20)),
         cost_estimate=pl.CostEstimate(
             flops=2 * vals.size * width, bytes_accessed=size, transcendentals=0
@@ -183,9 +187,9 @@
         if hop == 2:
             where, rep, vals = numbers()
             sources = tie([second, beside, across, far], behind_it)
-            own, partial = scatter_blocks(where, rep, vals, sources, n, own_blocks, scale)
+            own, partial, *moving = scatter_blocks(where, rep, vals, sources, n, own_blocks, scale, sent)
             term = lambda distance: partial[distance * rows : (distance + 1) * rows]
-            moving = term(half)[:mid].astype(sent), term(half)[mid:].astype(sent)
+            moving = tuple(moving)
             if "riders" in hooks:
                 rider = hooks["riders"](behind_it).astype(sent)
                 riders = rider.shape[0]

time: 115 us -> 115 us (level)
  transfers between devices with their start and end apart: 48 -> 48, of which waited for: 30 -> 31; matrix products, arithmetic and copies ran while one was open for 2% -> 2% of each run, Pallas kernels for 8% -> 8%
where the time goes in v7:
time: 115 us
  waiting for transfers between devices  55.8 us (49%)
  starting transfers between devices  42 us (37%)
  Pallas kernels  10.9 us (9%)
  local copies, waits for them, and re-layouts  3.62 us (3%)
  other arithmetic  1.35 us (1%)
    ppermute x16, waiting for transfers between devices, spread(): lax.ppermute(pair[0], 'rows', ahead)  27.9 us
    ppermute x16, starting transfers between devices, spread(): lax.ppermute(pair[0], 'rows', ahead)  24.3 us
    ppermute x16, waiting for transfers between devices, spread(): lax.ppermute(pair[1], 'rows', behind)  20 us
    ppermute x16, starting transfers between devices, spread(): lax.ppermute(pair[1], 'rows', behind)  8.62 us
    ppermute x2, waiting for transfers between devices, spread(): across = lax.ppermute(second, 'rep', pairs[2])  4.72 us
    ppermute x2, starting transfers between devices, spread(): across = lax.ppermute(second, 'rep', pairs[2])  4.22 us
    pallas_call x2, Pallas kernels, scatter_blocks(): pl.pallas_call(functools.partial(scatter_kernel, own_blocks, block, scale...  3.32 us
    pallas_call x2, Pallas kernels, gather_blocks(): pl.pallas_call(functools.partial(gather_kernel, n, own_blocks, block, sca...  3.04 us
  transfers between devices with their start and end apart: 48, of which 31 were waited for; matrix products, arithmetic and copies ran while one was open for 2% of the time, Pallas kernels for 8%

profile of v7, /device:TPU:0, one launch (start us, length us, event | category | flops | bytes accessed | tf_op | source)
XLA Modules:
  0.0 114.7 jit_solution(1250749631283267043)
XLA Ops:
  1.7 3.0 %collective-permute-start.2 = (bf16[1024,128]{1,0:T(8,128)(2,1)S(1)}, bf16[1024,128]{1,0:T(8,128)(2,1)S(1)}, u32[]{:S(2)}, u32[]{:S(2)}) collective-permute-start(bf16[1024,128]{1,0:T(8,128)(2,1)S(1)} %get-tuple-element.90.refs_0_), channel_id=1, source_target_pairs={{0,2},{1,3},{2,0},{3,1},{4,6},{5,7},{6,4},{7,5},{8,10},{9,11},{10,... | collective-permute-start | bytes 786440 | tf_op jit(solution)/shard_map/ppermute | solution.py:168
  4.7 1.6 %collective-permute-start = (bf16[1024,128]{1,0:T(8,128)(2,1)S(1)}, bf16[1024,128]{1,0:T(8,128)(2,1)S(1)}, u32[]{:S(2)}, u32[]{:S(2)}) collective-permute-start(bf16[1024,128]{1,0:T(8,128)(2,1)S(1)} %get-tuple-element.105.refs_0_), channel_id=1, source_target_pairs={{0,8},{8,16},{16,24},{24,28},{28,20},{20,12},{12,4},{4,0},{1,9},{9... | collective-permute-start | bytes 786440 | tf_op jit(solution)/shard_map/ppermute | solution.py:166
  7.6 1.6 %copy-done.1 = bf16[32,1,2,128,128]{4,3,2,1,0:T(8,128)(2,1)S(1)} copy-done((bf16[32,1,2,128,128]{4,3,2,1,0:T(8,128)(2,1)S(1)}, bf16[32,1,2,128,128]{4,3,2,1,0:T(8,128)(2,1)}, u32[]{:S(2)}) %copy-start.1) | copy-done | bytes 2097176
  13.8 1.6 %collective-permute-start.3 = (bf16[1024,128]{1,0:T(8,128)(2,1)S(1)}, bf16[1024,128]{1,0:T(8,128)(2,1)S(1)}, u32[]{:S(2)}, u32[]{:S(2)}) collective-permute-start(bf16[1024,128]{1,0:T(8,128)(2,1)S(1)} %collective-permute-done.refs_1_), channel_id=1, source_target_pairs={{0,8},{8,16},{16,24},{24,28},{28,20},{20,12},{12,4},{4,0},{1,9},{9... | collective-permute-start | bytes 786440 | tf_op jit(solution)/shard_map/ppermute | solution.py:166
  15.8 1.7 %scatter_blocks.2 = (f32[1024,128]{1,0:T(8,128)S(1)}, f32[8192,128]{1,0:T(8,128)S(1)}, bf16[512,128]{1,0:T(8,128)(2,1)S(1)}, bf16[512,128]{1,0:T(8,128)(2,1)S(1)}) custom-call(s32[64]{0:T(128)S(1)} %fusion.where_ref, s32[1]{0:T(128)} %bitcast.rep_ref, bf16[64,128,128]{2,1,0:T(8,128)(2,1)S(1)} %brought_near.1.vals_ref, ...), custom_call_target="tpu_custom_call" | custom-call | flops 268435456 | bytes 7864320 | tf_op jit(solution)/shard_map/scatter_blocks/pallas_call | solution.py:111
  18.0 1.6 %collective-permute-start.9 = (bf16[512,128]{1,0:T(8,128)(2,1)S(1)}, bf16[512,128]{1,0:T(8,128)(2,1)S(1)}, u32[]{:S(2)}, u32[]{:S(2)}) collective-permute-start(bf16[512,128]{1,0:T(8,128)(2,1)S(1)} %get-tuple-element.94), channel_id=1, source_target_pairs={{0,8},{8,16},{16,24},{24,28},{28,20},{20,12},{12,4},{4,0},{1,9},{9... | collective-permute-start | bytes 393224 | tf_op jit(solution)/shard_map/ppermute | solution.py:166
  19.8 2.0 %collective-permute-done.3.refs_2_ = bf16[1024,128]{1,0:T(8,128)(2,1)S(1)} collective-permute-done((bf16[1024,128]{1,0:T(8,128)(2,1)S(1)}, bf16[1024,128]{1,0:T(8,128)(2,1)S(1)}, u32[]{:S(2)}, u32[]{:S(2)}) %collective-permute-start.3) | collective-permute-done | bytes 262176 | tf_op jit(solution)/shard_map/ppermute | solution.py:166
  28.2 4.3 %collective-permute-done.7.refs_3_ = bf16[1024,128]{1,0:T(8,128)(2,1)S(1)} collective-permute-done((bf16[1024,128]{1,0:T(8,128)(2,1)S(1)}, bf16[1024,128]{1,0:T(8,128)(2,1)S(1)}, u32[]{:S(2)}, u32[]{:S(2)}) %collective-permute-start.7) | collective-permute-done | bytes 262176 | tf_op jit(solution)/shard_map/ppermute | solution.py:166
  38.1 1.6 %collective-permute-start.17 = (bf16[1024,128]{1,0:T(8,128)(2,1)S(1)}, bf16[1024,128]{1,0:T(8,128)(2,1)S(1)}, u32[]{:S(2)}, u32[]{:S(2)}) collective-permute-start(bf16[1024,128]{1,0:T(8,128)(2,1)S(1)} %get-tuple-element.103), channel_id=1, source_target_pairs={{0,8},{8,16},{16,24},{24,28},{28,20},{20,12},{12,4},{4,0},{1,9},{9... | collective-permute-start | bytes 786440 | tf_op jit(solution)/shard_map/ppermute | solution.py:166
  41.3 1.7 %gather_blocks.2 = (bf16[2048,128]{1,0:T(8,128)(2,1)S(1)}, f32[1024,128]{1,0:T(8,128)S(1)}, f32[1024,128]{1,0:T(8,128)S(1)}) custom-call(s32[64]{0:T(128)S(1)} %fusion.where_ref, s32[1]{0:T(128)} %bitcast.rep_ref, bf16[64,128,128]{2,1,0:T(8,128)(2,1)S(1)} %brought_near.1.vals_ref, bf16[1024,128]{1,0:T(8,128)(2,1)S(1)} %get-tuple-element.105.refs_0_, ...), custom_call_target="tpu_custom_call" | custom-call | flops 26843545600 | bytes 7864320 | tf_op jit(solution)/shard_map/gather_blocks/pallas_call | solution.py:71
  44.5 1.6 %collective-permute-done.18 = bf16[1024,128]{1,0:T(8,128)(2,1)S(1)} collective-permute-done((bf16[1024,128]{1,0:T(8,128)(2,1)S(1)}, bf16[1024,128]{1,0:T(8,128)(2,1)S(1)}, u32[]{:S(2)}, u32[]{:S(2)}) %collective-permute-start.18) | collective-permute-done | bytes 262176 | tf_op jit(solution)/shard_map/ppermute | solution.py:166
  48.6 4.8 %collective-permute-done.19.refs_4_ = bf16[1024,128]{1,0:T(8,128)(2,1)S(1)} collective-permute-done((bf16[1024,128]{1,0:T(8,128)(2,1)S(1)}, bf16[1024,128]{1,0:T(8,128)(2,1)S(1)}, u32[]{:S(2)}, u32[]{:S(2)}) %collective-permute-start.19) | collective-permute-done | bytes 262176 | tf_op jit(solution)/shard_map/ppermute | solution.py:166
  57.7 1.7 %collective-permute-start.21 = (bf16[1024,128]{1,0:T(8,128)(2,1)S(1)}, bf16[1024,128]{1,0:T(8,128)(2,1)S(1)}, u32[]{:S(2)}, u32[]{:S(2)}) collective-permute-start(bf16[1024,128]{1,0:T(8,128)(2,1)S(1)} %get-tuple-element.150.refs_0_), channel_id=1, source_target_pairs={{0,8},{8,16},{16,24},{24,28},{28,20},{20,12},{12,4},{4,0},{1,9},{9... | collective-permute-start | bytes 786440 | tf_op jit(solution)/shard_map/ppermute | solution.py:166
  59.7 3.2 %collective-permute-done.23.refs_2_ = bf16[1024,128]{1,0:T(8,128)(2,1)S(1)} collective-permute-done((bf16[1024,128]{1,0:T(8,128)(2,1)S(1)}, bf16[1024,128]{1,0:T(8,128)(2,1)S(1)}, u32[]{:S(2)}, u32[]{:S(2)}) %collective-permute-start.23) | collective-permute-done | bytes 262176 | tf_op jit(solution)/shard_map/ppermute | solution.py:168
  69.4 1.7 %scatter_blocks.3 = (f32[1024,128]{1,0:T(8,128)S(1)}, f32[8192,128]{1,0:T(8,128)S(1)}, bf16[512,128]{1,0:T(8,128)(2,1)S(1)}, bf16[512,128]{1,0:T(8,128)(2,1)S(1)}) custom-call(s32[64]{0:T(128)S(1)} %fusion.where_ref, s32[1]{0:T(128)} %bitcast.rep_ref, bf16[64,128,128]{2,1,0:T(8,128)(2,1)S(1)} %brought_near.1.vals_ref, ...), custom_call_target="tpu_custom_call" | custom-call | flops 268435456 | bytes 7864320 | tf_op jit(solution)/shard_map/scatter_blocks/pallas_call | solution.py:111
  75.0 2.1 %collective-permute-done.25.refs_7_ = bf16[1024,128]{1,0:T(8,128)(2,1)S(1)} collective-permute-done((bf16[1024,128]{1,0:T(8,128)(2,1)S(1)}, bf16[1024,128]{1,0:T(8,128)(2,1)S(1)}, u32[]{:S(2)}, u32[]{:S(2)}) %collective-permute-start.25) | collective-permute-done | bytes 262176 | tf_op jit(solution)/shard_map/ppermute | solution.py:166
  77.1 1.8 %collective-permute-start.31 = (bf16[1152,128]{1,0:T(8,128)(2,1)S(1)}, bf16[1152,128]{1,0:T(8,128)(2,1)S(1)}, u32[]{:S(2)}, u32[]{:S(2)}) collective-permute-start(bf16[1152,128]{1,0:T(8,128)(2,1)S(1)} %get-tuple-element.184), channel_id=1, source_target_pairs={{0,8},{8,16},{16,24},{24,28},{28,20},{20,12},{12,4},{4,0},{1,9},{9... | collective-permute-start | bytes 884744 | tf_op jit(solution)/shard_map/ppermute | solution.py:166
  82.5 4.6 %collective-permute-done.31.refs_3_ = bf16[1152,128]{1,0:T(8,128)(2,1)S(1)} collective-permute-done((bf16[1152,128]{1,0:T(8,128)(2,1)S(1)}, bf16[1152,128]{1,0:T(8,128)(2,1)S(1)}, u32[]{:S(2)}, u32[]{:S(2)}) %collective-permute-start.31) | collective-permute-done | bytes 294944 | tf_op jit(solution)/shard_map/ppermute | solution.py:166
  87.1 1.8 %collective-permute-done.32.refs_6_ = bf16[1152,128]{1,0:T(8,128)(2,1)S(1)} collective-permute-done((bf16[1152,128]{1,0:T(8,128)(2,1)S(1)}, bf16[1152,128]{1,0:T(8,128)(2,1)S(1)}, u32[]{:S(2)}, u32[]{:S(2)}) %collective-permute-start.32) | collective-permute-done | bytes 294944 | tf_op jit(solution)/shard_map/ppermute | solution.py:166
  91.0 2.7 %collective-permute-done.38.refs_2_ = bf16[1152,128]{1,0:T(8,128)(2,1)S(1)} collective-permute-done((bf16[1152,128]{1,0:T(8,128)(2,1)S(1)}, bf16[1152,128]{1,0:T(8,128)(2,1)S(1)}, u32[]{:S(2)}, u32[]{:S(2)}) %collective-permute-start.38) | collective-permute-done | bytes 294944 | tf_op jit(solution)/shard_map/ppermute | solution.py:166
  93.9 1.8 %collective-permute-start.41 = (bf16[1152,128]{1,0:T(8,128)(2,1)S(1)}, bf16[1152,128]{1,0:T(8,128)(2,1)S(1)}, u32[]{:S(2)}, u32[]{:S(2)}) collective-permute-start(bf16[1152,128]{1,0:T(8,128)(2,1)S(1)} %pad_maximum_fusion.4), channel_id=1, source_target_pairs={{0,8},{8,16},{16,24},{24,28},{28,20},{20,12},{12,4},{4,0},{1,9},{9... | collective-permute-start | bytes 884744 | tf_op jit(solution)/shard_map/ppermute | solution.py:166
  98.0 2.7 %collective-permute-done.41.refs_5_ = bf16[1152,128]{1,0:T(8,128)(2,1)S(1)} collective-permute-done((bf16[1152,128]{1,0:T(8,128)(2,1)S(1)}, bf16[1152,128]{1,0:T(8,128)(2,1)S(1)}, u32[]{:S(2)}, u32[]{:S(2)}) %collective-permute-start.41) | collective-permute-done | bytes 294944 | tf_op jit(solution)/shard_map/ppermute | solution.py:166
  100.7 1.7 %collective-permute-done.42.refs_3_ = bf16[1152,128]{1,0:T(8,128)(2,1)S(1)} collective-permute-done((bf16[1152,128]{1,0:T(8,128)(2,1)S(1)}, bf16[1152,128]{1,0:T(8,128)(2,1)S(1)}, u32[]{:S(2)}, u32[]{:S(2)}) %collective-permute-start.42) | collective-permute-done | bytes 294944 | tf_op jit(solution)/shard_map/ppermute | solution.py:166
  105.1 4.3 %collective-permute-done.43.refs_4_ = bf16[1152,128]{1,0:T(8,128)(2,1)S(1)} collective-permute-done((bf16[1152,128]{1,0:T(8,128)(2,1)S(1)}, bf16[1152,128]{1,0:T(8,128)(2,1)S(1)}, u32[]{:S(2)}, u32[]{:S(2)}) %collective-permute-start.43) | collective-permute-done | bytes 294944 | tf_op jit(solution)/shard_map/ppermute | solution.py:166
  (122 shorter events, 56.8 us)
Async XLA Ops:
  1.7 9.3 %collective-permute-start.2 = (bf16[1024,128]{1,0:T(8,128)(2,1)S(1)}, bf16[1024,128]{1,0:T(8,128)(2,1)S(1)}, u32[]{:S(2)}, u32[]{:S(2)}) collective-permute-start(bf16[1024,128]{1,0:T(8,128)(2,1)S(1)} %get-tuple-element.90.refs_0_), channel_id=1, source_target_pairs={{0,2},{1,3},{2,0},{3,1},{4,6},{5,7},{6,4},{7,5},{8,10},{9,11},{10,... | collective-permute-start | bytes 786440 | tf_op jit(solution)/shard_map/ppermute | solution.py:168
  4.7 7.8 %collective-permute-start = (bf16[1024,128]{1,0:T(8,128)(2,1)S(1)}, bf16[1024,128]{1,0:T(8,128)(2,1)S(1)}, u32[]{:S(2)}, u32[]{:S(2)}) collective-permute-start(bf16[1024,128]{1,0:T(8,128)(2,1)S(1)} %get-tuple-element.105.refs_0_), channel_id=1, source_target_pairs={{0,8},{8,16},{16,24},{24,28},{28,20},{20,12},{12,4},{4,0},{1,9},{9... | collective-permute-start | bytes 786440 | tf_op jit(solution)/shard_map/ppermute | solution.py:166
  6.3 7.5 %collective-permute-start.1 = (bf16[1024,128]{1,0:T(8,128)(2,1)S(1)}, bf16[1024,128]{1,0:T(8,128)(2,1)S(1)}, u32[]{:S(2)}, u32[]{:S(2)}) collective-permute-start(bf16[1024,128]{1,0:T(8,128)(2,1)S(1)} %get-tuple-element.105.refs_0_), channel_id=1, source_target_pairs={{8,0},{16,8},{24,16},{28,24},{20,28},{12,20},{4,12},{0,4},{9,1},{1... | collective-permute-start | bytes 786440 | tf_op jit(solution)/shard_map/ppermute | solution.py:166
  13.8 8.0 %collective-permute-start.3 = (bf16[1024,128]{1,0:T(8,128)(2,1)S(1)}, bf16[1024,128]{1,0:T(8,128)(2,1)S(1)}, u32[]{:S(2)}, u32[]{:S(2)}) collective-permute-start(bf16[1024,128]{1,0:T(8,128)(2,1)S(1)} %collective-permute-done.refs_1_), channel_id=1, source_target_pairs={{0,8},{8,16},{16,24},{24,28},{28,20},{20,12},{12,4},{4,0},{1,9},{9... | collective-permute-start | bytes 786440 | tf_op jit(solution)/shard_map/ppermute | solution.py:166
  15.3 7.8 %collective-permute-start.4 = (bf16[1024,128]{1,0:T(8,128)(2,1)S(1)}, bf16[1024,128]{1,0:T(8,128)(2,1)S(1)}, u32[]{:S(2)}, u32[]{:S(2)}) collective-permute-start(bf16[1024,128]{1,0:T(8,128)(2,1)S(1)} %collective-permute-done.1.refs_8_), channel_id=1, source_target_pairs={{8,0},{16,8},{24,16},{28,24},{20,28},{12,20},{4,12},{0,4},{9,1},{1... | collective-permute-start | bytes 786440 | tf_op jit(solution)/shard_map/ppermute | solution.py:166
  17.5 8.5 %collective-permute-start.10 = (bf16[512,128]{1,0:T(8,128)(2,1)S(1)}, bf16[512,128]{1,0:T(8,128)(2,1)S(1)}, u32[]{:S(2)}, u32[]{:S(2)}) collective-permute-start(bf16[512,128]{1,0:T(8,128)(2,1)S(1)} %get-tuple-element.95), channel_id=1, source_target_pairs={{8,0},{16,8},{24,16},{28,24},{20,28},{12,20},{4,12},{0,4},{9,1},{1... | collective-permute-start | bytes 393224 | tf_op jit(solution)/shard_map/ppermute | solution.py:166
  18.0 8.0 %collective-permute-start.9 = (bf16[512,128]{1,0:T(8,128)(2,1)S(1)}, bf16[512,128]{1,0:T(8,128)(2,1)S(1)}, u32[]{:S(2)}, u32[]{:S(2)}) collective-permute-start(bf16[512,128]{1,0:T(8,128)(2,1)S(1)} %get-tuple-element.94), channel_id=1, source_target_pairs={{0,8},{8,16},{16,24},{24,28},{28,20},{20,12},{12,4},{4,0},{1,9},{9... | collective-permute-start | bytes 393224 | tf_op jit(solution)/shard_map/ppermute | solution.py:166
  23.2 9.2 %collective-permute-start.7 = (bf16[1024,128]{1,0:T(8,128)(2,1)S(1)}, bf16[1024,128]{1,0:T(8,128)(2,1)S(1)}, u32[]{:S(2)}, u32[]{:S(2)}) collective-permute-start(bf16[1024,128]{1,0:T(8,128)(2,1)S(1)} %collective-permute-done.3.refs_2_), channel_id=1, source_target_pairs={{0,8},{8,16},{16,24},{24,28},{28,20},{20,12},{12,4},{4,0},{1,9},{9... | collective-permute-start | bytes 786440 | tf_op jit(solution)/shard_map/ppermute | solution.py:166
  24.7 9.2 %collective-permute-start.8 = (bf16[1024,128]{1,0:T(8,128)(2,1)S(1)}, bf16[1024,128]{1,0:T(8,128)(2,1)S(1)}, u32[]{:S(2)}, u32[]{:S(2)}) collective-permute-start(bf16[1024,128]{1,0:T(8,128)(2,1)S(1)} %collective-permute-done.4.refs_7_), channel_id=1, source_target_pairs={{8,0},{16,8},{24,16},{28,24},{20,28},{12,20},{4,12},{0,4},{9,1},{1... | collective-permute-start | bytes 786440 | tf_op jit(solution)/shard_map/ppermute | solution.py:166
  26.1 10.7 %collective-permute-start.13 = (bf16[1024,128]{1,0:T(8,128)(2,1)S(1)}, bf16[1024,128]{1,0:T(8,128)(2,1)S(1)}, u32[]{:S(2)}, u32[]{:S(2)}) collective-permute-start(bf16[1024,128]{1,0:T(8,128)(2,1)S(1)} %get-tuple-element.99), channel_id=1, source_target_pairs={{0,8},{8,16},{16,24},{24,28},{28,20},{20,12},{12,4},{4,0},{1,9},{9... | collective-permute-start | bytes 786440 | tf_op jit(solution)/shard_map/ppermute | solution.py:166
  27.6 10.3 %collective-permute-start.14 = (bf16[1024,128]{1,0:T(8,128)(2,1)S(1)}, bf16[1024,128]{1,0:T(8,128)(2,1)S(1)}, u32[]{:S(2)}, u32[]{:S(2)}) collective-permute-start(bf16[1024,128]{1,0:T(8,128)(2,1)S(1)} %get-tuple-element.100), channel_id=1, source_target_pairs={{8,0},{16,8},{24,16},{28,24},{20,28},{12,20},{4,12},{0,4},{9,1},{1... | collective-permute-start | bytes 786440 | tf_op jit(solution)/shard_map/ppermute | solution.py:166
  46.3 7.1 %collective-permute-start.19 = (bf16[1024,128]{1,0:T(8,128)(2,1)S(1)}, bf16[1024,128]{1,0:T(8,128)(2,1)S(1)}, u32[]{:S(2)}, u32[]{:S(2)}) collective-permute-start(bf16[1024,128]{1,0:T(8,128)(2,1)S(1)} %get-tuple-element.118), channel_id=1, source_target_pairs={{0,8},{8,16},{16,24},{24,28},{28,20},{20,12},{12,4},{4,0},{1,9},{9... | collective-permute-start | bytes 786440 | tf_op jit(solution)/shard_map/ppermute | solution.py:166
  47.7 7.0 %collective-permute-start.20 = (bf16[1024,128]{1,0:T(8,128)(2,1)S(1)}, bf16[1024,128]{1,0:T(8,128)(2,1)S(1)}, u32[]{:S(2)}, u32[]{:S(2)}) collective-permute-start(bf16[1024,128]{1,0:T(8,128)(2,1)S(1)} %get-tuple-element.119), channel_id=1, source_target_pairs={{8,0},{16,8},{24,16},{28,24},{20,28},{12,20},{4,12},{0,4},{9,1},{1... | collective-permute-start | bytes 786440 | tf_op jit(solution)/shard_map/ppermute | solution.py:166
  59.7 9.7 %collective-permute-start.26 = (bf16[1024,128]{1,0:T(8,128)(2,1)S(1)}, bf16[1024,128]{1,0:T(8,128)(2,1)S(1)}, u32[]{:S(2)}, u32[]{:S(2)}) collective-permute-start(bf16[1024,128]{1,0:T(8,128)(2,1)S(1)} %get-tuple-element.135.refs_1_.refs_0_), channel_id=1, source_target_pairs={{0,1},{1,0},{2,3},{3,2},{4,5},{5,4},{6,7},{7,6},{8,9},{9,8},{10,11... | collective-permute-start | bytes 786440 | tf_op jit(solution)/shard_map/ppermute | solution.py:169
  65.7 9.2 %collective-permute-start.24 = (bf16[1024,128]{1,0:T(8,128)(2,1)S(1)}, bf16[1024,128]{1,0:T(8,128)(2,1)S(1)}, u32[]{:S(2)}, u32[]{:S(2)}) collective-permute-start(bf16[1024,128]{1,0:T(8,128)(2,1)S(1)} %collective-permute-done.21.refs_1_), channel_id=1, source_target_pairs={{0,8},{8,16},{16,24},{24,28},{28,20},{20,12},{12,4},{4,0},{1,9},{9... | collective-permute-start | bytes 786440 | tf_op jit(solution)/shard_map/ppermute | solution.py:166
  68.2 8.9 %collective-permute-start.25 = (bf16[1024,128]{1,0:T(8,128)(2,1)S(1)}, bf16[1024,128]{1,0:T(8,128)(2,1)S(1)}, u32[]{:S(2)}, u32[]{:S(2)}) collective-permute-start(bf16[1024,128]{1,0:T(8,128)(2,1)S(1)} %collective-permute-done.22.refs_8_), channel_id=1, source_target_pairs={{8,0},{16,8},{24,16},{28,24},{20,28},{12,20},{4,12},{0,4},{9,1},{1... | collective-permute-start | bytes 786440 | tf_op jit(solution)/shard_map/ppermute | solution.py:166
  71.1 9.2 %collective-permute-start.33 = (bf16[640,128]{1,0:T(8,128)(2,1)S(1)}, bf16[640,128]{1,0:T(8,128)(2,1)S(1)}, u32[]{:S(2)}, u32[]{:S(2)}) collective-permute-start(bf16[640,128]{1,0:T(8,128)(2,1)S(1)} %get-tuple-element.186), channel_id=1, source_target_pairs={{0,8},{8,16},{16,24},{24,28},{28,20},{20,12},{12,4},{4,0},{1,9},{9... | collective-permute-start | bytes 491528 | tf_op jit(solution)/shard_map/ppermute | solution.py:166
  72.6 7.7 %collective-permute-start.34 = (bf16[640,128]{1,0:T(8,128)(2,1)S(1)}, bf16[640,128]{1,0:T(8,128)(2,1)S(1)}, u32[]{:S(2)}, u32[]{:S(2)}) collective-permute-start(bf16[640,128]{1,0:T(8,128)(2,1)S(1)} %get-tuple-element.185), channel_id=1, source_target_pairs={{8,0},{16,8},{24,16},{28,24},{20,28},{12,20},{4,12},{0,4},{9,1},{1... | collective-permute-start | bytes 491528 | tf_op jit(solution)/shard_map/ppermute | solution.py:166
  77.1 10.0 %collective-permute-start.31 = (bf16[1152,128]{1,0:T(8,128)(2,1)S(1)}, bf16[1152,128]{1,0:T(8,128)(2,1)S(1)}, u32[]{:S(2)}, u32[]{:S(2)}) collective-permute-start(bf16[1152,128]{1,0:T(8,128)(2,1)S(1)} %get-tuple-element.184), channel_id=1, source_target_pairs={{0,8},{8,16},{16,24},{24,28},{28,20},{20,12},{12,4},{4,0},{1,9},{9... | collective-permute-start | bytes 884744 | tf_op jit(solution)/shard_map/ppermute | solution.py:166
  78.9 9.9 %collective-permute-start.32 = (bf16[1152,128]{1,0:T(8,128)(2,1)S(1)}, bf16[1152,128]{1,0:T(8,128)(2,1)S(1)}, u32[]{:S(2)}, u32[]{:S(2)}) collective-permute-start(bf16[1152,128]{1,0:T(8,128)(2,1)S(1)} %get-tuple-element.183), channel_id=1, source_target_pairs={{8,0},{16,8},{24,16},{28,24},{20,28},{12,20},{4,12},{0,4},{9,1},{1... | collective-permute-start | bytes 884744 | tf_op jit(solution)/shard_map/ppermute | solution.py:166
  80.4 13.3 %collective-permute-start.38 = (bf16[1152,128]{1,0:T(8,128)(2,1)S(1)}, bf16[1152,128]{1,0:T(8,128)(2,1)S(1)}, u32[]{:S(2)}, u32[]{:S(2)}) collective-permute-start(bf16[1152,128]{1,0:T(8,128)(2,1)S(1)} %pad_maximum_fusion.3), channel_id=1, source_target_pairs={{8,0},{16,8},{24,16},{28,24},{20,28},{12,20},{4,12},{0,4},{9,1},{1... | collective-permute-start | bytes 884744 | tf_op jit(solution)/shard_map/ppermute | solution.py:166
  81.0 12.8 %collective-permute-start.37 = (bf16[1152,128]{1,0:T(8,128)(2,1)S(1)}, bf16[1152,128]{1,0:T(8,128)(2,1)S(1)}, u32[]{:S(2)}, u32[]{:S(2)}) collective-permute-start(bf16[1152,128]{1,0:T(8,128)(2,1)S(1)} %pad_maximum_fusion.2), channel_id=1, source_target_pairs={{0,8},{8,16},{16,24},{24,28},{28,20},{20,12},{12,4},{4,0},{1,9},{9... | collective-permute-start | bytes 884744 | tf_op jit(solution)/shard_map/ppermute | solution.py:166
  88.9 7.1 %collective-permute-start.35 = (bf16[512,128]{1,0:T(8,128)(2,1)S(1)}, bf16[512,128]{1,0:T(8,128)(2,1)S(1)}, u32[]{:S(2)}, u32[]{:S(2)}) collective-permute-start(bf16[512,128]{1,0:T(8,128)(2,1)S(1)} %slice.142), channel_id=1, source_target_pairs={{0,8},{8,16},{16,24},{24,28},{28,20},{20,12},{12,4},{4,0},{1,9},{9... | collective-permute-start | bytes 393224 | tf_op jit(solution)/shard_map/ppermute | solution.py:166
  103.5 7.8 %collective-permute-start.44 = (bf16[1024,128]{1,0:T(8,128)(2,1)S(1)}, bf16[1024,128]{1,0:T(8,128)(2,1)S(1)}, u32[]{:S(2)}, u32[]{:S(2)}) collective-permute-start(bf16[1024,128]{1,0:T(8,128)(2,1)S(1)} %get-tuple-element.164), channel_id=1, source_target_pairs={{8,0},{16,8},{24,16},{28,24},{20,28},{12,20},{4,12},{0,4},{9,1},{1... | collective-permute-start | bytes 786440 | tf_op jit(solution)/shard_map/ppermute | solution.py:166
  (27 other events, 160.0 us)
